TPU v7x, 128 devices: a whole 4x4x4 slice. The times are simulated.
128 devices in a mesh: img: 8 (over y, core), txt: 16 (over x, z).
Axes of the slice: x: 4, y: 4, z: 4, core: 2. Of those that a mesh axis runs over, the one named last changes fastest.
Arguments:
- features: bfloat16 [128, 64, 8192], P('txt'), may hold values from -6 to 6
- tile_count: int32 [128], P('txt'), may hold values from 1 to 4
- kv_weight: bfloat16 [8192, 2, 1024], P(None, None, 'img'), may hold values from -0.0625 to 0.0625
- queries: bfloat16 [24576, 8192], P('txt', 'img'), may hold values from -240 to 240
- out_grad: bfloat16 [24576, 8192], P('txt', 'img'), may hold values from -6 to 6
- image_ids: int32 [192, 2], P('txt'), may hold values from 0 to 127, as said below
- text_len: int32 [192], P('txt'), may hold values from 16 to 128
Outputs:
- attn_out: bfloat16 [24576, 8192], P('txt', 'img')
- query_grad: bfloat16 [24576, 8192], P('txt', 'img')
- weight_grad: float32 [8192, 2, 1024], P('txt', None, 'img')
Inputs may be any that keep to these rules, and one draw needn't show every extreme that they name: `image_ids`: each 12 consecutive sequences form one text shard; among its 24 entries at most 2 name images of one image shard (8 consecutive ids), and some image shard is named exactly 2 times there.
All inputs are finite; a program needn't handle non-finite values.
Results may differ from a plain program's by a relative error of at most 0.018.
The roundings to bfloat16 on the way count: a program that leaves them out, or rounds other values in their place, can miss the bound.
Values may be sent and summed in bfloat16 or wider, within the bound.
No kernel may reach another device: no remote copies, remote signals or barrier semaphores. Data moves between devices by JAX's collectives and lax.ppermute only.
A program may use at most 192 MiB of HBM per device.

v0:
```python
import math

import jax
import jax.numpy as jnp
from jax import lax
from jax.sharding import PartitionSpec as P

HEADS = 64
KVH = 8
HD = 128
MAXT = 4


def request_order(flat_ids, img_dev):
    shard_of = flat_ids // img_dev
    total = flat_ids.shape[0]
    same_shard = shard_of[:, None] == shard_of[None, :]
    earlier = jnp.arange(total)[None, :] < jnp.arange(total)[:, None]
    position = jnp.sum(jnp.logical_and(same_shard, earlier).astype(jnp.int32), axis=1)
    return (shard_of, position)


def attend_block(query_blk, pair_blk, key_live, row_live, grad_blk):
    inv_root = 1.0 / math.sqrt(query_blk.shape[-1])
    keys_blk = pair_blk[:, :, 0]
    vals_blk = pair_blk[:, :, 1]
    scores = (
        jnp.einsum("blhgd,bkhd->bhglk", query_blk, keys_blk, preferred_element_type=jnp.float32)
        * inv_root
    )
    scores = jnp.where(key_live[:, None, None, None, :], scores, -jnp.inf)
    top_score = jnp.max(scores, axis=-1, keepdims=True)
    expo = jnp.exp(scores - top_score)
    probs = expo / jnp.sum(expo, axis=-1, keepdims=True)
    probs_low = probs.astype(jnp.bfloat16)
    attended = jnp.einsum(
        "bhglk,bkhd->blhgd", probs_low, vals_blk, preferred_element_type=jnp.float32
    )
    row_mask = row_live[:, :, None, None, None]
    attended = jnp.where(row_mask, attended, 0.0)
    grad_live = jnp.where(row_mask, grad_blk, jnp.zeros_like(grad_blk))
    delta_sum = jnp.sum(grad_live.astype(jnp.float32) * attended, axis=-1)
    grad_probs = jnp.einsum(
        "blhgd,bkhd->bhglk", grad_live, vals_blk, preferred_element_type=jnp.float32
    )
    grad_scores = probs * (grad_probs - jnp.transpose(delta_sum, (0, 2, 3, 1))[..., None])
    scores_low = grad_scores.astype(jnp.bfloat16)
    grad_query = (
        jnp.einsum("bhglk,bkhd->blhgd", scores_low, keys_blk, preferred_element_type=jnp.float32)
        * inv_root
    )
    grad_keys = (
        jnp.einsum("bhglk,blhgd->bkhd", scores_low, query_blk, preferred_element_type=jnp.float32)
        * inv_root
    )
    grad_vals = jnp.einsum(
        "bhglk,blhgd->bkhd", probs_low, grad_live, preferred_element_type=jnp.float32
    )
    pair_grad = jnp.stack([grad_keys, grad_vals], axis=2).astype(jnp.bfloat16)
    return (attended.astype(jnp.bfloat16), grad_query.astype(jnp.bfloat16), pair_grad)


def shards(features, tile_count, kv_weight, queries, out_grad, image_ids, text_len):
    txt_count = lax.axis_size("txt")
    shard_index = lax.axis_index("txt")
    img_dev, keys_img, feat_width = features.shape
    seq_dev, picks = image_ids.shape
    head_cols = kv_weight.shape[2]
    heads_kv = head_cols // HD
    group_size = HEADS // KVH
    seq_len = queries.shape[0] // seq_dev
    request_total = seq_dev * picks
    capacity = (request_total + txt_count - 1) // txt_count
    slot_total = txt_count * capacity
    tile_rows = keys_img // MAXT
    flat_weight = kv_weight.reshape(feat_width, 2 * head_cols)
    contract_rows = (((0,), (0,)), ((), ()))
    every_ids = lax.all_gather(image_ids, "txt", axis=0, tiled=True).reshape(
        txt_count, request_total
    )
    all_shard, all_position = jax.vmap(lambda row_ids: request_order(row_ids, img_dev))(every_ids)
    slot_range = jnp.arange(capacity)
    chosen = jnp.logical_and(
        (all_shard == shard_index)[:, None, :],
        all_position[:, None, :] == slot_range[None, :, None],
    )
    local_image = every_ids - shard_index * img_dev
    slot_image = jnp.sum(jnp.where(chosen, local_image[:, None, :], 0), axis=-1).reshape(slot_total)
    slot_live = jnp.any(chosen, axis=-1).reshape(slot_total)
    image_match = slot_image[:, None] == jnp.arange(img_dev)[None, :]
    slot_tiles = jnp.sum(jnp.where(image_match, tile_count[None, :], 0), axis=1)
    slot_tiles = jnp.where(slot_live, slot_tiles, 0).reshape(txt_count, capacity)
    own_shard, own_position = request_order(image_ids.reshape(request_total), img_dev)
    flat_index = own_shard * capacity + own_position
    own_pairs = jnp.dot(
        features.reshape(img_dev * keys_img, feat_width),
        flat_weight,
        preferred_element_type=jnp.float32,
    ).astype(jnp.bfloat16)
    own_pairs = own_pairs.reshape(img_dev, keys_img, 2 * head_cols)
    sent_pairs = jnp.take(own_pairs, slot_image, axis=0)
    sent_pairs = jnp.where(slot_live[:, None, None], sent_pairs, jnp.zeros_like(sent_pairs))
    got_pairs, got_tiles = (
        lax.all_to_all(
            sent_pairs.reshape(txt_count, capacity, keys_img, 2 * head_cols),
            "txt",
            split_axis=0,
            concat_axis=0,
            tiled=True,
        ),
        lax.all_to_all(slot_tiles, "txt", split_axis=0, concat_axis=0, tiled=True),
    )
    slot_pairs = got_pairs.reshape(slot_total, keys_img, 2 * head_cols)
    request_pairs = jnp.take(slot_pairs, flat_index, axis=0)
    request_tiles = jnp.take(got_tiles.reshape(slot_total), flat_index, axis=0)
    key_tile = jnp.arange(keys_img) // tile_rows
    key_live = (key_tile[None, :] < request_tiles[:, None]).reshape(seq_dev, picks * keys_img)
    row_live = jnp.arange(seq_len)[None, :] < text_len[:, None]
    block_seqs = max(
        [
            size
            for size in range(1, seq_dev + 1)
            if seq_dev % size == 0 and size * seq_len <= max(512, seq_len)
        ]
    )
    block_count = seq_dev // block_seqs
    query_blocks = queries.reshape(block_count, block_seqs, seq_len, heads_kv, group_size, HD)
    grad_blocks = out_grad.reshape(block_count, block_seqs, seq_len, heads_kv, group_size, HD)
    pair_blocks = request_pairs.reshape(block_count, block_seqs, picks * keys_img, 2, heads_kv, HD)
    live_blocks = key_live.reshape(block_count, block_seqs, picks * keys_img)
    row_blocks = row_live.reshape(block_count, block_seqs, seq_len)
    attended, grad_query, pair_grad = lax.map(
        lambda packed: attend_block(*packed),
        (query_blocks, pair_blocks, live_blocks, row_blocks, grad_blocks),
    )
    request_grad = pair_grad.reshape(request_total, keys_img, 2 * head_cols)
    slot_grad = (
        jnp.zeros((slot_total, keys_img, 2 * head_cols), jnp.bfloat16)
        .at[flat_index]
        .set(request_grad)
    )
    back_grad = lax.all_to_all(
        slot_grad.reshape(txt_count, capacity, keys_img, 2 * head_cols),
        "txt",
        split_axis=0,
        concat_axis=0,
        tiled=True,
    )
    slot_rows = jnp.take(features, slot_image, axis=0).reshape(slot_total * keys_img, feat_width)
    local_grad = lax.dot_general(
        slot_rows,
        back_grad.reshape(slot_total * keys_img, 2 * head_cols),
        contract_rows,
        preferred_element_type=jnp.float32,
    )
    weight_grad = lax.psum_scatter(local_grad, "txt", scatter_dimension=0, tiled=True)
    weight_grad = weight_grad.reshape(weight_grad.shape[0], 2, head_cols)
    token_total = seq_dev * seq_len
    return (
        attended.reshape(token_total, heads_kv * group_size * HD),
        grad_query.reshape(token_total, heads_kv * group_size * HD),
        weight_grad,
    )


def solution(mesh):
    in_specs = (
        P("txt", None, None),
        P("txt"),
        P(None, None, "img"),
        P("txt", "img"),
        P("txt", "img"),
        P("txt", None),
        P("txt"),
    )
    out_specs = (P("txt", "img"), P("txt", "img"), P("txt", None, "img"))
    return jax.shard_map(shards, mesh=mesh, in_specs=in_specs, out_specs=out_specs, check_vma=False)
```

profile of v0, /device:TPU:0, one launch (start us, length us, event | category | flops | bytes accessed | tf_op | source)
XLA Modules:
  0.0 290.2 jit_solution(9874205077770620299)
XLA Ops:
  7.2 24.7 %all-gather = s32[16,12,2]{1,2,0:T(2,128)S(1)} all-gather(s32[1,12,2]{1,2,0:T(2,128)} %bitcast.318), channel_id=1, replica_groups=mesh['img'=8,'txt'=16] {'txt'}, dimensions={0}, use_global_device_ids=true | all-gather | bytes 1632 | tf_op jit(solution)/shard_map/all_gather | solution.py:78
  34.6 4.7 %all-to-all-start.1 = ((s32[16,1,2]{2,1,0:T(1,128)}), s32[16,1,2]{2,1,0:T(1,128)S(1)}, u32[]{:S(2)}, u32[]{:S(2)}) async-start(s32[16,1,2]{2,1,0:T(1,128)} %copy.139), calls=%async_computation.1 | async-start | bytes 16384 | tf_op jit(solution)/shard_map/all_to_all | solution.py:111
  42.6 16.4 %gather_fusion.3 = bf16[32,64,8192]{2,1,0:T(8,128)(2,1)} fusion(bf16[8,64,8192]{2,1,0:T(8,128)(2,1)} %param.9, s32[1024]{0:T(1024)S(1)} %pad_clamp_fusion.1), kind=kCustom, calls=%fused_computation.3 | custom fusion | bytes 67108992 | tf_op jit(solution)/shard_map/jit(_take)/gather | solution.py:149
  59.0 6.9 %fusion.30 = bf16[512,256]{1,0:T(8,128)(2,1)S(1)} fusion(bf16[512,8192]{1,0:T(8,128)(2,1)} %bitcast.298, bf16[1024,8,2,128]{3,2,1,0:T(2,128)(2,1)} %bitcast.319), kind=kOutput, calls=%fused_computation.62 | convolution fusion | flops 2147614720 | bytes 12845056 | tf_op jit(solution)/shard_map/dot_general | solution.py:95
  66.5 4.5 %copy.174 = bf16[192,8,8,128]{3,2,1,0:T(8,128)(2,1)} copy(bf16[192,8,8,128]{3,1,2,0:T(8,128)(2,1)} %bitcast.309) | data formatting | bytes 6291456
  71.1 1.2 select_select_fusion
  72.3 2.4 copy.175
  74.7 7.2 %all-to-all-start = ((bf16[16,2,64,256]{3,2,1,0:T(8,128)(2,1)}), bf16[16,2,64,256]{3,2,1,0:T(8,128)(2,1)S(1)}, u32[]{:S(2)}, u32[]{:S(2)}) async-start(bf16[16,2,64,256]{3,2,1,0:T(8,128)(2,1)} %select_select_fusion), calls=%async_computation | async-start | bytes 2097152 | tf_op jit(solution)/shard_map/all_to_all | solution.py:104
  84.9 10.0 %all-to-all-done = bf16[16,2,64,256]{3,2,1,0:T(8,128)(2,1)S(1)} async-done(((bf16[16,2,64,256]{3,2,1,0:T(8,128)(2,1)}), bf16[16,2,64,256]{3,2,1,0:T(8,128)(2,1)S(1)}, u32[]{:S(2)}, u32[]{:S(2)}) %all-to-all-start) | async-done | bytes 1048608 | tf_op jit(solution)/shard_map/all_to_all | solution.py:104
  95.7 4.6 %broadcast_select_fusion.1 = bf16[3,4,128,2,1,128]{5,3,2,1,0,4:T(2,128)(2,1)} fusion(bf16[3,4,128,2,1,128]{5,3,2,1,0,4:T(2,128)(2,1)S(1)} %gather.25, pred[3,4,128]{2,1,0:T(4,128)(4,1)S(1)} %broadcast_in_dim.147), kind=kLoop, calls=%fused_computation.61 | loop fusion | flops 393216 | bytes 1574400 | tf_op jit(solution)/shard_map/jit(_take)/select_n | solution.py:114
  100.3 41.7 %while.14 = (s32[]{:T(128)}, bf16[3,4,128,1,8,128]{5,4,2,1,0,3:T(8,128)(2,1)}, bf16[3,4,128,1,8,128]{5,4,2,1,0,3:T(8,128)(2,1)}, bf16[3,4,128,2,1,128]{5,3,2,1,0...) while((s32[]{:T(128)}, ...), condition=%wide.region_9.10_spmd, body=%wide.region_5.9_spmd.sunk | while | flops 823971840 | bytes 41344136 | solution.py:132
  101.5 1.3 constant_dynamic-slice_fusion.9
  102.8 1.3 constant_dynamic-slice_fusion.8
  106.8 1.1 fusion.67
  112.7 1.5 constant_dynamic-update-slice_fusion.5
  115.4 1.3 constant_dynamic-slice_fusion.9
  116.7 1.3 constant_dynamic-slice_fusion.8
  120.7 1.1 fusion.67
  126.6 1.5 constant_dynamic-update-slice_fusion.5
  129.3 1.3 constant_dynamic-slice_fusion.9
  130.6 1.3 constant_dynamic-slice_fusion.8
  140.5 1.5 constant_dynamic-update-slice_fusion.5
  142.0 2.4 reshape.615
  145.5 4.5 %scatter_fusion = bf16[32,64,256]{2,1,0:T(8,128)(2,1)} fusion(bf16[32,64,256]{2,1,0:T(8,128)(2,1)} %broadcast.519, s32[24]{0:T(128)S(1)} %fusion.42, bf16[24,64,256]{2,1,0:T(8,128)(2,1)S(1)} %reshape.615), kind=kCustom, calls=%fused_computation.4 | custom fusion | bytes 2359392 | tf_op jit(solution)/shard_map/scatter | solution.py:140
  150.1 3.7 %all-to-all-start.2 = ((bf16[16,2,64,256]{3,2,1,0:T(8,128)(2,1)}), bf16[16,2,64,256]{3,2,1,0:T(8,128)(2,1)S(1)}, u32[]{:S(2)}, u32[]{:S(2)}) async-start(bf16[16,2,64,256]{3,2,1,0:T(8,128)(2,1)} %bitcast.50), calls=%async_computation.2 | async-start | bytes 2097152 | tf_op jit(solution)/shard_map/all_to_all | solution.py:142
  154.0 22.8 %broadcast_select_fusion = bf16[32,64,8192]{2,1,0:T(8,128)(2,1)} fusion(bf16[32,64,8192]{2,1,0:T(8,128)(2,1)} %gather_fusion.3, pred[32]{0:T(512)(128)(4,1)S(1)} %compare_and_fusion.1), kind=kLoop, calls=%fused_computation.55 | loop fusion | flops 16777216 | bytes 67108896 | tf_op jit(solution)/shard_map/jit(_take)/select_n | solution.py:149
  176.8 17.6 %fusion.43 = f32[8192,256]{1,0:T(8,128)} fusion(bf16[2048,8192]{1,0:T(8,128)(2,1)} %bitcast.299, bf16[2048,256]{1,0:T(8,128)(2,1)S(1)} %bitcast.315), kind=kOutput, calls=%fused_computation.120 | convolution fusion | flops 8589934592 | bytes 42991616 | tf_op jit(solution)/shard_map/dot_general | solution.py:150
  194.5 1.9 copy-done.2
  196.3 2.5 copy.194
  198.8 2.5 copy.193
  201.3 80.0 %reduce-scatter.2.cloned.1.call-done = f32[512,256]{1,0:T(8,128)} async-done(((f32[8192,256]{1,0:T(8,128)}), f32[512,256]{1,0:T(8,128)}) %reduce-scatter.2.cloned.1.call-update) | async-done | bytes 524304 | tf_op jit(solution)/shard_map/reduce_scatter | solution.py:156
  281.3 2.1 reshape.578
  (119 shorter events, 38.4 us)
Async XLA Ops:
  34.6 40.1 %all-to-all-start.1 = ((s32[16,1,2]{2,1,0:T(1,128)}), s32[16,1,2]{2,1,0:T(1,128)S(1)}, u32[]{:S(2)}, u32[]{:S(2)}) async-start(s32[16,1,2]{2,1,0:T(1,128)} %copy.139), calls=%async_computation.1 | async-start | bytes 16384 | tf_op jit(solution)/shard_map/all_to_all | solution.py:111
  66.5 5.8 %copy-start = (bf16[1536,1024]{1,0:T(8,128)(2,1)S(1)}, bf16[1536,1024]{1,0:T(8,128)(2,1)}, u32[]{:S(2)}) copy-start(bf16[1536,1024]{1,0:T(8,128)(2,1)} %param.13) | copy-start | bytes 9437188
  74.7 20.1 %all-to-all-start = ((bf16[16,2,64,256]{3,2,1,0:T(8,128)(2,1)}), bf16[16,2,64,256]{3,2,1,0:T(8,128)(2,1)S(1)}, u32[]{:S(2)}, u32[]{:S(2)}) async-start(bf16[16,2,64,256]{3,2,1,0:T(8,128)(2,1)} %select_select_fusion), calls=%async_computation | async-start | bytes 2097152 | tf_op jit(solution)/shard_map/all_to_all | solution.py:104
  150.1 26.8 %all-to-all-start.2 = ((bf16[16,2,64,256]{3,2,1,0:T(8,128)(2,1)}), bf16[16,2,64,256]{3,2,1,0:T(8,128)(2,1)S(1)}, u32[]{:S(2)}, u32[]{:S(2)}) async-start(bf16[16,2,64,256]{3,2,1,0:T(8,128)(2,1)} %bitcast.50), calls=%async_computation.2 | async-start | bytes 2097152 | tf_op jit(solution)/shard_map/all_to_all | solution.py:142
  153.7 127.6 %reduce-scatter.2.cloned.1.call-start = ((), (), s32[]{:S(2)}) async-start(), calls=%async_computation.4 | async-start | bytes 8912896 | tf_op jit(solution)/shard_map/reduce_scatter | solution.py:156
  194.4 1.9 copy-start.2
  196.3 2.5 copy-start.1
Sparse Core Ops, SparseCore 0:
  194.6 86.6 reduce-scatter.1
where the time goes:
time: 291 us; the launch traced here: 290 us
  waiting for transfers between devices  90 us (31%)
  local copies, waits for them, and re-layouts  73.7 us (25%)
  matrix products  37.4 us (13%)
  other arithmetic  33.9 us (12%)
  blocking collectives  24.7 us (8%)
  starting transfers between devices  15.8 us (5%)
  between operations  14.3 us (5%)
    reduce_scatter x1, waiting for transfers between devices, shards(): lax.psum_scatter(local_grad, 'txt', scatter_dimension=0, tiled=True)  80 us
    all_gather x1, blocking collectives, shards(): lax.all_gather(image_ids, 'txt', axis=0, tiled=True)  24.7 us
    select_n x1, other arithmetic, shards(): jnp.take(features, slot_image, axis=0)  22.8 us
    dot_general x1, matrix products, shards(): lax.dot_general(slot_rows, back_grad.reshape(slot_total * keys_img, 2 * h...  17.6 us
    gather x1, local copies, waits for them, and re-layouts, shards(): jnp.take(features, slot_image, axis=0)  16.4 us
    unnamed x11, local copies, waits for them, and re-layouts  14.6 us
    dynamic_slice x15, local copies, waits for them, and re-layouts, shards(): lax.map(lambda packed: attend_block(*packed), (query_blocks, pair_blocks,...  13.7 us
    dynamic_update_slice x15, local copies, waits for them, and re-layouts, shards(): lax.map(lambda packed: attend_block(*packed), (query_blocks, pair_blocks,...  11.9 us
  transfers between devices with their start and end apart: 4, of which 2 were waited for; matrix products, arithmetic and copies ran while one was open for 23% of the time, Pallas kernels for 0%

commit v1 on v0

v1 whole, which is shorter than its diff:
```python
import functools
import math

import jax
import jax.numpy as jnp
from jax import lax
from jax.experimental import pallas as pl
from jax.experimental.pallas import tpu as pltpu
from jax.sharding import PartitionSpec as P

HD = 128
MAXT = 4
SIDE = 4
CAP = 2
BF16 = jnp.bfloat16
F32 = jnp.float32
VMEM_LIMIT = 48 * 1024 * 1024


def request_order(flat_ids, img_dev):
    shard_of = flat_ids // img_dev
    total = flat_ids.shape[0]
    same_shard = shard_of[:, None] == shard_of[None, :]
    earlier = jnp.arange(total)[None, :] < jnp.arange(total)[:, None]
    position = jnp.sum(jnp.logical_and(same_shard, earlier).astype(jnp.int32), axis=1)
    return shard_of, position


def fill_kernel(table, pairs, slots):
    for slot in range(slots.shape[0]):
        image = jnp.maximum(table[slot // CAP, slot % CAP] - 1, 0)
        slots[slot] = pairs[image]


def attend_kernel(meta, table, queries, grads, slots, attn, query_grad, slot_grad, *, seq_dev, img_dev):
    seq = pl.program_id(0)
    seq_len = queries.shape[0]
    groups = queries.shape[1] // HD
    keys_img = slots.shape[1]
    inv_root = 1.0 / math.sqrt(HD)
    scale = inv_root * math.log2(math.e)

    @pl.when(seq == 0)
    def _():
        slot_grad[...] = jnp.zeros_like(slot_grad)

    text_len = meta[4 * seq_dev + seq]
    slot_ids = [meta[2 * seq + pick] for pick in range(2)]
    images = [meta[2 * seq_dev + 2 * seq + pick] for pick in range(2)]
    tiles = [table[image // img_dev, 8 + image % img_dev] for image in images]
    pair = [slots[slot] for slot in slot_ids]
    keys = jnp.concatenate([blk[:, :HD] for blk in pair], axis=0)
    vals = jnp.concatenate([blk[:, HD:] for blk in pair], axis=0)
    none = jnp.zeros_like(keys)
    key_val = jnp.concatenate(
        [jnp.concatenate([keys, none], axis=1), jnp.concatenate([none, vals], axis=1)], axis=0
    )
    val_key = jnp.concatenate(
        [jnp.concatenate([vals, none], axis=1), jnp.concatenate([none, keys], axis=1)], axis=0
    )
    column = lax.broadcasted_iota(jnp.int32, (1, 2 * keys_img), 1)
    tile_rows = keys_img // MAXT
    live_to = jnp.where(
        column < keys_img, tiles[0] * tile_rows, keys_img + tiles[1] * tile_rows
    )
    bias = jnp.where(column < live_to, 0.0, -jnp.inf).astype(F32)
    row = lax.broadcasted_iota(jnp.int32, (groups, seq_len, 1), 1).reshape(groups * seq_len, 1)
    row_live = row < text_len

    both = jnp.concatenate(
        [
            jnp.concatenate(
                [queries[:, h * HD : (h + 1) * HD], grads[:, h * HD : (h + 1) * HD]], axis=1
            )
            for h in range(groups)
        ],
        axis=0,
    )
    wide = lax.dot_general(both, key_val, (((1,), (1,)), ((), ())), preferred_element_type=F32)
    scores = wide[:, :HD] + bias
    grad_probs = wide[:, HD:]
    top = jnp.max(scores, axis=1, keepdims=True)
    expo = jnp.exp2((scores - top) * scale)
    inverse = jnp.where(row_live, 1.0 / jnp.sum(expo, axis=1, keepdims=True), 0.0)
    probs = expo * inverse
    probs_low = probs.astype(BF16)
    delta = jnp.sum(probs_low.astype(F32) * grad_probs, axis=1, keepdims=True)
    scores_low = (probs * (grad_probs - delta)).astype(BF16)
    low = jnp.concatenate([probs_low, scores_low], axis=1)
    result = jnp.dot(low, val_key, preferred_element_type=F32)
    for h in range(groups):
        rows = slice(h * seq_len, (h + 1) * seq_len)
        cols = slice(h * HD, (h + 1) * HD)
        attn[:, cols] = result[rows, :HD].astype(BF16)
        query_grad[:, cols] = (result[rows, HD:] * inv_root).astype(BF16)
    back = lax.dot_general(low, both, (((0,), (0,)), ((), ())), preferred_element_type=F32)
    val_grad = back[:HD, HD:].astype(BF16)
    key_grad = (back[HD:, :HD] * inv_root).astype(BF16)
    for pick in range(2):
        rows = slice(pick * keys_img, (pick + 1) * keys_img)
        slot_grad[slot_ids[pick]] = jnp.concatenate([key_grad[rows], val_grad[rows]], axis=1)


def weight_kernel(table, place, slot_grad, features, *rest, img_dev):
    outs = rest[:10]
    image_grad, rows, sems = rest[10:]
    slot_total, keys_img, cols = slot_grad.shape
    block = rows.shape[2]
    x_at, z_at = place[0], place[1]
    order = [2, 1, 3, 0]
    steps = sorted(
        [(dx, dz) for dx in range(SIDE) for dz in range(SIDE)],
        key=lambda d: min(order.index(d[0]), order.index(d[1])),
    )

    def fetch(step):
        dx, dz = steps[step]
        dest = lax.rem(x_at + dx, SIDE) * SIDE + lax.rem(z_at + dz, SIDE)
        start = pl.multiple_of(dest * block, block)
        return pltpu.make_async_copy(
            features.at[:, pl.ds(start, block)], rows.at[step], sems.at[step]
        )

    for step in range(len(steps)):
        fetch(step).start()
    image_grad[...] = jnp.zeros_like(image_grad)
    for slot in range(slot_total):
        image = table[slot // CAP, slot % CAP]

        @pl.when(image > 0)
        def _():
            image_grad[image - 1] += slot_grad[slot].astype(F32)

    grad_low = image_grad[...].reshape(img_dev * keys_img, cols).astype(BF16)
    for step, (dx, dz) in enumerate(steps):
        fetch(step).wait()
        part = lax.dot_general(
            grad_low, rows[step], (((0,), (0,)), ((), ())), preferred_element_type=F32
        ).astype(BF16)
        for half, (first, second) in enumerate(((dx, dz), (dz, dx))):
            piece = part[half * HD : (half + 1) * HD]
            five = outs[5 * half : 5 * half + 5]
            if first == 0:
                five[4][second] = piece
            elif first == 1:
                five[0][second] = piece
            elif first == 3:
                five[1][second] = piece
            elif second < 2:
                five[2][second] = piece
            else:
                five[3][second - 2] = piece


def final_kernel(*refs):
    out = refs[-1]
    for half in range(2):
        own, one, two, three = refs[4 * half : 4 * half + 4]
        total = own[...] + one[...].astype(F32) + two[...].astype(F32) + three[...].astype(F32)
        out[:, half, :] = total.T


def shift(values, axis, step):
    pairs = []
    for x in range(SIDE):
        for z in range(SIDE):
            to = ((x + step) % SIDE, z) if axis == "x" else (x, (z + step) % SIDE)
            pairs.append((x * SIDE + z, to[0] * SIDE + to[1]))
    return lax.ppermute(values, "txt", pairs)


def add(*terms):
    return functools.reduce(lambda a, b: a + b, [term.astype(F32) for term in terms])


def shards(features, tile_count, kv_weight, queries, out_grad, image_ids, text_len):
    txt_count = lax.axis_size("txt")
    shard_index = lax.axis_index("txt")
    img_dev, keys_img, feat_width = features.shape
    seq_dev, picks = image_ids.shape
    head_cols = kv_weight.shape[2]
    cols = 2 * head_cols
    request_total = seq_dev * picks
    slot_total = txt_count * CAP
    seq_len = queries.shape[0] // seq_dev
    whole = pl.BlockSpec(memory_space=pltpu.VMEM)
    scalars = pl.BlockSpec(memory_space=pltpu.SMEM)
    params = pltpu.CompilerParams(vmem_limit_bytes=VMEM_LIMIT)

    flat_ids = image_ids.reshape(request_total)
    own_shard, own_position = request_order(flat_ids, img_dev)
    flat_index = own_shard * CAP + own_position
    lane = jnp.arange(128)
    wanted = jnp.sum(
        jnp.where(
            flat_index[None, None, :]
            == jnp.arange(txt_count)[:, None, None] * CAP + lane[None, :, None],
            jnp.where(lane[None, :, None] < CAP, flat_ids % img_dev + 1, 0),
            0,
        ),
        axis=-1,
    )
    counts = jnp.pad(tile_count, (8, 128 - 8 - img_dev))
    table = lax.all_to_all(wanted + counts[None, :], "txt", 0, 0, tiled=True)
    meta = jnp.concatenate([flat_index, flat_ids, text_len])
    place = jnp.stack([shard_index // SIDE, shard_index % SIDE])

    flat_features = features.reshape(img_dev * keys_img, feat_width)
    own_pairs = jnp.dot(
        flat_features, kv_weight.reshape(feat_width, cols), preferred_element_type=F32
    ).astype(BF16)
    sent_pairs = pl.pallas_call(
        fill_kernel,
        out_shape=jax.ShapeDtypeStruct((slot_total, keys_img, cols), BF16),
        in_specs=[scalars, whole],
        out_specs=whole,
        compiler_params=params,
        name="fill_slots",
    )(table, own_pairs.reshape(img_dev, keys_img, cols))
    got_pairs = lax.all_to_all(
        sent_pairs.reshape(txt_count, CAP, keys_img, cols), "txt", 0, 0, tiled=True
    ).reshape(slot_total, keys_img, cols)

    token_block = pl.BlockSpec((seq_len, queries.shape[1]), lambda s, *_: (s, 0))
    slot_block = pl.BlockSpec((slot_total, keys_img, cols), lambda s, *_: (0, 0, 0))
    attended, grad_query, slot_grad = pl.pallas_call(
        functools.partial(attend_kernel, seq_dev=seq_dev, img_dev=img_dev),
        out_shape=[
            jax.ShapeDtypeStruct(queries.shape, BF16),
            jax.ShapeDtypeStruct(queries.shape, BF16),
            jax.ShapeDtypeStruct((slot_total, keys_img, cols), BF16),
        ],
        grid_spec=pltpu.PrefetchScalarGridSpec(
            num_scalar_prefetch=2,
            grid=(seq_dev,),
            in_specs=[token_block, token_block, slot_block],
            out_specs=[token_block, token_block, slot_block],
        ),
        compiler_params=params,
        name="attend",
    )(meta, table, queries, out_grad, got_pairs)

    back_grad = lax.all_to_all(
        slot_grad.reshape(txt_count, CAP, keys_img, cols), "txt", 0, 0, tiled=True
    ).reshape(slot_total, keys_img, cols)

    block = feat_width // txt_count
    message = [(SIDE, HD, block), (SIDE, HD, block), (2, HD, block), (2, HD, block), (SIDE, HD, block)]
    pieces = pl.pallas_call(
        functools.partial(weight_kernel, img_dev=img_dev),
        out_shape=[jax.ShapeDtypeStruct(shape, BF16) for shape in message * 2],
        in_specs=[scalars, scalars, whole, pl.BlockSpec(memory_space=pl.ANY)],
        out_specs=[whole] * 10,
        scratch_shapes=[
            pltpu.VMEM((img_dev, keys_img, cols), F32),
            pltpu.VMEM((txt_count, img_dev * keys_img, block), BF16),
            pltpu.SemaphoreType.DMA((txt_count,)),
        ],
        compiler_params=params,
        name="weight_part",
    )(table, place, back_grad, flat_features)

    final = []
    for half, (first, second) in enumerate((("x", "z"), ("z", "x"))):
        up, down, far_low, far_high, own = pieces[5 * half : 5 * half + 5]
        far_up = shift(far_low, first, 1)
        far_down = shift(far_high, first, -1)
        near_up = shift(up[2:], first, 1)
        near_down = shift(down[:2], first, -1)
        relay_up = shift(add(up[:2], far_up).astype(BF16), first, 1)
        relay_down = shift(add(down[2:], far_down).astype(BF16), first, -1)
        low = add(own[:2], relay_up, near_down)
        high = add(own[2:], near_up, relay_down)
        final += [
            low[0],
            shift(low[1].astype(BF16), second, 1),
            shift(high[0].astype(BF16), second, 2),
            shift(high[1].astype(BF16), second, -1),
        ]
    weight_grad = pl.pallas_call(
        final_kernel,
        out_shape=jax.ShapeDtypeStruct((block, 2, head_cols), F32),
        in_specs=[whole] * 8,
        out_specs=whole,
        compiler_params=params,
        name="weight_total",
    )(*final)
    return attended, grad_query, weight_grad


def solution(mesh):
    in_specs = (
        P("txt", None, None),
        P("txt"),
        P(None, None, "img"),
        P("txt", "img"),
        P("txt", "img"),
        P("txt", None),
        P("txt"),
    )
    out_specs = (P("txt", "img"), P("txt", "img"), P("txt", None, "img"))
    return jax.shard_map(shards, mesh=mesh, in_specs=in_specs, out_specs=out_specs, check_vma=False)
```

time: 291 us -> 131 us (0.45)
  local copies, waits for them, and re-layouts: 73.7 us -> 3.67 us
  waiting for transfers between devices: 90 us -> 50.9 us
  other arithmetic: 33.9 us -> 1.87 us
  matrix products: 37.4 us -> 6.91 us
  Pallas kernels: 0 us -> 29.5 us
  blocking collectives: 24.7 us -> 0 us
  starting transfers between devices: 15.8 us -> 36.6 us
  between operations: 14.3 us -> 0.87 us
    reduce_scatter x1 -> x0, waiting for transfers between devices: 80 us -> none  [shards(): lax.psum_scatter(local_grad, 'txt', scatter_dimension=0, tiled=True)]
    dot_general x20 -> x1, matrix products: 37.4 us -> 6.91 us  [shards(): jnp.dot(flat_features, kv_weight.reshape(feat_width, cols), preferred_ele...]
    pallas_call x0 -> x4, Pallas kernels: none -> 29.5 us  [the longest x1 19.9 us: shards(): pl.pallas_call(functools.partial(attend_kernel, seq_dev=seq_dev, img_dev=...]
    select_n x9 -> x1, other arithmetic: 28.7 us -> 0.07 us  [shards(): jnp.where(lane[None, :, None] < CAP, flat_ids % img_dev + 1, 0)]
    all_gather x1 -> x0, blocking collectives: 24.7 us -> none  [shards(): lax.all_gather(image_ids, 'txt', axis=0, tiled=True)]
    all_to_all x3, waiting for transfers between devices: 10 us -> 32.5 us  [the longest x1 16.8 us: shards(): lax.all_to_all(sent_pairs.reshape(txt_count, CAP, keys_img, cols), 'txt',...]
    gather x7 -> x0, local copies, waits for them, and re-layouts: 18.7 us -> none  [the longest x1 16.4 us: shards(): jnp.take(features, slot_image, axis=0)]
    ppermute x0 -> x18, waiting for transfers between devices: none -> 18.4 us  [shift(): return lax.ppermute(values, 'txt', pairs)]
  transfers between devices with their start and end apart: 4 -> 21, of which waited for: 2 -> 12; matrix products, arithmetic and copies ran while one was open for 23% -> 6% of each run, Pallas kernels for 0% -> 0%
where the time goes in v1:
time: 131 us; the launch traced here: 130 us
  waiting for transfers between devices  50.9 us (39%)
  starting transfers between devices  36.6 us (28%)
  Pallas kernels  29.5 us (23%)
  matrix products  6.91 us (5%)
  local copies, waits for them, and re-layouts  3.67 us (3%)
  other arithmetic  1.87 us (1%)
    pallas_call x1, Pallas kernels, shards(): pl.pallas_call(functools.partial(attend_kernel, seq_dev=seq_dev, img_dev=...  19.9 us
    ppermute x18, waiting for transfers between devices, shift(): return lax.ppermute(values, 'txt', pairs)  18.4 us
    ppermute x18, starting transfers between devices, shift(): return lax.ppermute(values, 'txt', pairs)  18.3 us
    all_to_all x1, waiting for transfers between devices, shards(): lax.all_to_all(sent_pairs.reshape(txt_count, CAP, keys_img, cols), 'txt',...  16.8 us
    all_to_all x1, waiting for transfers between devices, shards(): lax.all_to_all(slot_grad.reshape(txt_count, CAP, keys_img, cols), 'txt',...  15.2 us
    all_to_all x1, starting transfers between devices, shards(): table = lax.all_to_all(wanted + counts[None, :], 'txt', 0, 0, tiled=True)  7.96 us
    dot_general x1, matrix products, shards(): jnp.dot(flat_features, kv_weight.reshape(feat_width, cols), preferred_ele...  6.91 us
    pallas_call x1, Pallas kernels, shards(): pl.pallas_call(functools.partial(weight_kernel, img_dev=img_dev), out_sha...  6.73 us
  transfers between devices with their start and end apart: 21, of which 12 were waited for; matrix products, arithmetic and copies ran while one was open for 6% of the time, Pallas kernels for 0%

profile of v1, /device:TPU:0, one launch (start us, length us, event | category | flops | bytes accessed | tf_op | source)
XLA Modules:
  0.0 130.3 jit_solution(762876648084422511)
XLA Ops:
  0.7 0.8 copy.13
  1.9 0.7 pad.4
  3.3 8.0 %all-to-all-start = ((s32[16,1,128]{2,1,0:T(1,128)}), s32[16,1,128]{2,1,0:T(1,128)S(1)}, u32[]{:S(2)}, u32[]{:S(2)}) async-start(s32[16,1,128]{2,1,0:T(1,128)} %bitcast.1), calls=%async_computation | async-start | bytes 16384 | tf_op jit(solution)/shard_map/all_to_all | solution.py:204
  11.3 6.9 %fusion.3 = bf16[512,256]{1,0:T(8,128)(2,1)S(1)} fusion(bf16[512,8192]{1,0:T(8,128)(2,1)} %bitcast.41, bf16[1024,8,2,128]{3,2,1,0:T(2,128)(2,1)} %bitcast.43), kind=kOutput, calls=%fused_computation.3 | convolution fusion | flops 2147614720 | bytes 12845056 | tf_op jit(solution)/shard_map/dot_general | solution.py:209
  18.8 1.7 %fill_slots.1 = bf16[32,64,256]{2,1,0:T(8,128)(2,1)} custom-call(s32[16,128]{1,0:T(8,128)S(1)} %bitcast.38, bf16[8,64,256]{2,1,0:T(8,128)(2,1)S(1)} %bitcast.37), custom_call_target="tpu_custom_call" | custom-call | tf_op jit(solution)/shard_map/fill_slots/pallas_call | solution.py:212
  20.5 6.7 %all-to-all-start.1 = ((bf16[16,2,64,256]{3,2,1,0:T(8,128)(2,1)}), bf16[16,2,64,256]{3,2,1,0:T(8,128)(2,1)S(1)}, u32[]{:S(2)}, u32[]{:S(2)}) async-start(bf16[16,2,64,256]{3,2,1,0:T(8,128)(2,1)} %bitcast.5), calls=%async_computation.1 | async-start | bytes 2097152 | tf_op jit(solution)/shard_map/all_to_all | solution.py:220
  27.2 16.8 %all-to-all-done.1 = bf16[16,2,64,256]{3,2,1,0:T(8,128)(2,1)S(1)} async-done(((bf16[16,2,64,256]{3,2,1,0:T(8,128)(2,1)}), bf16[16,2,64,256]{3,2,1,0:T(8,128)(2,1)S(1)}, u32[]{:S(2)}, u32[]{:S(2)}) %all-to-all-start.1) | async-done | bytes 1048608 | tf_op jit(solution)/shard_map/all_to_all | solution.py:220
  44.0 1.9 %copy-done = bf16[1536,1024]{1,0:T(8,128)(2,1)S(1)} copy-done((bf16[1536,1024]{1,0:T(8,128)(2,1)S(1)}, bf16[1536,1024]{1,0:T(8,128)(2,1)}, u32[]{:S(2)}) %copy-start) | copy-done | bytes 3145752
  45.9 19.9 %attend.1 = (bf16[1536,1024]{1,0:T(8,128)(2,1)}, bf16[1536,1024]{1,0:T(8,128)(2,1)}, bf16[32,64,256]{2,1,0:T(8,128)(2,1)}) custom-call(s32[60]{0:T(128)S(1)} %pad_add_fusion.meta, s32[16,128]{1,0:T(8,128)S(1)} %bitcast.39, bf16[1536,1024]{1,0:T(8,128)(2,1)S(1)} %copy-done, bf16[1536,1024]{1,0:T(8,128)(2,1)} %grads.1, bf16[32,64,256]{2,1,0:T(8,128)(2,1)S(1)} %bitcast.35), custom_call_target="tpu_custom_call" | custom-call | tf_op jit(solution)/shard_map/attend/pallas_call | solution.py:226
  65.7 3.7 %all-to-all-start.2 = ((bf16[16,2,64,256]{3,2,1,0:T(8,128)(2,1)}), bf16[16,2,64,256]{3,2,1,0:T(8,128)(2,1)S(1)}, u32[]{:S(2)}, u32[]{:S(2)}) async-start(bf16[16,2,64,256]{3,2,1,0:T(8,128)(2,1)} %bitcast.9), calls=%async_computation.2 | async-start | bytes 2097152 | tf_op jit(solution)/shard_map/all_to_all | solution.py:243
  69.5 15.2 %all-to-all-done.2 = bf16[16,2,64,256]{3,2,1,0:T(8,128)(2,1)S(1)} async-done(((bf16[16,2,64,256]{3,2,1,0:T(8,128)(2,1)}), bf16[16,2,64,256]{3,2,1,0:T(8,128)(2,1)S(1)}, u32[]{:S(2)}, u32[]{:S(2)}) %all-to-all-start.2) | async-done | bytes 1048608 | tf_op jit(solution)/shard_map/all_to_all | solution.py:243
  84.7 6.7 %weight_part.1 = (bf16[4,128,512]{2,1,0:T(8,128)(2,1)S(1)}, bf16[4,128,512]{2,1,0:T(8,128)(2,1)S(1)}, bf16[2,128,512]{2,1,0:T(8,128)(2,1)S(1)}, bf16[2,128,512]{...) custom-call(s32[16,128]{1,0:T(8,128)S(1)} %bitcast.40, ...), custom_call_target="tpu_custom_call" | custom-call | tf_op jit(solution)/shard_map/weight_part/pallas_call | solution.py:249
  91.4 1.3 %collective-permute-start.5 = (bf16[2,128,512]{2,1,0:T(8,128)(2,1)S(1)}, bf16[2,128,512]{2,1,0:T(8,128)(2,1)S(1)}, u32[]{:S(2)}, u32[]{:S(2)}) collective-permute-start(bf16[2,128,512]{2,1,0:T(8,128)(2,1)S(1)} %get-tuple-element.23), channel_id=1, source_target_pairs={{0,12},{1,13},{2,14},{3,15},{4,0},{5,1},{6,2},{7,3},{8,4},{9,5},{1... | collective-permute-start | bytes 786440 | tf_op jit(solution)/shard_map/ppermute | solution.py:169
  92.7 0.8 collective-permute-start
  93.5 1.0 collective-permute-start.14
  94.6 1.1 collective-permute-start.9
  95.8 3.8 %collective-permute-done.5 = bf16[2,128,512]{2,1,0:T(8,128)(2,1)S(1)} collective-permute-done((bf16[2,128,512]{2,1,0:T(8,128)(2,1)S(1)}, bf16[2,128,512]{2,1,0:T(8,128)(2,1)S(1)}, u32[]{:S(2)}, u32[]{:S(2)}) %collective-permute-start.5) | collective-permute-done | bytes 262176 | tf_op jit(solution)/shard_map/ppermute | solution.py:169
  99.6 1.1 collective-permute-start.2
  100.8 2.4 %collective-permute-done = bf16[2,128,512]{2,1,0:T(8,128)(2,1)S(1)} collective-permute-done((bf16[2,128,512]{2,1,0:T(8,128)(2,1)S(1)}, bf16[2,128,512]{2,1,0:T(8,128)(2,1)S(1)}, u32[]{:S(2)}, u32[]{:S(2)}) %collective-permute-start) | collective-permute-done | bytes 262176 | tf_op jit(solution)/shard_map/ppermute | solution.py:169
  103.3 2.1 %collective-permute-start.1 = (bf16[2,128,512]{2,1,0:T(8,128)(2,1)S(1)}, bf16[2,128,512]{2,1,0:T(8,128)(2,1)S(1)}, u32[]{:S(2)}, u32[]{:S(2)}) collective-permute-start(bf16[2,128,512]{2,1,0:T(8,128)(2,1)S(1)} %add_convert_fusion.5), channel_id=1, source_target_pairs={{0,4},{1,5},{2,6},{3,7},{4,8},{5,9},{6,10},{7,11},{8,12},{9,13},{1... | collective-permute-start | bytes 786440 | tf_op jit(solution)/shard_map/ppermute | solution.py:169
  106.1 1.0 collective-permute-done.4
  107.2 1.7 %collective-permute-start.11 = (bf16[2,128,512]{2,1,0:T(8,128)(2,1)S(1)}, bf16[2,128,512]{2,1,0:T(8,128)(2,1)S(1)}, u32[]{:S(2)}, u32[]{:S(2)}) collective-permute-start(bf16[2,128,512]{2,1,0:T(8,128)(2,1)S(1)} %slice.78), channel_id=1, source_target_pairs={{0,3},{1,0},{2,1},{3,2},{4,7},{5,4},{6,5},{7,6},{8,11},{9,8},{10,9... | collective-permute-start | bytes 786440 | tf_op jit(solution)/shard_map/ppermute | solution.py:169
  108.9 1.5 %collective-permute-start.15 = (bf16[2,128,512]{2,1,0:T(8,128)(2,1)S(1)}, bf16[2,128,512]{2,1,0:T(8,128)(2,1)S(1)}, u32[]{:S(2)}, u32[]{:S(2)}) collective-permute-start(bf16[2,128,512]{2,1,0:T(8,128)(2,1)S(1)} %add_convert_fusion.1), channel_id=1, source_target_pairs={{0,3},{1,0},{2,1},{3,2},{4,7},{5,4},{6,5},{7,6},{8,11},{9,8},{10,9... | collective-permute-start | bytes 786440 | tf_op jit(solution)/shard_map/ppermute | solution.py:169
  111.2 1.0 collective-permute-start.3
  112.2 3.7 %collective-permute-done.13 = bf16[2,128,512]{2,1,0:T(8,128)(2,1)S(1)} collective-permute-done((bf16[2,128,512]{2,1,0:T(8,128)(2,1)S(1)}, bf16[2,128,512]{2,1,0:T(8,128)(2,1)S(1)}, u32[]{:S(2)}, u32[]{:S(2)}) %collective-permute-start.13) | collective-permute-done | bytes 262176 | tf_op jit(solution)/shard_map/ppermute | solution.py:169
  115.9 2.2 %collective-permute-start.8 = (bf16[128,512]{1,0:T(8,128)(2,1)S(1)}, bf16[128,512]{1,0:T(8,128)(2,1)S(1)}, u32[]{:S(2)}, u32[]{:S(2)}) collective-permute-start(bf16[128,512]{1,0:T(8,128)(2,1)S(1)} %get-tuple-element.35), channel_id=1, source_target_pairs={{0,3},{1,0},{2,1},{3,2},{4,7},{5,4},{6,5},{7,6},{8,11},{9,8},{10,9... | collective-permute-start | bytes 393224 | tf_op jit(solution)/shard_map/ppermute | solution.py:169
  118.0 1.1 collective-permute-done.15
  119.2 1.0 collective-permute-done.10
  120.6 2.7 %collective-permute-start.16 = (bf16[128,512]{1,0:T(8,128)(2,1)S(1)}, bf16[128,512]{1,0:T(8,128)(2,1)S(1)}, u32[]{:S(2)}, u32[]{:S(2)}) collective-permute-start(bf16[128,512]{1,0:T(8,128)(2,1)S(1)} %get-tuple-element.34), channel_id=1, source_target_pairs={{0,8},{1,9},{2,10},{3,11},{4,12},{5,13},{6,14},{7,15},{8,0},{9,1},... | collective-permute-start | bytes 393224 | tf_op jit(solution)/shard_map/ppermute | solution.py:169
  124.0 4.1 %collective-permute-done.12.refs_5_ = bf16[128,512]{1,0:T(8,128)(2,1)S(1)} collective-permute-done((bf16[128,512]{1,0:T(8,128)(2,1)S(1)}, bf16[128,512]{1,0:T(8,128)(2,1)S(1)}, u32[]{:S(2)}, u32[]{:S(2)}) %collective-permute-start.12) | collective-permute-done | bytes 131104 | tf_op jit(solution)/shard_map/ppermute | solution.py:169
  128.1 1.0 collective-permute-done.17.refs_7_
  129.1 1.2 weight_total.1
  (48 shorter events, 4.7 us)
Async XLA Ops:
  3.3 15.5 %all-to-all-start = ((s32[16,1,128]{2,1,0:T(1,128)}), s32[16,1,128]{2,1,0:T(1,128)S(1)}, u32[]{:S(2)}, u32[]{:S(2)}) async-start(s32[16,1,128]{2,1,0:T(1,128)} %bitcast.1), calls=%async_computation | async-start | bytes 16384 | tf_op jit(solution)/shard_map/all_to_all | solution.py:204
  11.3 15.9 %copy-start.1 = (s32[12]{0:T(128)S(1)}, s32[12]{0:T(128)}, u32[]{:S(2)}) copy-start(s32[12]{0:T(128)} %param.13) | copy-start | bytes 148
  20.5 23.5 %all-to-all-start.1 = ((bf16[16,2,64,256]{3,2,1,0:T(8,128)(2,1)}), bf16[16,2,64,256]{3,2,1,0:T(8,128)(2,1)S(1)}, u32[]{:S(2)}, u32[]{:S(2)}) async-start(bf16[16,2,64,256]{3,2,1,0:T(8,128)(2,1)} %bitcast.5), calls=%async_computation.1 | async-start | bytes 2097152 | tf_op jit(solution)/shard_map/all_to_all | solution.py:220
  44.0 1.9 %copy-start = (bf16[1536,1024]{1,0:T(8,128)(2,1)S(1)}, bf16[1536,1024]{1,0:T(8,128)(2,1)}, u32[]{:S(2)}) copy-start(bf16[1536,1024]{1,0:T(8,128)(2,1)} %queries.1) | copy-start | bytes 9437188
  65.7 18.9 %all-to-all-start.2 = ((bf16[16,2,64,256]{3,2,1,0:T(8,128)(2,1)}), bf16[16,2,64,256]{3,2,1,0:T(8,128)(2,1)S(1)}, u32[]{:S(2)}, u32[]{:S(2)}) async-start(bf16[16,2,64,256]{3,2,1,0:T(8,128)(2,1)} %bitcast.9), calls=%async_computation.2 | async-start | bytes 2097152 | tf_op jit(solution)/shard_map/all_to_all | solution.py:243
  91.4 8.2 %collective-permute-start.5 = (bf16[2,128,512]{2,1,0:T(8,128)(2,1)S(1)}, bf16[2,128,512]{2,1,0:T(8,128)(2,1)S(1)}, u32[]{:S(2)}, u32[]{:S(2)}) collective-permute-start(bf16[2,128,512]{2,1,0:T(8,128)(2,1)S(1)} %get-tuple-element.23), channel_id=1, source_target_pairs={{0,12},{1,13},{2,14},{3,15},{4,0},{5,1},{6,2},{7,3},{8,4},{9,5},{1... | collective-permute-start | bytes 786440 | tf_op jit(solution)/shard_map/ppermute | solution.py:169
  92.7 10.5 %collective-permute-start = (bf16[2,128,512]{2,1,0:T(8,128)(2,1)S(1)}, bf16[2,128,512]{2,1,0:T(8,128)(2,1)S(1)}, u32[]{:S(2)}, u32[]{:S(2)}) collective-permute-start(bf16[2,128,512]{2,1,0:T(8,128)(2,1)S(1)} %get-tuple-element.21), channel_id=1, source_target_pairs={{0,4},{1,5},{2,6},{3,7},{4,8},{5,9},{6,10},{7,11},{8,12},{9,13},{1... | collective-permute-start | bytes 786440 | tf_op jit(solution)/shard_map/ppermute | solution.py:169
  93.5 9.8 %collective-permute-start.14 = (bf16[2,128,512]{2,1,0:T(8,128)(2,1)S(1)}, bf16[2,128,512]{2,1,0:T(8,128)(2,1)S(1)}, u32[]{:S(2)}, u32[]{:S(2)}) collective-permute-start(bf16[2,128,512]{2,1,0:T(8,128)(2,1)S(1)} %get-tuple-element.28), channel_id=1, source_target_pairs={{0,3},{1,0},{2,1},{3,2},{4,7},{5,4},{6,5},{7,6},{8,11},{9,8},{10,9... | collective-permute-start | bytes 786440 | tf_op jit(solution)/shard_map/ppermute | solution.py:169
  94.6 10.9 %collective-permute-start.9 = (bf16[2,128,512]{2,1,0:T(8,128)(2,1)S(1)}, bf16[2,128,512]{2,1,0:T(8,128)(2,1)S(1)}, u32[]{:S(2)}, u32[]{:S(2)}) collective-permute-start(bf16[2,128,512]{2,1,0:T(8,128)(2,1)S(1)} %get-tuple-element.26), channel_id=1, source_target_pairs={{0,1},{1,2},{2,3},{3,0},{4,5},{5,6},{6,7},{7,4},{8,9},{9,10},{10,1... | collective-permute-start | bytes 786440 | tf_op jit(solution)/shard_map/ppermute | solution.py:169
  95.6 11.5 %collective-permute-start.4 = (bf16[2,128,512]{2,1,0:T(8,128)(2,1)S(1)}, bf16[2,128,512]{2,1,0:T(8,128)(2,1)S(1)}, u32[]{:S(2)}, u32[]{:S(2)}) collective-permute-start(bf16[2,128,512]{2,1,0:T(8,128)(2,1)S(1)} %slice.72), channel_id=1, source_target_pairs={{0,4},{1,5},{2,6},{3,7},{4,8},{5,9},{6,10},{7,11},{8,12},{9,13},{1... | collective-permute-start | bytes 786440 | tf_op jit(solution)/shard_map/ppermute | solution.py:169
  99.6 9.3 %collective-permute-start.2 = (bf16[2,128,512]{2,1,0:T(8,128)(2,1)S(1)}, bf16[2,128,512]{2,1,0:T(8,128)(2,1)S(1)}, u32[]{:S(2)}, u32[]{:S(2)}) collective-permute-start(bf16[2,128,512]{2,1,0:T(8,128)(2,1)S(1)} %slice.68), channel_id=1, source_target_pairs={{0,12},{1,13},{2,14},{3,15},{4,0},{5,1},{6,2},{7,3},{8,4},{9,5},{1... | collective-permute-start | bytes 786440 | tf_op jit(solution)/shard_map/ppermute | solution.py:169
  103.2 7.3 %collective-permute-start.6 = (bf16[2,128,512]{2,1,0:T(8,128)(2,1)S(1)}, bf16[2,128,512]{2,1,0:T(8,128)(2,1)S(1)}, u32[]{:S(2)}, u32[]{:S(2)}) collective-permute-start(bf16[2,128,512]{2,1,0:T(8,128)(2,1)S(1)} %add_convert_fusion.4), channel_id=1, source_target_pairs={{0,12},{1,13},{2,14},{3,15},{4,0},{5,1},{6,2},{7,3},{8,4},{9,5},{1... | collective-permute-start | bytes 786440 | tf_op jit(solution)/shard_map/ppermute | solution.py:169
  103.3 7.7 %collective-permute-start.1 = (bf16[2,128,512]{2,1,0:T(8,128)(2,1)S(1)}, bf16[2,128,512]{2,1,0:T(8,128)(2,1)S(1)}, u32[]{:S(2)}, u32[]{:S(2)}) collective-permute-start(bf16[2,128,512]{2,1,0:T(8,128)(2,1)S(1)} %add_convert_fusion.5), channel_id=1, source_target_pairs={{0,4},{1,5},{2,6},{3,7},{4,8},{5,9},{6,10},{7,11},{8,12},{9,13},{1... | collective-permute-start | bytes 786440 | tf_op jit(solution)/shard_map/ppermute | solution.py:169
  105.4 10.4 %collective-permute-start.13 = (bf16[2,128,512]{2,1,0:T(8,128)(2,1)S(1)}, bf16[2,128,512]{2,1,0:T(8,128)(2,1)S(1)}, u32[]{:S(2)}, u32[]{:S(2)}) collective-permute-start(bf16[2,128,512]{2,1,0:T(8,128)(2,1)S(1)} %slice.82), channel_id=1, source_target_pairs={{0,1},{1,2},{2,3},{3,0},{4,5},{5,6},{6,7},{7,4},{8,9},{9,10},{10,1... | collective-permute-start | bytes 786440 | tf_op jit(solution)/shard_map/ppermute | solution.py:169
  107.2 8.7 %collective-permute-start.11 = (bf16[2,128,512]{2,1,0:T(8,128)(2,1)S(1)}, bf16[2,128,512]{2,1,0:T(8,128)(2,1)S(1)}, u32[]{:S(2)}, u32[]{:S(2)}) collective-permute-start(bf16[2,128,512]{2,1,0:T(8,128)(2,1)S(1)} %slice.78), channel_id=1, source_target_pairs={{0,3},{1,0},{2,1},{3,2},{4,7},{5,4},{6,5},{7,6},{8,11},{9,8},{10,9... | collective-permute-start | bytes 786440 | tf_op jit(solution)/shard_map/ppermute | solution.py:169
  108.9 10.3 %collective-permute-start.15 = (bf16[2,128,512]{2,1,0:T(8,128)(2,1)S(1)}, bf16[2,128,512]{2,1,0:T(8,128)(2,1)S(1)}, u32[]{:S(2)}, u32[]{:S(2)}) collective-permute-start(bf16[2,128,512]{2,1,0:T(8,128)(2,1)S(1)} %add_convert_fusion.1), channel_id=1, source_target_pairs={{0,3},{1,0},{2,1},{3,2},{4,7},{5,4},{6,5},{7,6},{8,11},{9,8},{10,9... | collective-permute-start | bytes 786440 | tf_op jit(solution)/shard_map/ppermute | solution.py:169
  110.4 9.8 %collective-permute-start.10 = (bf16[2,128,512]{2,1,0:T(8,128)(2,1)S(1)}, bf16[2,128,512]{2,1,0:T(8,128)(2,1)S(1)}, u32[]{:S(2)}, u32[]{:S(2)}) collective-permute-start(bf16[2,128,512]{2,1,0:T(8,128)(2,1)S(1)} %add_convert_fusion.2), channel_id=1, source_target_pairs={{0,1},{1,2},{2,3},{3,0},{4,5},{5,6},{6,7},{7,4},{8,9},{9,10},{10,1... | collective-permute-start | bytes 786440 | tf_op jit(solution)/shard_map/ppermute | solution.py:169
  111.2 12.3 %collective-permute-start.3 = (bf16[128,512]{1,0:T(8,128)(2,1)S(1)}, bf16[128,512]{1,0:T(8,128)(2,1)S(1)}, u32[]{:S(2)}, u32[]{:S(2)}) collective-permute-start(bf16[128,512]{1,0:T(8,128)(2,1)S(1)} %fusion.6), channel_id=1, source_target_pairs={{0,1},{1,2},{2,3},{3,0},{4,5},{5,6},{6,7},{7,4},{8,9},{9,10},{10,1... | collective-permute-start | bytes 393224 | tf_op jit(solution)/shard_map/ppermute | solution.py:169
  115.9 8.1 %collective-permute-start.7 = (bf16[128,512]{1,0:T(8,128)(2,1)S(1)}, bf16[128,512]{1,0:T(8,128)(2,1)S(1)}, u32[]{:S(2)}, u32[]{:S(2)}) collective-permute-start(bf16[128,512]{1,0:T(8,128)(2,1)S(1)} %get-tuple-element.36), channel_id=1, source_target_pairs={{0,2},{1,3},{2,0},{3,1},{4,6},{5,7},{6,4},{7,5},{8,10},{9,11},{10,... | collective-permute-start | bytes 393224 | tf_op jit(solution)/shard_map/ppermute | solution.py:169
  115.9 8.1 %collective-permute-start.8 = (bf16[128,512]{1,0:T(8,128)(2,1)S(1)}, bf16[128,512]{1,0:T(8,128)(2,1)S(1)}, u32[]{:S(2)}, u32[]{:S(2)}) collective-permute-start(bf16[128,512]{1,0:T(8,128)(2,1)S(1)} %get-tuple-element.35), channel_id=1, source_target_pairs={{0,3},{1,0},{2,1},{3,2},{4,7},{5,4},{6,5},{7,6},{8,11},{9,8},{10,9... | collective-permute-start | bytes 393224 | tf_op jit(solution)/shard_map/ppermute | solution.py:169
  120.4 7.7 %collective-permute-start.12 = (bf16[128,512]{1,0:T(8,128)(2,1)S(1)}, bf16[128,512]{1,0:T(8,128)(2,1)S(1)}, u32[]{:S(2)}, u32[]{:S(2)}) collective-permute-start(bf16[128,512]{1,0:T(8,128)(2,1)S(1)} %fusion.7), channel_id=1, source_target_pairs={{0,4},{1,5},{2,6},{3,7},{4,8},{5,9},{6,10},{7,11},{8,12},{9,13},{1... | collective-permute-start | bytes 393224 | tf_op jit(solution)/shard_map/ppermute | solution.py:169
  120.6 7.5 %collective-permute-start.16 = (bf16[128,512]{1,0:T(8,128)(2,1)S(1)}, bf16[128,512]{1,0:T(8,128)(2,1)S(1)}, u32[]{:S(2)}, u32[]{:S(2)}) collective-permute-start(bf16[128,512]{1,0:T(8,128)(2,1)S(1)} %get-tuple-element.34), channel_id=1, source_target_pairs={{0,8},{1,9},{2,10},{3,11},{4,12},{5,13},{6,14},{7,15},{8,0},{9,1},... | collective-permute-start | bytes 393224 | tf_op jit(solution)/shard_map/ppermute | solution.py:169
  123.5 5.6 %collective-permute-start.17 = (bf16[128,512]{1,0:T(8,128)(2,1)S(1)}, bf16[128,512]{1,0:T(8,128)(2,1)S(1)}, u32[]{:S(2)}, u32[]{:S(2)}) collective-permute-start(bf16[128,512]{1,0:T(8,128)(2,1)S(1)} %get-tuple-element.33), channel_id=1, source_target_pairs={{0,12},{1,13},{2,14},{3,15},{4,0},{5,1},{6,2},{7,3},{8,4},{9,5},{1... | collective-permute-start | bytes 393224 | tf_op jit(solution)/shard_map/ppermute | solution.py:169

commit v2 on v1

v2 whole, which is shorter than its diff:
```python
import functools
import math

import jax
import jax.numpy as jnp
from jax import lax
from jax.experimental import pallas as pl
from jax.experimental.pallas import tpu as pltpu
from jax.sharding import PartitionSpec as P

HD = 128
MAXT = 4
SIDE = 4
CAP = 2
BF16 = jnp.bfloat16
F32 = jnp.float32
MIB = 1024 * 1024


def request_kernel(ids, counts, table, meta, seen, *, img_dev):
    shards, lanes = table.shape
    picks, seq_dev = ids.shape
    for shard in range(shards):
        seen[shard] = 0
    row = lax.broadcasted_iota(jnp.int32, (shards, lanes), 0)
    lane = lax.broadcasted_iota(jnp.int32, (shards, lanes), 1)
    value = jnp.zeros((shards, lanes), jnp.int32)
    for image in range(img_dev):
        value = jnp.where(lane == 8 + image, counts[image], value)
    for request in range(picks * seq_dev):
        image = ids[request % picks, request // picks]
        shard = image // img_dev
        position = seen[shard]
        seen[shard] = position + 1
        value = jnp.where(
            jnp.logical_and(row == shard, lane == position), image % img_dev + 1, value
        )
        meta[request] = shard * CAP + position
        meta[picks * seq_dev + request] = image
    table[...] = value


def fill_kernel(table, pairs, slots):
    for slot in range(slots.shape[0]):
        image = jnp.maximum(table[slot // CAP, slot % CAP] - 1, 0)
        slots[slot] = pairs[image]


def attend_kernel(meta, table, lengths, queries, grads, slots, attn, query_grad, slot_grad, *scratch, img_dev):
    q_all, g_all, out_all, dq_all, sems = scratch
    seq_dev = lengths.shape[0]
    seq_len = queries.shape[0] // seq_dev
    groups = queries.shape[1] // HD
    keys_img = slots.shape[1]
    inv_root = 1.0 / math.sqrt(HD)
    scale = inv_root * math.log2(math.e)
    unroll = 6

    def rows_of(seq):
        return pl.ds(pl.multiple_of(seq * seq_len, seq_len), seq_len)

    ends = ((queries, q_all), (grads, g_all), (out_all, attn), (dq_all, query_grad))

    def copies(seq, kinds):
        rows = rows_of(seq)
        return [
            pltpu.make_async_copy(
                ends[kind][0].at[rows], ends[kind][1].at[rows], sems.at[kind, seq]
            )
            for kind in kinds
        ]

    def begin(seq):
        for copy in copies(seq, (0, 1)):
            copy.wait()
        slot_ids = [meta[2 * seq + pick] for pick in range(2)]
        images = [meta[2 * seq_dev + 2 * seq + pick] for pick in range(2)]
        tiles = [table[image // img_dev, 8 + image % img_dev] for image in images]
        pair = [slots[slot] for slot in slot_ids]
        keys = jnp.concatenate([blk[:, :HD] for blk in pair], axis=0)
        vals = jnp.concatenate([blk[:, HD:] for blk in pair], axis=0)
        none = jnp.zeros_like(keys)
        key_val = jnp.concatenate(
            [jnp.concatenate([keys, none], axis=1), jnp.concatenate([none, vals], axis=1)], axis=0
        )
        val_key = jnp.concatenate(
            [jnp.concatenate([vals, none], axis=1), jnp.concatenate([none, keys], axis=1)], axis=0
        )
        key = lax.broadcasted_iota(jnp.int32, (2 * keys_img, 1), 0)
        tile_rows = keys_img // MAXT
        live_to = jnp.where(key < keys_img, tiles[0] * tile_rows, keys_img + tiles[1] * tile_rows)
        bias = jnp.where(key < live_to, 0.0, -jnp.inf).astype(F32)
        rows = rows_of(seq)
        both = jnp.concatenate(
            [
                jnp.concatenate(
                    [q_all[rows, h * HD : (h + 1) * HD], g_all[rows, h * HD : (h + 1) * HD]], axis=1
                )
                for h in range(groups)
            ],
            axis=0,
        )
        wide = lax.dot_general(key_val, both, (((1,), (1,)), ((), ())), preferred_element_type=F32)
        return slot_ids, val_key, both, wide[: 2 * keys_img] + bias, wide[2 * keys_img :]

    def finish(seq, state):
        slot_ids, val_key, both, scores, grad_probs = state
        token = lax.broadcasted_iota(jnp.int32, (1, groups * seq_len), 1)
        live = token % seq_len < lengths[seq]
        top = jnp.max(scores, axis=0, keepdims=True)
        expo = jnp.exp2((scores - top) * scale)
        probs = expo * jnp.where(live, 1.0 / jnp.sum(expo, axis=0, keepdims=True), 0.0)
        probs_low = probs.astype(BF16)
        delta = jnp.sum(probs_low.astype(F32) * grad_probs, axis=0, keepdims=True)
        scores_low = (probs * (grad_probs - delta)).astype(BF16)
        low = jnp.concatenate([probs_low, scores_low], axis=0)
        back = jnp.dot(low, both, preferred_element_type=F32)
        result = lax.dot_general(low, val_key, (((0,), (0,)), ((), ())), preferred_element_type=F32)
        rows = rows_of(seq)
        for h in range(groups):
            part = result[h * seq_len : (h + 1) * seq_len]
            out_all[rows, h * HD : (h + 1) * HD] = part[:, :HD].astype(BF16)
            dq_all[rows, h * HD : (h + 1) * HD] = (part[:, HD:] * inv_root).astype(BF16)
        for copy in copies(seq, (2, 3)):
            copy.start()
        val_grad = back[: 2 * keys_img, HD:].astype(BF16)
        key_grad = (back[2 * keys_img :, :HD] * inv_root).astype(BF16)
        for pick in range(2):
            part = slice(pick * keys_img, (pick + 1) * keys_img)
            slot_grad[slot_ids[pick]] = jnp.concatenate([key_grad[part], val_grad[part]], axis=1)

    for seq in range(seq_dev):
        for copy in copies(seq, (0, 1)):
            copy.start()

    @pl.loop(0, seq_dev // unroll)
    def _(turn):
        state = begin(turn * unroll)
        for step in range(unroll):
            seq = turn * unroll + step
            after = begin(seq + 1) if step + 1 < unroll else None
            finish(seq, state)
            state = after

    for seq in range(seq_dev):
        for copy in copies(seq, (2, 3)):
            copy.wait()


def weight_kernel(table, place, slot_grad, features, *rest, img_dev):
    outs = rest[:10]
    image_grad, grad_low, rows, sems = rest[10:]
    slot_total, keys_img, cols = slot_grad.shape
    block = outs[0].shape[2]
    x_at, z_at = place[0], place[1]
    order = (2, 1, 3, 0)

    def fetch(dx):
        start = pl.multiple_of(lax.rem(x_at + dx, SIDE) * (SIDE * block), SIDE * block)
        return pltpu.make_async_copy(
            features.at[:, pl.ds(start, SIDE * block)], rows.at[dx], sems.at[dx]
        )

    for dx in order:
        fetch(dx).start()
    image_grad[...] = jnp.zeros_like(image_grad)
    for slot in range(slot_total):
        image = table[slot // CAP, slot % CAP]

        @pl.when(image > 0)
        def _():
            image_grad[image - 1] += slot_grad[slot].astype(F32)

    grad_low[...] = image_grad[...].reshape(img_dev * keys_img, cols).T.astype(BF16)
    for dx in order:
        fetch(dx).wait()
        for dz in range(SIDE):
            start = pl.multiple_of(lax.rem(z_at + dz, SIDE) * block, block)
            part = jnp.dot(
                grad_low[...], rows[dx, :, pl.ds(start, block)], preferred_element_type=F32
            ).astype(BF16)
            for half, (first, second) in enumerate(((dx, dz), (dz, dx))):
                piece = part[half * HD : (half + 1) * HD]
                five = outs[5 * half : 5 * half + 5]
                if first == 0:
                    five[4][second] = piece
                elif first == 1:
                    five[0][second] = piece
                elif first == 3:
                    five[1][second] = piece
                elif second < 2:
                    five[2][second] = piece
                else:
                    five[3][second - 2] = piece


def final_kernel(*refs):
    out = refs[-1]
    for half in range(2):
        own, one, two, three = refs[4 * half : 4 * half + 4]
        total = own[...] + one[...].astype(F32) + two[...].astype(F32) + three[...].astype(F32)
        out[:, half, :] = total.T


def shift(values, axis, step):
    pairs = []
    for x in range(SIDE):
        for z in range(SIDE):
            to = ((x + step) % SIDE, z) if axis == "x" else (x, (z + step) % SIDE)
            pairs.append((x * SIDE + z, to[0] * SIDE + to[1]))
    return lax.ppermute(values, "txt", pairs)


def add(*terms):
    return functools.reduce(lambda a, b: a + b, [term.astype(F32) for term in terms])


def shards(features, tile_count, kv_weight, queries, out_grad, image_ids, text_len):
    txt_count = lax.axis_size("txt")
    shard_index = lax.axis_index("txt")
    img_dev, keys_img, feat_width = features.shape
    seq_dev, picks = image_ids.shape
    head_cols = kv_weight.shape[2]
    cols = 2 * head_cols
    request_total = seq_dev * picks
    slot_total = txt_count * CAP
    whole = pl.BlockSpec(memory_space=pltpu.VMEM)
    scalars = pl.BlockSpec(memory_space=pltpu.SMEM)

    def params(mib):
        return pltpu.CompilerParams(vmem_limit_bytes=mib * MIB)


    wanted, meta = pl.pallas_call(
        functools.partial(request_kernel, img_dev=img_dev),
        out_shape=[
            jax.ShapeDtypeStruct((txt_count, 128), jnp.int32),
            jax.ShapeDtypeStruct((2 * request_total,), jnp.int32),
        ],
        in_specs=[scalars, scalars],
        out_specs=[whole, scalars],
        scratch_shapes=[pltpu.SMEM((txt_count,), jnp.int32)],
        name="request_table",
    )(image_ids.T, tile_count)
    table = lax.all_to_all(wanted, "txt", 0, 0, tiled=True)
    place = jnp.stack([shard_index // SIDE, shard_index % SIDE])

    flat_features = features.reshape(img_dev * keys_img, feat_width)
    own_pairs = jnp.dot(
        flat_features, kv_weight.reshape(feat_width, cols), preferred_element_type=F32
    ).astype(BF16)
    sent_pairs = pl.pallas_call(
        fill_kernel,
        out_shape=jax.ShapeDtypeStruct((slot_total, keys_img, cols), BF16),
        in_specs=[scalars, whole],
        out_specs=whole,
        compiler_params=params(8),
        name="fill_slots",
    )(table, own_pairs.reshape(img_dev, keys_img, cols))
    got_pairs = lax.all_to_all(
        sent_pairs.reshape(txt_count, CAP, keys_img, cols), "txt", 0, 0, tiled=True
    ).reshape(slot_total, keys_img, cols)

    in_hbm = pl.BlockSpec(memory_space=pltpu.HBM)
    attended, grad_query, slot_grad = pl.pallas_call(
        functools.partial(attend_kernel, img_dev=img_dev),
        out_shape=[
            jax.ShapeDtypeStruct(queries.shape, BF16),
            jax.ShapeDtypeStruct(queries.shape, BF16),
            jax.ShapeDtypeStruct((slot_total, keys_img, cols), BF16),
        ],
        in_specs=[scalars, scalars, scalars, in_hbm, in_hbm, whole],
        out_specs=[in_hbm, in_hbm, whole],
        scratch_shapes=[pltpu.VMEM(queries.shape, BF16)] * 4
        + [pltpu.SemaphoreType.DMA((4, seq_dev))],
        compiler_params=params(24),
        name="attend",
    )(meta, table, text_len, *[pltpu.with_memory_space_constraint(x, pltpu.HBM) for x in (queries, out_grad)], got_pairs)
    back_grad = lax.all_to_all(
        slot_grad.reshape(txt_count, CAP, keys_img, cols), "txt", 0, 0, tiled=True
    ).reshape(slot_total, keys_img, cols)

    block = feat_width // txt_count
    message = [(SIDE, HD, block), (SIDE, HD, block), (2, HD, block), (2, HD, block), (SIDE, HD, block)]
    pieces = pl.pallas_call(
        functools.partial(weight_kernel, img_dev=img_dev),
        out_shape=[jax.ShapeDtypeStruct(shape, BF16) for shape in message * 2],
        in_specs=[scalars, scalars, whole, in_hbm],
        out_specs=[whole] * 10,
        scratch_shapes=[
            pltpu.VMEM((img_dev, keys_img, cols), F32),
            pltpu.VMEM((cols, img_dev * keys_img), BF16),
            pltpu.VMEM((SIDE, img_dev * keys_img, SIDE * block), BF16),
            pltpu.SemaphoreType.DMA((SIDE,)),
        ],
        compiler_params=params(20),
        name="weight_part",
    )(table, place, back_grad, pltpu.with_memory_space_constraint(flat_features, pltpu.HBM))

    final = []
    for half, (first, second) in enumerate((("x", "z"), ("z", "x"))):
        up, down, far_low, far_high, own = pieces[5 * half : 5 * half + 5]
        far_up = shift(far_low, first, 1)
        far_down = shift(far_high, first, -1)
        near_up = shift(up[2:], first, 1)
        near_down = shift(down[:2], first, -1)
        relay_up = shift(add(up[:2], far_up).astype(BF16), first, 1)
        relay_down = shift(add(down[2:], far_down).astype(BF16), first, -1)
        low = add(own[:2], relay_up, near_down)
        high = add(own[2:], near_up, relay_down)
        final += [
            low[0],
            shift(low[1].astype(BF16), second, 1),
            shift(high[0].astype(BF16), second, 2),
            shift(high[1].astype(BF16), second, -1),
        ]
    weight_grad = pl.pallas_call(
        final_kernel,
        out_shape=jax.ShapeDtypeStruct((block, 2, head_cols), F32),
        in_specs=[whole] * 8,
        out_specs=whole,
        compiler_params=params(8),
        name="weight_total",
    )(*final)
    return attended, grad_query, weight_grad


def solution(mesh):
    in_specs = (
        P("txt", None, None),
        P("txt"),
        P(None, None, "img"),
        P("txt", "img"),
        P("txt", "img"),
        P("txt", None),
        P("txt"),
    )
    out_specs = (P("txt", "img"), P("txt", "img"), P("txt", None, "img"))
    return jax.shard_map(shards, mesh=mesh, in_specs=in_specs, out_specs=out_specs, check_vma=False)
```

time: 131 us -> 117 us (0.89)
  blocking collectives: 0 us -> 23 us
  waiting for transfers between devices: 50.9 us -> 34.4 us
  Pallas kernels: 29.5 us -> 20.4 us
  starting transfers between devices: 36.6 us -> 29.8 us
  local copies, waits for them, and re-layouts: 3.67 us -> 0.2 us
    all_to_all x0 -> x1, blocking collectives: none -> 23 us  [shards(): lax.all_to_all(sent_pairs.reshape(txt_count, CAP, keys_img, cols), 'txt',...]
    all_to_all x2 -> x1, waiting for transfers between devices: 17.3 us -> 0.54 us  [shards(): table = lax.all_to_all(wanted, 'txt', 0, 0, tiled=True)]
    all_to_all x2 -> x1, starting transfers between devices: 14.6 us -> 7.97 us  [shards(): table = lax.all_to_all(wanted, 'txt', 0, 0, tiled=True)]
    pallas_call x1 -> x2, Pallas kernels: 19.9 us -> 13.3 us  [the longest x1 11.8 us: shards(): pl.pallas_call(functools.partial(attend_kernel, img_dev=img_dev), out_sha...]
    unnamed x5 -> x4, local copies, waits for them, and re-layouts: 2.67 us -> 0.01 us
    pallas_call x1, Pallas kernels: 6.73 us -> 5.18 us  [shards(): pl.pallas_call(functools.partial(weight_kernel, img_dev=img_dev), out_sha...]
  transfers between devices with their start and end apart: 21 -> 20, of which waited for: 12 -> 11; matrix products, arithmetic and copies ran while one was open for 6% -> 7% of each run, Pallas kernels for 0% -> 0%
where the time goes in v2:
time: 117 us; the launch traced here: 116 us
  waiting for transfers between devices  34.4 us (29%)
  starting transfers between devices  29.8 us (25%)
  blocking collectives  23 us (20%)
  Pallas kernels  20.4 us (17%)
  matrix products  6.91 us (6%)
    all_to_all x1, blocking collectives, shards(): lax.all_to_all(sent_pairs.reshape(txt_count, CAP, keys_img, cols), 'txt',...  23 us
    ppermute x18, waiting for transfers between devices, shift(): return lax.ppermute(values, 'txt', pairs)  18.8 us
    ppermute x18, starting transfers between devices, shift(): return lax.ppermute(values, 'txt', pairs)  18.1 us
    all_to_all x1, waiting for transfers between devices, shards(): lax.all_to_all(slot_grad.reshape(txt_count, CAP, keys_img, cols), 'txt',...  15 us
    pallas_call x1, Pallas kernels, shards(): pl.pallas_call(functools.partial(attend_kernel, img_dev=img_dev), out_sha...  11.8 us
    all_to_all x1, starting transfers between devices, shards(): table = lax.all_to_all(wanted, 'txt', 0, 0, tiled=True)  7.97 us
    dot_general x1, matrix products, shards(): jnp.dot(flat_features, kv_weight.reshape(feat_width, cols), preferred_ele...  6.91 us
    pallas_call x1, Pallas kernels, shards(): pl.pallas_call(functools.partial(weight_kernel, img_dev=img_dev), out_sha...  5.18 us
  transfers between devices with their start and end apart: 20, of which 11 were waited for; matrix products, arithmetic and copies ran while one was open for 7% of the time, Pallas kernels for 0%

profile of v2, /device:TPU:0, one launch (start us, length us, event | category | flops | bytes accessed | tf_op | source)
XLA Modules:
  0.0 116.3 jit_solution(16130663479551398062)
XLA Ops:
  0.6 1.5 %request_table.1 = (s32[16,128]{1,0:T(8,128)}, s32[48]{0:T(128)}) custom-call(s32[2,12]{1,0:T(2,128)} %bitcast.47, s32[8]{0:T(128)} %counts.1), custom_call_target="tpu_custom_call" | custom-call | tf_op jit(solution)/shard_map/request_table/pallas_call | solution.py:234
  2.1 8.0 %all-to-all-start = ((s32[16,1,128]{2,1,0:T(1,128)}), s32[16,1,128]{2,1,0:T(1,128)S(1)}, u32[]{:S(2)}, u32[]{:S(2)}) async-start(s32[16,1,128]{2,1,0:T(1,128)} %bitcast.45), calls=%async_computation | async-start | bytes 16384 | tf_op jit(solution)/shard_map/all_to_all | solution.py:245
  10.1 6.9 %fusion.3 = bf16[512,256]{1,0:T(8,128)(2,1)S(1)} fusion(bf16[512,8192]{1,0:T(8,128)(2,1)} %bitcast.43, bf16[1024,8,2,128]{3,2,1,0:T(2,128)(2,1)} %bitcast.46), kind=kOutput, calls=%fused_computation.3 | convolution fusion | flops 2147614720 | bytes 12845056 | tf_op jit(solution)/shard_map/dot_general | solution.py:249
  17.6 0.7 fill_slots.1
  18.3 23.0 %all_to_all.21 = bf16[16,2,64,256]{3,2,1,0:T(8,128)(2,1)S(1)} all-to-all(bf16[16,2,64,256]{3,2,1,0:T(8,128)(2,1)S(1)} %bitcast.37), channel_id=1, replica_groups=mesh['img'=8,'txt'=16] {'txt'}, dimensions={0} | all-to-all | bytes 2097152 | tf_op jit(solution)/shard_map/all_to_all | solution.py:260
  41.4 11.8 %attend.1 = (bf16[1536,1024]{1,0:T(8,128)(2,1)}, bf16[1536,1024]{1,0:T(8,128)(2,1)}, bf16[32,64,256]{2,1,0:T(8,128)(2,1)}) custom-call(s32[48]{0:T(128)S(1)} %copy-done.1, s32[16,128]{1,0:T(8,128)S(1)} %bitcast.41, s32[12]{0:T(128)S(1)} %copy-done, bf16[1536,1024]{1,0:T(8,128)(2,1)} %queries.1, bf16[1536,1024]{1,0:T(8,128)(2,1)} %grads.1, ...), custom_call_target="tpu_custom_call" | custom-call | tf_op jit(solution)/shard_map/attend/pallas_call | solution.py:265
  53.2 3.7 %all-to-all-start.2 = ((bf16[16,2,64,256]{3,2,1,0:T(8,128)(2,1)}), bf16[16,2,64,256]{3,2,1,0:T(8,128)(2,1)S(1)}, u32[]{:S(2)}, u32[]{:S(2)}) async-start(bf16[16,2,64,256]{3,2,1,0:T(8,128)(2,1)} %bitcast.10), calls=%async_computation.2 | async-start | bytes 2097152 | tf_op jit(solution)/shard_map/all_to_all | solution.py:279
  57.0 15.0 %all-to-all-done.2 = bf16[16,2,64,256]{3,2,1,0:T(8,128)(2,1)S(1)} async-done(((bf16[16,2,64,256]{3,2,1,0:T(8,128)(2,1)}), bf16[16,2,64,256]{3,2,1,0:T(8,128)(2,1)S(1)}, u32[]{:S(2)}, u32[]{:S(2)}) %all-to-all-start.2) | async-done | bytes 1048608 | tf_op jit(solution)/shard_map/all_to_all | solution.py:279
  72.0 5.2 %weight_part.1 = (bf16[4,128,512]{2,1,0:T(8,128)(2,1)S(1)}, bf16[4,128,512]{2,1,0:T(8,128)(2,1)S(1)}, bf16[2,128,512]{2,1,0:T(8,128)(2,1)S(1)}, bf16[2,128,512]{...) custom-call(s32[16,128]{1,0:T(8,128)S(1)} %bitcast.42, ...), custom_call_target="tpu_custom_call" | custom-call | tf_op jit(solution)/shard_map/weight_part/pallas_call | solution.py:285
  77.2 1.3 %collective-permute-start.5 = (bf16[2,128,512]{2,1,0:T(8,128)(2,1)S(1)}, bf16[2,128,512]{2,1,0:T(8,128)(2,1)S(1)}, u32[]{:S(2)}, u32[]{:S(2)}) collective-permute-start(bf16[2,128,512]{2,1,0:T(8,128)(2,1)S(1)} %get-tuple-element.27), channel_id=1, source_target_pairs={{0,12},{1,13},{2,14},{3,15},{4,0},{5,1},{6,2},{7,3},{8,4},{9,5},{1... | collective-permute-start | bytes 786440 | tf_op jit(solution)/shard_map/ppermute | solution.py:211
  78.6 0.8 collective-permute-start
  79.3 1.0 collective-permute-start.14
  80.4 1.1 collective-permute-start.9
  81.6 3.9 %collective-permute-done.5 = bf16[2,128,512]{2,1,0:T(8,128)(2,1)S(1)} collective-permute-done((bf16[2,128,512]{2,1,0:T(8,128)(2,1)S(1)}, bf16[2,128,512]{2,1,0:T(8,128)(2,1)S(1)}, u32[]{:S(2)}, u32[]{:S(2)}) %collective-permute-start.5) | collective-permute-done | bytes 262176 | tf_op jit(solution)/shard_map/ppermute | solution.py:211
  85.6 1.2 %collective-permute-start.2 = (bf16[2,128,512]{2,1,0:T(8,128)(2,1)S(1)}, bf16[2,128,512]{2,1,0:T(8,128)(2,1)S(1)}, u32[]{:S(2)}, u32[]{:S(2)}) collective-permute-start(bf16[2,128,512]{2,1,0:T(8,128)(2,1)S(1)} %slice.68), channel_id=1, source_target_pairs={{0,12},{1,13},{2,14},{3,15},{4,0},{5,1},{6,2},{7,3},{8,4},{9,5},{1... | collective-permute-start | bytes 786440 | tf_op jit(solution)/shard_map/ppermute | solution.py:211
  86.8 1.8 %collective-permute-done = bf16[2,128,512]{2,1,0:T(8,128)(2,1)S(1)} collective-permute-done((bf16[2,128,512]{2,1,0:T(8,128)(2,1)S(1)}, bf16[2,128,512]{2,1,0:T(8,128)(2,1)S(1)}, u32[]{:S(2)}, u32[]{:S(2)}) %collective-permute-start) | collective-permute-done | bytes 262176 | tf_op jit(solution)/shard_map/ppermute | solution.py:211
  88.7 2.1 %collective-permute-start.1 = (bf16[2,128,512]{2,1,0:T(8,128)(2,1)S(1)}, bf16[2,128,512]{2,1,0:T(8,128)(2,1)S(1)}, u32[]{:S(2)}, u32[]{:S(2)}) collective-permute-start(bf16[2,128,512]{2,1,0:T(8,128)(2,1)S(1)} %add_convert_fusion.5), channel_id=1, source_target_pairs={{0,4},{1,5},{2,6},{3,7},{4,8},{5,9},{6,10},{7,11},{8,12},{9,13},{1... | collective-permute-start | bytes 786440 | tf_op jit(solution)/shard_map/ppermute | solution.py:211
  90.9 0.7 collective-permute-start.13
  91.7 1.1 collective-permute-done.4
  92.8 1.5 %collective-permute-start.11 = (bf16[2,128,512]{2,1,0:T(8,128)(2,1)S(1)}, bf16[2,128,512]{2,1,0:T(8,128)(2,1)S(1)}, u32[]{:S(2)}, u32[]{:S(2)}) collective-permute-start(bf16[2,128,512]{2,1,0:T(8,128)(2,1)S(1)} %slice.78), channel_id=1, source_target_pairs={{0,3},{1,0},{2,1},{3,2},{4,7},{5,4},{6,5},{7,6},{8,11},{9,8},{10,9... | collective-permute-start | bytes 786440 | tf_op jit(solution)/shard_map/ppermute | solution.py:211
  94.3 1.9 %collective-permute-start.15 = (bf16[2,128,512]{2,1,0:T(8,128)(2,1)S(1)}, bf16[2,128,512]{2,1,0:T(8,128)(2,1)S(1)}, u32[]{:S(2)}, u32[]{:S(2)}) collective-permute-start(bf16[2,128,512]{2,1,0:T(8,128)(2,1)S(1)} %add_convert_fusion.1), channel_id=1, source_target_pairs={{0,3},{1,0},{2,1},{3,2},{4,7},{5,4},{6,5},{7,6},{8,11},{9,8},{10,9... | collective-permute-start | bytes 786440 | tf_op jit(solution)/shard_map/ppermute | solution.py:211
  96.6 1.4 %collective-permute-start.3 = (bf16[128,512]{1,0:T(8,128)(2,1)S(1)}, bf16[128,512]{1,0:T(8,128)(2,1)S(1)}, u32[]{:S(2)}, u32[]{:S(2)}) collective-permute-start(bf16[128,512]{1,0:T(8,128)(2,1)S(1)} %fusion.6), channel_id=1, source_target_pairs={{0,1},{1,2},{2,3},{3,0},{4,5},{5,6},{6,7},{7,4},{8,9},{9,10},{10,1... | collective-permute-start | bytes 393224 | tf_op jit(solution)/shard_map/ppermute | solution.py:211
  98.1 3.2 %collective-permute-done.13 = bf16[2,128,512]{2,1,0:T(8,128)(2,1)S(1)} collective-permute-done((bf16[2,128,512]{2,1,0:T(8,128)(2,1)S(1)}, bf16[2,128,512]{2,1,0:T(8,128)(2,1)S(1)}, u32[]{:S(2)}, u32[]{:S(2)}) %collective-permute-start.13) | collective-permute-done | bytes 262176 | tf_op jit(solution)/shard_map/ppermute | solution.py:211
  101.3 2.1 %collective-permute-start.8 = (bf16[128,512]{1,0:T(8,128)(2,1)S(1)}, bf16[128,512]{1,0:T(8,128)(2,1)S(1)}, u32[]{:S(2)}, u32[]{:S(2)}) collective-permute-start(bf16[128,512]{1,0:T(8,128)(2,1)S(1)} %get-tuple-element.39), channel_id=1, source_target_pairs={{0,3},{1,0},{2,1},{3,2},{4,7},{5,4},{6,5},{7,6},{8,11},{9,8},{10,9... | collective-permute-start | bytes 393224 | tf_op jit(solution)/shard_map/ppermute | solution.py:211
  103.5 1.4 %collective-permute-done.15 = bf16[2,128,512]{2,1,0:T(8,128)(2,1)S(1)} collective-permute-done((bf16[2,128,512]{2,1,0:T(8,128)(2,1)S(1)}, bf16[2,128,512]{2,1,0:T(8,128)(2,1)S(1)}, u32[]{:S(2)}, u32[]{:S(2)}) %collective-permute-start.15) | collective-permute-done | bytes 262176 | tf_op jit(solution)/shard_map/ppermute | solution.py:211
  104.8 1.4 %collective-permute-done.10 = bf16[2,128,512]{2,1,0:T(8,128)(2,1)S(1)} collective-permute-done((bf16[2,128,512]{2,1,0:T(8,128)(2,1)S(1)}, bf16[2,128,512]{2,1,0:T(8,128)(2,1)S(1)}, u32[]{:S(2)}, u32[]{:S(2)}) %collective-permute-start.10) | collective-permute-done | bytes 262176 | tf_op jit(solution)/shard_map/ppermute | solution.py:211
  106.6 2.0 %collective-permute-start.16 = (bf16[128,512]{1,0:T(8,128)(2,1)S(1)}, bf16[128,512]{1,0:T(8,128)(2,1)S(1)}, u32[]{:S(2)}, u32[]{:S(2)}) collective-permute-start(bf16[128,512]{1,0:T(8,128)(2,1)S(1)} %get-tuple-element.38), channel_id=1, source_target_pairs={{0,8},{1,9},{2,10},{3,11},{4,12},{5,13},{6,14},{7,15},{8,0},{9,1},... | collective-permute-start | bytes 393224 | tf_op jit(solution)/shard_map/ppermute | solution.py:211
  108.6 0.8 collective-permute-done.3.refs_1_
  109.4 0.6 collective-permute-start.17
  110.0 4.1 %collective-permute-done.12.refs_5_ = bf16[128,512]{1,0:T(8,128)(2,1)S(1)} collective-permute-done((bf16[128,512]{1,0:T(8,128)(2,1)S(1)}, bf16[128,512]{1,0:T(8,128)(2,1)S(1)}, u32[]{:S(2)}, u32[]{:S(2)}) %collective-permute-start.12) | collective-permute-done | bytes 131104 | tf_op jit(solution)/shard_map/ppermute | solution.py:211
  114.1 1.0 collective-permute-done.17.refs_7_
  115.1 1.2 %weight_total.1 = f32[512,2,128]{2,1,0:T(2,128)} custom-call(f32[128,512]{1,0:T(8,128)S(1)} %get-tuple-element.42.refs_0_, bf16[128,512]{1,0:T(8,128)(2,1)S(1)} %collective-permute-done.3.refs_1_, bf16[128,512]{1,0:T(8,128)(2,1)S(1)} %collective-permute-done.7.refs_2_, bf16[128,512]{1,0:T(8,128)(2,1)S(1)} %collective-permute-done.8.refs_3_, ...), custom_call_target="tpu_custom_call" | custom-call | tf_op jit(solution)/shard_map/weight_total/pallas_call | solution.py:317
  (35 shorter events, 1.9 us)
Async XLA Ops:
  2.1 15.5 %all-to-all-start = ((s32[16,1,128]{2,1,0:T(1,128)}), s32[16,1,128]{2,1,0:T(1,128)S(1)}, u32[]{:S(2)}, u32[]{:S(2)}) async-start(s32[16,1,128]{2,1,0:T(1,128)} %bitcast.45), calls=%async_computation | async-start | bytes 16384 | tf_op jit(solution)/shard_map/all_to_all | solution.py:245
  10.1 31.3 %copy-start = (s32[12]{0:T(128)S(1)}, s32[12]{0:T(128)}, u32[]{:S(2)}) copy-start(s32[12]{0:T(128)} %lengths.1) | copy-start | bytes 148
  10.1 31.3 %copy-start.1 = (s32[48]{0:T(128)S(1)}, s32[48]{0:T(128)}, u32[]{:S(2)}) copy-start(s32[48]{0:T(128)} %get-tuple-element.18.meta) | copy-start | bytes 580
  53.2 18.8 %all-to-all-start.2 = ((bf16[16,2,64,256]{3,2,1,0:T(8,128)(2,1)}), bf16[16,2,64,256]{3,2,1,0:T(8,128)(2,1)S(1)}, u32[]{:S(2)}, u32[]{:S(2)}) async-start(bf16[16,2,64,256]{3,2,1,0:T(8,128)(2,1)} %bitcast.10), calls=%async_computation.2 | async-start | bytes 2097152 | tf_op jit(solution)/shard_map/all_to_all | solution.py:279
  77.2 8.3 %collective-permute-start.5 = (bf16[2,128,512]{2,1,0:T(8,128)(2,1)S(1)}, bf16[2,128,512]{2,1,0:T(8,128)(2,1)S(1)}, u32[]{:S(2)}, u32[]{:S(2)}) collective-permute-start(bf16[2,128,512]{2,1,0:T(8,128)(2,1)S(1)} %get-tuple-element.27), channel_id=1, source_target_pairs={{0,12},{1,13},{2,14},{3,15},{4,0},{5,1},{6,2},{7,3},{8,4},{9,5},{1... | collective-permute-start | bytes 786440 | tf_op jit(solution)/shard_map/ppermute | solution.py:211
  78.6 10.1 %collective-permute-start = (bf16[2,128,512]{2,1,0:T(8,128)(2,1)S(1)}, bf16[2,128,512]{2,1,0:T(8,128)(2,1)S(1)}, u32[]{:S(2)}, u32[]{:S(2)}) collective-permute-start(bf16[2,128,512]{2,1,0:T(8,128)(2,1)S(1)} %get-tuple-element.25), channel_id=1, source_target_pairs={{0,4},{1,5},{2,6},{3,7},{4,8},{5,9},{6,10},{7,11},{8,12},{9,13},{1... | collective-permute-start | bytes 786440 | tf_op jit(solution)/shard_map/ppermute | solution.py:211
  79.3 9.4 %collective-permute-start.14 = (bf16[2,128,512]{2,1,0:T(8,128)(2,1)S(1)}, bf16[2,128,512]{2,1,0:T(8,128)(2,1)S(1)}, u32[]{:S(2)}, u32[]{:S(2)}) collective-permute-start(bf16[2,128,512]{2,1,0:T(8,128)(2,1)S(1)} %get-tuple-element.32), channel_id=1, source_target_pairs={{0,3},{1,0},{2,1},{3,2},{4,7},{5,4},{6,5},{7,6},{8,11},{9,8},{10,9... | collective-permute-start | bytes 786440 | tf_op jit(solution)/shard_map/ppermute | solution.py:211
  80.4 10.5 %collective-permute-start.9 = (bf16[2,128,512]{2,1,0:T(8,128)(2,1)S(1)}, bf16[2,128,512]{2,1,0:T(8,128)(2,1)S(1)}, u32[]{:S(2)}, u32[]{:S(2)}) collective-permute-start(bf16[2,128,512]{2,1,0:T(8,128)(2,1)S(1)} %get-tuple-element.30), channel_id=1, source_target_pairs={{0,1},{1,2},{2,3},{3,0},{4,5},{5,6},{6,7},{7,4},{8,9},{9,10},{10,1... | collective-permute-start | bytes 786440 | tf_op jit(solution)/shard_map/ppermute | solution.py:211
  81.5 11.3 %collective-permute-start.4 = (bf16[2,128,512]{2,1,0:T(8,128)(2,1)S(1)}, bf16[2,128,512]{2,1,0:T(8,128)(2,1)S(1)}, u32[]{:S(2)}, u32[]{:S(2)}) collective-permute-start(bf16[2,128,512]{2,1,0:T(8,128)(2,1)S(1)} %slice.72), channel_id=1, source_target_pairs={{0,4},{1,5},{2,6},{3,7},{4,8},{5,9},{6,10},{7,11},{8,12},{9,13},{1... | collective-permute-start | bytes 786440 | tf_op jit(solution)/shard_map/ppermute | solution.py:211
  85.6 8.8 %collective-permute-start.2 = (bf16[2,128,512]{2,1,0:T(8,128)(2,1)S(1)}, bf16[2,128,512]{2,1,0:T(8,128)(2,1)S(1)}, u32[]{:S(2)}, u32[]{:S(2)}) collective-permute-start(bf16[2,128,512]{2,1,0:T(8,128)(2,1)S(1)} %slice.68), channel_id=1, source_target_pairs={{0,12},{1,13},{2,14},{3,15},{4,0},{5,1},{6,2},{7,3},{8,4},{9,5},{1... | collective-permute-start | bytes 786440 | tf_op jit(solution)/shard_map/ppermute | solution.py:211
  88.6 7.6 %collective-permute-start.6 = (bf16[2,128,512]{2,1,0:T(8,128)(2,1)S(1)}, bf16[2,128,512]{2,1,0:T(8,128)(2,1)S(1)}, u32[]{:S(2)}, u32[]{:S(2)}) collective-permute-start(bf16[2,128,512]{2,1,0:T(8,128)(2,1)S(1)} %add_convert_fusion.4), channel_id=1, source_target_pairs={{0,12},{1,13},{2,14},{3,15},{4,0},{5,1},{6,2},{7,3},{8,4},{9,5},{1... | collective-permute-start | bytes 786440 | tf_op jit(solution)/shard_map/ppermute | solution.py:211
  88.7 7.7 %collective-permute-start.1 = (bf16[2,128,512]{2,1,0:T(8,128)(2,1)S(1)}, bf16[2,128,512]{2,1,0:T(8,128)(2,1)S(1)}, u32[]{:S(2)}, u32[]{:S(2)}) collective-permute-start(bf16[2,128,512]{2,1,0:T(8,128)(2,1)S(1)} %add_convert_fusion.5), channel_id=1, source_target_pairs={{0,4},{1,5},{2,6},{3,7},{4,8},{5,9},{6,10},{7,11},{8,12},{9,13},{1... | collective-permute-start | bytes 786440 | tf_op jit(solution)/shard_map/ppermute | solution.py:211
  90.9 10.4 %collective-permute-start.13 = (bf16[2,128,512]{2,1,0:T(8,128)(2,1)S(1)}, bf16[2,128,512]{2,1,0:T(8,128)(2,1)S(1)}, u32[]{:S(2)}, u32[]{:S(2)}) collective-permute-start(bf16[2,128,512]{2,1,0:T(8,128)(2,1)S(1)} %slice.82), channel_id=1, source_target_pairs={{0,1},{1,2},{2,3},{3,0},{4,5},{5,6},{6,7},{7,4},{8,9},{9,10},{10,1... | collective-permute-start | bytes 786440 | tf_op jit(solution)/shard_map/ppermute | solution.py:211
  92.8 8.5 %collective-permute-start.11 = (bf16[2,128,512]{2,1,0:T(8,128)(2,1)S(1)}, bf16[2,128,512]{2,1,0:T(8,128)(2,1)S(1)}, u32[]{:S(2)}, u32[]{:S(2)}) collective-permute-start(bf16[2,128,512]{2,1,0:T(8,128)(2,1)S(1)} %slice.78), channel_id=1, source_target_pairs={{0,3},{1,0},{2,1},{3,2},{4,7},{5,4},{6,5},{7,6},{8,11},{9,8},{10,9... | collective-permute-start | bytes 786440 | tf_op jit(solution)/shard_map/ppermute | solution.py:211
  94.3 10.5 %collective-permute-start.15 = (bf16[2,128,512]{2,1,0:T(8,128)(2,1)S(1)}, bf16[2,128,512]{2,1,0:T(8,128)(2,1)S(1)}, u32[]{:S(2)}, u32[]{:S(2)}) collective-permute-start(bf16[2,128,512]{2,1,0:T(8,128)(2,1)S(1)} %add_convert_fusion.1), channel_id=1, source_target_pairs={{0,3},{1,0},{2,1},{3,2},{4,7},{5,4},{6,5},{7,6},{8,11},{9,8},{10,9... | collective-permute-start | bytes 786440 | tf_op jit(solution)/shard_map/ppermute | solution.py:211
  96.2 10.0 %collective-permute-start.10 = (bf16[2,128,512]{2,1,0:T(8,128)(2,1)S(1)}, bf16[2,128,512]{2,1,0:T(8,128)(2,1)S(1)}, u32[]{:S(2)}, u32[]{:S(2)}) collective-permute-start(bf16[2,128,512]{2,1,0:T(8,128)(2,1)S(1)} %add_convert_fusion.2), channel_id=1, source_target_pairs={{0,1},{1,2},{2,3},{3,0},{4,5},{5,6},{6,7},{7,4},{8,9},{9,10},{10,1... | collective-permute-start | bytes 786440 | tf_op jit(solution)/shard_map/ppermute | solution.py:211
  96.6 12.7 %collective-permute-start.3 = (bf16[128,512]{1,0:T(8,128)(2,1)S(1)}, bf16[128,512]{1,0:T(8,128)(2,1)S(1)}, u32[]{:S(2)}, u32[]{:S(2)}) collective-permute-start(bf16[128,512]{1,0:T(8,128)(2,1)S(1)} %fusion.6), channel_id=1, source_target_pairs={{0,1},{1,2},{2,3},{3,0},{4,5},{5,6},{6,7},{7,4},{8,9},{9,10},{10,1... | collective-permute-start | bytes 393224 | tf_op jit(solution)/shard_map/ppermute | solution.py:211
  101.3 8.8 %collective-permute-start.7 = (bf16[128,512]{1,0:T(8,128)(2,1)S(1)}, bf16[128,512]{1,0:T(8,128)(2,1)S(1)}, u32[]{:S(2)}, u32[]{:S(2)}) collective-permute-start(bf16[128,512]{1,0:T(8,128)(2,1)S(1)} %get-tuple-element.40), channel_id=1, source_target_pairs={{0,2},{1,3},{2,0},{3,1},{4,6},{5,7},{6,4},{7,5},{8,10},{9,11},{10,... | collective-permute-start | bytes 393224 | tf_op jit(solution)/shard_map/ppermute | solution.py:211
  101.3 8.7 %collective-permute-start.8 = (bf16[128,512]{1,0:T(8,128)(2,1)S(1)}, bf16[128,512]{1,0:T(8,128)(2,1)S(1)}, u32[]{:S(2)}, u32[]{:S(2)}) collective-permute-start(bf16[128,512]{1,0:T(8,128)(2,1)S(1)} %get-tuple-element.39), channel_id=1, source_target_pairs={{0,3},{1,0},{2,1},{3,2},{4,7},{5,4},{6,5},{7,6},{8,11},{9,8},{10,9... | collective-permute-start | bytes 393224 | tf_op jit(solution)/shard_map/ppermute | solution.py:211
  106.5 7.7 %collective-permute-start.12 = (bf16[128,512]{1,0:T(8,128)(2,1)S(1)}, bf16[128,512]{1,0:T(8,128)(2,1)S(1)}, u32[]{:S(2)}, u32[]{:S(2)}) collective-permute-start(bf16[128,512]{1,0:T(8,128)(2,1)S(1)} %fusion.7), channel_id=1, source_target_pairs={{0,4},{1,5},{2,6},{3,7},{4,8},{5,9},{6,10},{7,11},{8,12},{9,13},{1... | collective-permute-start | bytes 393224 | tf_op jit(solution)/shard_map/ppermute | solution.py:211
  106.6 7.5 %collective-permute-start.16 = (bf16[128,512]{1,0:T(8,128)(2,1)S(1)}, bf16[128,512]{1,0:T(8,128)(2,1)S(1)}, u32[]{:S(2)}, u32[]{:S(2)}) collective-permute-start(bf16[128,512]{1,0:T(8,128)(2,1)S(1)} %get-tuple-element.38), channel_id=1, source_target_pairs={{0,8},{1,9},{2,10},{3,11},{4,12},{5,13},{6,14},{7,15},{8,0},{9,1},... | collective-permute-start | bytes 393224 | tf_op jit(solution)/shard_map/ppermute | solution.py:211
  109.4 5.8 %collective-permute-start.17 = (bf16[128,512]{1,0:T(8,128)(2,1)S(1)}, bf16[128,512]{1,0:T(8,128)(2,1)S(1)}, u32[]{:S(2)}, u32[]{:S(2)}) collective-permute-start(bf16[128,512]{1,0:T(8,128)(2,1)S(1)} %get-tuple-element.37), channel_id=1, source_target_pairs={{0,12},{1,13},{2,14},{3,15},{4,0},{5,1},{6,2},{7,3},{8,4},{9,5},{1... | collective-permute-start | bytes 393224 | tf_op jit(solution)/shard_map/ppermute | solution.py:211

commit v3 on v2

--- a/solution.py
+++ b/solution.py
@@ -40,14 +40,19 @@
     table[...] = value
 
 
-def fill_kernel(table, pairs, slots):
+def fill_kernel(table, pairs, slots, sems):
+    copies = []
     for slot in range(slots.shape[0]):
         image = jnp.maximum(table[slot // CAP, slot % CAP] - 1, 0)
-        slots[slot] = pairs[image]
+        copies.append(pltpu.make_async_copy(pairs.at[image], slots.at[slot], sems.at[slot]))
+    for copy in copies:
+        copy.start()
+    for copy in copies:
+        copy.wait()
 
 
 def attend_kernel(meta, table, lengths, queries, grads, slots, attn, query_grad, slot_grad, *scratch, img_dev):
-    q_all, g_all, out_all, dq_all, sems = scratch
+    q_all, g_all, out_all, dq_all, pair_grad, sems, pair_sems = scratch
     seq_dev = lengths.shape[0]
     seq_len = queries.shape[0] // seq_dev
     groups = queries.shape[1] // HD
@@ -69,6 +74,12 @@
             )
             for kind in kinds
         ]
+
+    def pair_copy(seq, pick):
+        at = 2 * seq + pick
+        return pltpu.make_async_copy(
+            pair_grad.at[at], slot_grad.at[meta[at]], pair_sems.at[at]
+        )
 
     def begin(seq):
         for copy in copies(seq, (0, 1)):
@@ -101,10 +112,10 @@
             axis=0,
         )
         wide = lax.dot_general(key_val, both, (((1,), (1,)), ((), ())), preferred_element_type=F32)
-        return slot_ids, val_key, both, wide[: 2 * keys_img] + bias, wide[2 * keys_img :]
+        return val_key, both, wide[: 2 * keys_img] + bias, wide[2 * keys_img :]
 
     def finish(seq, state):
-        slot_ids, val_key, both, scores, grad_probs = state
+        val_key, both, scores, grad_probs = state
         token = lax.broadcasted_iota(jnp.int32, (1, groups * seq_len), 1)
         live = token % seq_len < lengths[seq]
         top = jnp.max(scores, axis=0, keepdims=True)
@@ -127,7 +138,8 @@
         key_grad = (back[2 * keys_img :, :HD] * inv_root).astype(BF16)
         for pick in range(2):
             part = slice(pick * keys_img, (pick + 1) * keys_img)
-            slot_grad[slot_ids[pick]] = jnp.concatenate([key_grad[part], val_grad[part]], axis=1)
+            pair_grad[2 * seq + pick] = jnp.concatenate([key_grad[part], val_grad[part]], axis=1)
+            pair_copy(seq, pick).start()
 
     for seq in range(seq_dev):
         for copy in copies(seq, (0, 1)):
@@ -145,24 +157,36 @@
     for seq in range(seq_dev):
         for copy in copies(seq, (2, 3)):
             copy.wait()
-
-
-def weight_kernel(table, place, slot_grad, features, *rest, img_dev):
-    outs = rest[:10]
-    image_grad, grad_low, rows, sems = rest[10:]
+        for pick in range(2):
+            pair_copy(seq, pick).wait()
+
+
+def pack_kernel(place, after, features, *rest):
+    del after
+    *outs, sems = rest
+    x_at, z_at, core = place[0], place[1], place[2]
+    width = outs[0].shape[1] // SIDE
+    copies = []
+    for step, out in enumerate(outs):
+        for k in range(SIDE):
+            low = (lax.rem(x_at + step + 1, SIDE) * SIDE + k) * (2 * width)
+            high = (k * SIDE + lax.rem(z_at + step + 1, SIDE)) * (2 * width) + width
+            start = pl.multiple_of(jnp.where(core == 0, low, high), width)
+            copies.append(
+                pltpu.make_async_copy(
+                    features.at[:, pl.ds(start, width)],
+                    out.at[:, pl.ds(k * width, width)],
+                    sems.at[step, k],
+                )
+            )
+    for copy in copies:
+        copy.start()
+    for copy in copies:
+        copy.wait()
+
+
+def image_kernel(table, slot_grad, grad_low, image_grad):
     slot_total, keys_img, cols = slot_grad.shape
-    block = outs[0].shape[2]
-    x_at, z_at = place[0], place[1]
-    order = (2, 1, 3, 0)
-
-    def fetch(dx):
-        start = pl.multiple_of(lax.rem(x_at + dx, SIDE) * (SIDE * block), SIDE * block)
-        return pltpu.make_async_copy(
-            features.at[:, pl.ds(start, SIDE * block)], rows.at[dx], sems.at[dx]
-        )
-
-    for dx in order:
-        fetch(dx).start()
     image_grad[...] = jnp.zeros_like(image_grad)
     for slot in range(slot_total):
         image = table[slot // CAP, slot % CAP]
@@ -171,35 +195,68 @@
         def _():
             image_grad[image - 1] += slot_grad[slot].astype(F32)
 
-    grad_low[...] = image_grad[...].reshape(img_dev * keys_img, cols).T.astype(BF16)
-    for dx in order:
-        fetch(dx).wait()
-        for dz in range(SIDE):
-            start = pl.multiple_of(lax.rem(z_at + dz, SIDE) * block, block)
+    total = image_grad[...].reshape(image_grad.shape[0] * keys_img, cols)
+    grad_low[...] = total.T.astype(BF16)
+
+
+def weight_kernel(place, *refs, half):
+    grads, features, sources = refs[:SIDE], refs[SIDE], refs[SIDE + 1 : 3 * SIDE - 1]
+    outs = refs[3 * SIDE - 1 : 4 * SIDE - 1]
+    rows, total, sems = refs[4 * SIDE - 1 :]
+    x_at, z_at, core = place[0], place[1], place[2]
+    width = rows.shape[2] // SIDE
+
+    def own_copy(k):
+        if half == 0:
+            start = (x_at * SIDE + k) * (2 * width)
+        else:
+            start = (k * SIDE + z_at) * (2 * width) + width
+        return pltpu.make_async_copy(
+            features.at[:, pl.ds(pl.multiple_of(start, width), width)],
+            rows.at[0, :, pl.ds(k * width, width)],
+            sems.at[k],
+        )
+
+    def far_copy(step, source):
+        return pltpu.make_async_copy(source, rows.at[step + 1], sems.at[SIDE + step])
+
+    for k in range(SIDE):
+        own_copy(k).start()
+    for at, part in ((half, sources[: SIDE - 1]), (1 - half, sources[SIDE - 1 :])):
+
+        @pl.when(core == at)
+        def _():
+            for step in range(SIDE - 1):
+                far_copy(step, part[step]).start()
+
+    for k in range(SIDE):
+        own_copy(k).wait()
+    for index in range(SIDE):
+        if index:
+            far_copy(index - 1, sources[index - 1]).wait()
+        for k in range(SIDE):
             part = jnp.dot(
-                grad_low[...], rows[dx, :, pl.ds(start, block)], preferred_element_type=F32
-            ).astype(BF16)
-            for half, (first, second) in enumerate(((dx, dz), (dz, dx))):
-                piece = part[half * HD : (half + 1) * HD]
-                five = outs[5 * half : 5 * half + 5]
-                if first == 0:
-                    five[4][second] = piece
-                elif first == 1:
-                    five[0][second] = piece
-                elif first == 3:
-                    five[1][second] = piece
-                elif second < 2:
-                    five[2][second] = piece
-                else:
-                    five[3][second - 2] = piece
+                grads[index][...],
+                rows[index, :, k * width : (k + 1) * width],
+                preferred_element_type=F32,
+            )
+            if index:
+                total[k] += part
+            else:
+                total[k] = part
+    for step in range(SIDE):
+        piece = total[lax.rem(place[1 - half] + step, SIDE)]
+        outs[step][...] = piece.astype(outs[step].dtype)
 
 
 def final_kernel(*refs):
     out = refs[-1]
+    width = refs[0].shape[1]
     for half in range(2):
         own, one, two, three = refs[4 * half : 4 * half + 4]
         total = own[...] + one[...].astype(F32) + two[...].astype(F32) + three[...].astype(F32)
-        out[:, half, :] = total.T
+        for kind in range(2):
+            out[half * width : (half + 1) * width, kind, :] = total[kind * HD : (kind + 1) * HD].T
 
 
 def shift(values, axis, step):
@@ -211,8 +268,19 @@
     return lax.ppermute(values, "txt", pairs)
 
 
-def add(*terms):
-    return functools.reduce(lambda a, b: a + b, [term.astype(F32) for term in terms])
+def feature_shift(values, step):
+    pairs = []
+    for img in range(lax.axis_size("img")):
+        for x in range(SIDE):
+            for z in range(SIDE):
+                to = ((x + step) % SIDE, z) if img % 2 == 0 else (x, (z + step) % SIDE)
+                side = SIDE * SIDE
+                pairs.append((img * side + x * SIDE + z, img * side + to[0] * SIDE + to[1]))
+    return lax.ppermute(values, ("img", "txt"), pairs)
+
+
+def swap_cores(values):
+    return lax.ppermute(values, "img", [(i, i ^ 1) for i in range(lax.axis_size("img"))])
 
 
 def shards(features, tile_count, kv_weight, queries, out_grad, image_ids, text_len):
@@ -226,6 +294,7 @@
     slot_total = txt_count * CAP
     whole = pl.BlockSpec(memory_space=pltpu.VMEM)
     scalars = pl.BlockSpec(memory_space=pltpu.SMEM)
+    in_hbm = pl.BlockSpec(memory_space=pltpu.HBM)
 
     def params(mib):
         return pltpu.CompilerParams(vmem_limit_bytes=mib * MIB)
@@ -243,7 +312,7 @@
         name="request_table",
     )(image_ids.T, tile_count)
     table = lax.all_to_all(wanted, "txt", 0, 0, tiled=True)
-    place = jnp.stack([shard_index // SIDE, shard_index % SIDE])
+    place = jnp.stack([shard_index // SIDE, shard_index % SIDE, lax.axis_index("img") % 2])
 
     flat_features = features.reshape(img_dev * keys_img, feat_width)
     own_pairs = jnp.dot(
@@ -253,7 +322,8 @@
         fill_kernel,
         out_shape=jax.ShapeDtypeStruct((slot_total, keys_img, cols), BF16),
         in_specs=[scalars, whole],
-        out_specs=whole,
+        out_specs=in_hbm,
+        scratch_shapes=[pltpu.SemaphoreType.DMA((slot_total,))],
         compiler_params=params(8),
         name="fill_slots",
     )(table, own_pairs.reshape(img_dev, keys_img, cols))
@@ -261,7 +331,23 @@
         sent_pairs.reshape(txt_count, CAP, keys_img, cols), "txt", 0, 0, tiled=True
     ).reshape(slot_total, keys_img, cols)
 
-    in_hbm = pl.BlockSpec(memory_space=pltpu.HBM)
+    block = feat_width // txt_count
+    width = block // 2
+    held_features = pltpu.with_memory_space_constraint(flat_features, pltpu.HBM)
+    messages = pl.pallas_call(
+        pack_kernel,
+        out_shape=[jax.ShapeDtypeStruct((img_dev * keys_img, SIDE * width), BF16)] * (SIDE - 1),
+        in_specs=[scalars, in_hbm, in_hbm],
+        out_specs=[whole] * (SIDE - 1),
+        scratch_shapes=[pltpu.SemaphoreType.DMA((SIDE - 1, SIDE))],
+        compiler_params=params(4),
+        cost_estimate=pl.CostEstimate(
+            flops=0, bytes_accessed=2 * flat_features.size, transcendentals=0
+        ),
+        name="pack_features",
+    )(place, sent_pairs, held_features)
+    got_features = [feature_shift(part, step + 1) for step, part in enumerate(messages)]
+    swapped_features = [swap_cores(part) for part in got_features]
     attended, grad_query, slot_grad = pl.pallas_call(
         functools.partial(attend_kernel, img_dev=img_dev),
         out_shape=[
@@ -270,9 +356,13 @@
             jax.ShapeDtypeStruct((slot_total, keys_img, cols), BF16),
         ],
         in_specs=[scalars, scalars, scalars, in_hbm, in_hbm, whole],
-        out_specs=[in_hbm, in_hbm, whole],
+        out_specs=[in_hbm] * 3,
         scratch_shapes=[pltpu.VMEM(queries.shape, BF16)] * 4
-        + [pltpu.SemaphoreType.DMA((4, seq_dev))],
+        + [
+            pltpu.VMEM((request_total, keys_img, cols), BF16),
+            pltpu.SemaphoreType.DMA((4, seq_dev)),
+            pltpu.SemaphoreType.DMA((request_total,)),
+        ],
         compiler_params=params(24),
         name="attend",
     )(meta, table, text_len, *[pltpu.with_memory_space_constraint(x, pltpu.HBM) for x in (queries, out_grad)], got_pairs)
@@ -280,40 +370,44 @@
         slot_grad.reshape(txt_count, CAP, keys_img, cols), "txt", 0, 0, tiled=True
     ).reshape(slot_total, keys_img, cols)
 
-    block = feat_width // txt_count
-    message = [(SIDE, HD, block), (SIDE, HD, block), (2, HD, block), (2, HD, block), (SIDE, HD, block)]
-    pieces = pl.pallas_call(
-        functools.partial(weight_kernel, img_dev=img_dev),
-        out_shape=[jax.ShapeDtypeStruct(shape, BF16) for shape in message * 2],
-        in_specs=[scalars, scalars, whole, in_hbm],
-        out_specs=[whole] * 10,
-        scratch_shapes=[
-            pltpu.VMEM((img_dev, keys_img, cols), F32),
-            pltpu.VMEM((cols, img_dev * keys_img), BF16),
-            pltpu.VMEM((SIDE, img_dev * keys_img, SIDE * block), BF16),
-            pltpu.SemaphoreType.DMA((SIDE,)),
-        ],
-        compiler_params=params(20),
-        name="weight_part",
-    )(table, place, back_grad, pltpu.with_memory_space_constraint(flat_features, pltpu.HBM))
-
+    grad_low = pl.pallas_call(
+        image_kernel,
+        out_shape=jax.ShapeDtypeStruct((cols, img_dev * keys_img), BF16),
+        in_specs=[scalars, whole],
+        out_specs=whole,
+        scratch_shapes=[pltpu.VMEM((img_dev, keys_img, cols), F32)],
+        compiler_params=params(8),
+        name="image_grads",
+    )(table, back_grad)
+    along = {
+        (half, step): shift(grad_low, "xz"[half], step) for step in (2, 1, 3) for half in range(2)
+    }
     final = []
-    for half, (first, second) in enumerate((("x", "z"), ("z", "x"))):
-        up, down, far_low, far_high, own = pieces[5 * half : 5 * half + 5]
-        far_up = shift(far_low, first, 1)
-        far_down = shift(far_high, first, -1)
-        near_up = shift(up[2:], first, 1)
-        near_down = shift(down[:2], first, -1)
-        relay_up = shift(add(up[:2], far_up).astype(BF16), first, 1)
-        relay_down = shift(add(down[2:], far_down).astype(BF16), first, -1)
-        low = add(own[:2], relay_up, near_down)
-        high = add(own[2:], near_up, relay_down)
-        final += [
-            low[0],
-            shift(low[1].astype(BF16), second, 1),
-            shift(high[0].astype(BF16), second, 2),
-            shift(high[1].astype(BF16), second, -1),
-        ]
+    for half in range(2):
+        own, *others = pl.pallas_call(
+            functools.partial(weight_kernel, half=half),
+            out_shape=[
+                jax.ShapeDtypeStruct((cols, width), F32 if step == 0 else BF16)
+                for step in range(SIDE)
+            ],
+            in_specs=[scalars] + [whole] * SIDE + [in_hbm] * (2 * SIDE - 1),
+            out_specs=[whole] * SIDE,
+            scratch_shapes=[
+                pltpu.VMEM((SIDE, img_dev * keys_img, SIDE * width), BF16),
+                pltpu.VMEM((SIDE, cols, width), F32),
+                pltpu.SemaphoreType.DMA((2 * SIDE,)),
+            ],
+            compiler_params=params(12),
+            name="weight_part",
+        )(
+            place,
+            grad_low,
+            *[along[half, step] for step in range(1, SIDE)],
+            held_features,
+            *got_features,
+            *swapped_features,
+        )
+        final += [own] + [shift(part, "zx"[half], step + 1) for step, part in enumerate(others)]
     weight_grad = pl.pallas_call(
         final_kernel,
         out_shape=jax.ShapeDtypeStruct((block, 2, head_cols), F32),

time: 117 us -> 113 us (0.966)
  blocking collectives: 23 us -> 0 us
  starting transfers between devices: 29.8 us -> 39.8 us
  Pallas kernels: 20.4 us -> 30.1 us
    all_to_all x1 -> x0, blocking collectives: 23 us -> none  [shards(): lax.all_to_all(sent_pairs.reshape(txt_count, CAP, keys_img, cols), 'txt',...]
    pallas_call x1 -> x4, Pallas kernels: 5.18 us -> 12.7 us  [the longest x2 6.78 us: shards(): pl.pallas_call(functools.partial(weight_kernel, half=half), out_shape=[ja...]
    ppermute x18 -> x12, waiting for transfers between devices: 18.8 us -> 11.4 us  [shift(): return lax.ppermute(values, 'txt', pairs)]
    all_to_all x0 -> x1, starting transfers between devices: none -> 6.75 us  [shards(): lax.all_to_all(sent_pairs.reshape(txt_count, CAP, keys_img, cols), 'txt',...]
    ppermute x0 -> x6, starting transfers between devices: none -> 6.68 us  [the longest x3 6.08 us: feature_shift(): return lax.ppermute(values, ('img', 'txt'), pairs)]
    all_to_all x0 -> x1, waiting for transfers between devices: none -> 6.6 us  [shards(): lax.all_to_all(sent_pairs.reshape(txt_count, CAP, keys_img, cols), 'txt',...]
    ppermute x18 -> x12, starting transfers between devices: 18.1 us -> 14 us  [shift(): return lax.ppermute(values, 'txt', pairs)]
    ppermute x0 -> x6, waiting for transfers between devices: none -> 2.11 us  [the longest x3 2.1 us: feature_shift(): return lax.ppermute(values, ('img', 'txt'), pairs)]
  transfers between devices with their start and end apart: 20 -> 21, of which waited for: 11 -> 9; matrix products, arithmetic and copies ran while one was open for 7% -> 6% of each run, Pallas kernels for 0% -> 23%
where the time goes in v3:
time: 113 us; the launch traced here: 112 us
  starting transfers between devices  39.8 us (35%)
  waiting for transfers between devices  33.7 us (30%)
  Pallas kernels  30.1 us (27%)
  matrix products  6.91 us (6%)
    ppermute x12, starting transfers between devices, shift(): return lax.ppermute(values, 'txt', pairs)  14 us
    all_to_all x1, waiting for transfers between devices, shards(): lax.all_to_all(slot_grad.reshape(txt_count, CAP, keys_img, cols), 'txt',...  13 us
    pallas_call x1, Pallas kernels, shards(): pl.pallas_call(functools.partial(attend_kernel, img_dev=img_dev), out_sha...  12.8 us
    ppermute x12, waiting for transfers between devices, shift(): return lax.ppermute(values, 'txt', pairs)  11.4 us
    all_to_all x1, starting transfers between devices, shards(): table = lax.all_to_all(wanted, 'txt', 0, 0, tiled=True)  7.97 us
    dot_general x1, matrix products, shards(): jnp.dot(flat_features, kv_weight.reshape(feat_width, cols), preferred_ele...  6.91 us
    pallas_call x2, Pallas kernels, shards(): pl.pallas_call(functools.partial(weight_kernel, half=half), out_shape=[ja...  6.78 us
    all_to_all x1, starting transfers between devices, shards(): lax.all_to_all(sent_pairs.reshape(txt_count, CAP, keys_img, cols), 'txt',...  6.75 us
  transfers between devices with their start and end apart: 21, of which 9 were waited for; matrix products, arithmetic and copies ran while one was open for 6% of the time, Pallas kernels for 23%

profile of v3, /device:TPU:0, one launch (start us, length us, event | category | flops | bytes accessed | tf_op | source)
XLA Modules:
  0.0 112.3 jit_solution(1073998993997263143)
XLA Ops:
  0.6 1.5 %request_table.1 = (s32[16,128]{1,0:T(8,128)}, s32[48]{0:T(128)}) custom-call(s32[2,12]{1,0:T(2,128)} %bitcast.32, s32[8]{0:T(128)} %counts.1), custom_call_target="tpu_custom_call" | custom-call | tf_op jit(solution)/shard_map/request_table/pallas_call | solution.py:303
  2.1 8.0 %all-to-all-start = ((s32[16,1,128]{2,1,0:T(1,128)}), s32[16,1,128]{2,1,0:T(1,128)S(1)}, u32[]{:S(2)}, u32[]{:S(2)}) async-start(s32[16,1,128]{2,1,0:T(1,128)} %bitcast.30), calls=%async_computation | async-start | bytes 16384 | tf_op jit(solution)/shard_map/all_to_all | solution.py:314
  10.1 6.9 %fusion.3 = bf16[512,256]{1,0:T(8,128)(2,1)S(1)} fusion(bf16[512,8192]{1,0:T(8,128)(2,1)} %bitcast.26, bf16[1024,8,2,128]{3,2,1,0:T(2,128)(2,1)} %bitcast.31), kind=kOutput, calls=%fused_computation.3 | convolution fusion | flops 2147614720 | bytes 12845056 | tf_op jit(solution)/shard_map/dot_general | solution.py:318
  17.6 1.9 %fill_slots.1.after = bf16[32,64,256]{2,1,0:T(8,128)(2,1)} custom-call(s32[16,128]{1,0:T(8,128)S(1)} %bitcast.23, bf16[8,64,256]{2,1,0:T(8,128)(2,1)S(1)} %bitcast.22), custom_call_target="tpu_custom_call" | custom-call | tf_op jit(solution)/shard_map/fill_slots/pallas_call | solution.py:321
  19.5 6.7 %all-to-all-start.1 = ((bf16[16,2,64,256]{3,2,1,0:T(8,128)(2,1)}), bf16[16,2,64,256]{3,2,1,0:T(8,128)(2,1)}, u32[]{:S(2)}, u32[]{:S(2)}) async-start(bf16[16,2,64,256]{3,2,1,0:T(8,128)(2,1)} %bitcast.6), calls=%async_computation.1 | async-start | bytes 2097152 | tf_op jit(solution)/shard_map/all_to_all | solution.py:330
  26.3 4.2 %pack_features.1 = (bf16[512,1024]{1,0:T(8,128)(2,1)}, bf16[512,1024]{1,0:T(8,128)(2,1)}, bf16[512,1024]{1,0:T(8,128)(2,1)}) custom-call(s32[3]{0:T(128)S(1)} %pad_add_fusion.place, bf16[32,64,256]{2,1,0:T(8,128)(2,1)} %fill_slots.1.after, bf16[512,8192]{1,0:T(8,128)(2,1)} %bitcast.27), custom_call_target="tpu_custom_call" | custom-call | bytes 8388608 | tf_op jit(solution)/shard_map/pack_features/pallas_call | solution.py:337
  30.6 1.9 %collective-permute-start.3 = (bf16[512,1024]{1,0:T(8,128)(2,1)}, bf16[512,1024]{1,0:T(8,128)(2,1)S(1)}, u32[]{:S(2)}, u32[]{:S(2)}) collective-permute-start(bf16[512,1024]{1,0:T(8,128)(2,1)} %get-tuple-element.24), channel_id=1, source_target_pairs={{0,4},{1,5},{2,6},{3,7},{4,8},{5,9},{6,10},{7,11},{8,12},{9,13},{1... | collective-permute-start | bytes 3145736 | tf_op jit(solution)/shard_map/ppermute | solution.py:279
  32.5 2.7 %collective-permute-start.4 = (bf16[512,1024]{1,0:T(8,128)(2,1)}, bf16[512,1024]{1,0:T(8,128)(2,1)S(1)}, u32[]{:S(2)}, u32[]{:S(2)}) collective-permute-start(bf16[512,1024]{1,0:T(8,128)(2,1)} %get-tuple-element.25), channel_id=1, source_target_pairs={{0,8},{1,9},{2,10},{3,11},{4,12},{5,13},{6,14},{7,15},{8,0},{9,1},... | collective-permute-start | bytes 3145736 | tf_op jit(solution)/shard_map/ppermute | solution.py:279
  35.2 1.5 %collective-permute-start.5 = (bf16[512,1024]{1,0:T(8,128)(2,1)}, bf16[512,1024]{1,0:T(8,128)(2,1)S(1)}, u32[]{:S(2)}, u32[]{:S(2)}) collective-permute-start(bf16[512,1024]{1,0:T(8,128)(2,1)} %get-tuple-element.26), channel_id=1, source_target_pairs={{0,12},{1,13},{2,14},{3,15},{4,0},{5,1},{6,2},{7,3},{8,4},{9,5},{1... | collective-permute-start | bytes 3145736 | tf_op jit(solution)/shard_map/ppermute | solution.py:279
  36.6 6.6 %all-to-all-done.1 = bf16[16,2,64,256]{3,2,1,0:T(8,128)(2,1)} async-done(((bf16[16,2,64,256]{3,2,1,0:T(8,128)(2,1)}), bf16[16,2,64,256]{3,2,1,0:T(8,128)(2,1)}, u32[]{:S(2)}, u32[]{:S(2)}) %all-to-all-start.1) | async-done | bytes 1048608 | tf_op jit(solution)/shard_map/all_to_all | solution.py:330
  43.2 12.8 %attend.1 = (bf16[1536,1024]{1,0:T(8,128)(2,1)}, bf16[1536,1024]{1,0:T(8,128)(2,1)}, bf16[32,64,256]{2,1,0:T(8,128)(2,1)S(1)}) custom-call(s32[48]{0:T(128)S(1)} %copy-done.2, s32[16,128]{1,0:T(8,128)S(1)} %bitcast.24, s32[12]{0:T(128)S(1)} %copy-done.1, bf16[1536,1024]{1,0:T(8,128)(2,1)} %queries.1, bf16[1536,1024]{1,0:T(8,128)(2,1)} %grads.1, ...), custom_call_target="tpu_custom_call" | custom-call | tf_op jit(solution)/shard_map/attend/pallas_call | solution.py:351
  56.0 1.0 copy-done
  57.0 4.3 %all-to-all-start.2 = ((bf16[16,2,64,256]{3,2,1,0:T(8,128)(2,1)}), bf16[16,2,64,256]{3,2,1,0:T(8,128)(2,1)}, u32[]{:S(2)}, u32[]{:S(2)}) async-start(bf16[16,2,64,256]{3,2,1,0:T(8,128)(2,1)} %bitcast.21), calls=%async_computation.2 | async-start | bytes 2097152 | tf_op jit(solution)/shard_map/all_to_all | solution.py:369
  61.5 2.1 %collective-permute-done.4.refs_6_ = bf16[512,1024]{1,0:T(8,128)(2,1)S(1)} collective-permute-done((bf16[512,1024]{1,0:T(8,128)(2,1)}, bf16[512,1024]{1,0:T(8,128)(2,1)S(1)}, u32[]{:S(2)}, u32[]{:S(2)}) %collective-permute-start.4) | collective-permute-done | bytes 1048608 | tf_op jit(solution)/shard_map/ppermute | solution.py:279
  64.1 13.0 %all-to-all-done.2 = bf16[16,2,64,256]{3,2,1,0:T(8,128)(2,1)} async-done(((bf16[16,2,64,256]{3,2,1,0:T(8,128)(2,1)}), bf16[16,2,64,256]{3,2,1,0:T(8,128)(2,1)}, u32[]{:S(2)}, u32[]{:S(2)}) %all-to-all-start.2) | async-done | bytes 1048608 | tf_op jit(solution)/shard_map/all_to_all | solution.py:369
  77.1 1.7 %image_grads.1.refs_0_ = bf16[256,512]{1,0:T(8,128)(2,1)S(1)} custom-call(s32[16,128]{1,0:T(8,128)S(1)} %bitcast.25, bf16[32,64,256]{2,1,0:T(8,128)(2,1)} %bitcast.12.slot_grad), custom_call_target="tpu_custom_call" | custom-call | tf_op jit(solution)/shard_map/image_grads/pallas_call | solution.py:373
  78.8 0.6 collective-permute-start.14
  79.4 2.1 %collective-permute-start.13 = (bf16[256,512]{1,0:T(8,128)(2,1)S(1)}, bf16[256,512]{1,0:T(8,128)(2,1)S(1)}, u32[]{:S(2)}, u32[]{:S(2)}) collective-permute-start(bf16[256,512]{1,0:T(8,128)(2,1)S(1)} %image_grads.1.refs_0_), channel_id=1, source_target_pairs={{0,2},{1,3},{2,0},{3,1},{4,6},{5,7},{6,4},{7,5},{8,10},{9,11},{10,... | collective-permute-start | bytes 786440 | tf_op jit(solution)/shard_map/ppermute | solution.py:268
  81.5 1.3 %collective-permute-start.2 = (bf16[256,512]{1,0:T(8,128)(2,1)S(1)}, bf16[256,512]{1,0:T(8,128)(2,1)S(1)}, u32[]{:S(2)}, u32[]{:S(2)}) collective-permute-start(bf16[256,512]{1,0:T(8,128)(2,1)S(1)} %image_grads.1.refs_0_), channel_id=1, source_target_pairs={{0,12},{1,13},{2,14},{3,15},{4,0},{5,1},{6,2},{7,3},{8,4},{9,5},{1... | collective-permute-start | bytes 786440 | tf_op jit(solution)/shard_map/ppermute | solution.py:268
  82.8 1.1 collective-permute-start.1
  83.9 3.3 %collective-permute-done.14.refs_3_ = bf16[256,512]{1,0:T(8,128)(2,1)S(1)} collective-permute-done((bf16[256,512]{1,0:T(8,128)(2,1)S(1)}, bf16[256,512]{1,0:T(8,128)(2,1)S(1)}, u32[]{:S(2)}, u32[]{:S(2)}) %collective-permute-start.14) | collective-permute-done | bytes 262176 | tf_op jit(solution)/shard_map/ppermute | solution.py:268
  87.2 1.7 %collective-permute-done.13.refs_2_ = bf16[256,512]{1,0:T(8,128)(2,1)S(1)} collective-permute-done((bf16[256,512]{1,0:T(8,128)(2,1)S(1)}, bf16[256,512]{1,0:T(8,128)(2,1)S(1)}, u32[]{:S(2)}, u32[]{:S(2)}) %collective-permute-start.13) | collective-permute-done | bytes 262176 | tf_op jit(solution)/shard_map/ppermute | solution.py:268
  88.9 2.7 %collective-permute-done.12.refs_1_ = bf16[256,512]{1,0:T(8,128)(2,1)S(1)} collective-permute-done((bf16[256,512]{1,0:T(8,128)(2,1)S(1)}, bf16[256,512]{1,0:T(8,128)(2,1)S(1)}, u32[]{:S(2)}, u32[]{:S(2)}) %collective-permute-start.12) | collective-permute-done | bytes 262176 | tf_op jit(solution)/shard_map/ppermute | solution.py:268
  91.6 3.4 %weight_part.3 = (f32[256,256]{1,0:T(8,128)S(1)}, bf16[256,256]{1,0:T(8,128)(2,1)S(1)}, bf16[256,256]{1,0:T(8,128)(2,1)S(1)}, bf16[256,256]{1,0:T(8,128)(2,1)S(1)}) custom-call(s32[3]{0:T(128)S(1)} %pad_add_fusion.place, bf16[256,512]{1,0:T(8,128)(2,1)S(1)} %image_grads.1.refs_0_, bf16[256,512]{1,0:T(8,128)(2,1)S(1)} %collective-permute-done.12.refs_1_, ...), custom_call_target="tpu_custom_call" | custom-call | tf_op jit(solution)/shard_map/weight_part/pallas_call | solution.py:387
  95.1 2.6 %collective-permute-start.16 = (bf16[256,256]{1,0:T(8,128)(2,1)S(1)}, bf16[256,256]{1,0:T(8,128)(2,1)S(1)}, u32[]{:S(2)}, u32[]{:S(2)}) collective-permute-start(bf16[256,256]{1,0:T(8,128)(2,1)S(1)} %get-tuple-element.33), channel_id=1, source_target_pairs={{0,8},{1,9},{2,10},{3,11},{4,12},{5,13},{6,14},{7,15},{8,0},{9,1},... | collective-permute-start | bytes 393224 | tf_op jit(solution)/shard_map/ppermute | solution.py:268
  97.8 1.3 %collective-permute-start.17 = (bf16[256,256]{1,0:T(8,128)(2,1)S(1)}, bf16[256,256]{1,0:T(8,128)(2,1)S(1)}, u32[]{:S(2)}, u32[]{:S(2)}) collective-permute-start(bf16[256,256]{1,0:T(8,128)(2,1)S(1)} %get-tuple-element.34), channel_id=1, source_target_pairs={{0,12},{1,13},{2,14},{3,15},{4,0},{5,1},{6,2},{7,3},{8,4},{9,5},{1... | collective-permute-start | bytes 393224 | tf_op jit(solution)/shard_map/ppermute | solution.py:268
  99.1 3.4 %weight_part.2 = (f32[256,256]{1,0:T(8,128)S(1)}, bf16[256,256]{1,0:T(8,128)(2,1)S(1)}, bf16[256,256]{1,0:T(8,128)(2,1)S(1)}, bf16[256,256]{1,0:T(8,128)(2,1)S(1)}) custom-call(s32[3]{0:T(128)S(1)} %pad_add_fusion.place, bf16[256,512]{1,0:T(8,128)(2,1)S(1)} %image_grads.1.refs_0_, bf16[256,512]{1,0:T(8,128)(2,1)S(1)} %collective-permute-done.refs_1_, ...), custom_call_target="tpu_custom_call" | custom-call | tf_op jit(solution)/shard_map/weight_part/pallas_call | solution.py:387
  102.5 2.1 %collective-permute-start.9 = (bf16[256,256]{1,0:T(8,128)(2,1)S(1)}, bf16[256,256]{1,0:T(8,128)(2,1)S(1)}, u32[]{:S(2)}, u32[]{:S(2)}) collective-permute-start(bf16[256,256]{1,0:T(8,128)(2,1)S(1)} %get-tuple-element.28), channel_id=1, source_target_pairs={{0,1},{1,2},{2,3},{3,0},{4,5},{5,6},{6,7},{7,4},{8,9},{9,10},{10,1... | collective-permute-start | bytes 393224 | tf_op jit(solution)/shard_map/ppermute | solution.py:268
  105.0 2.4 %collective-permute-start.11 = (bf16[256,256]{1,0:T(8,128)(2,1)S(1)}, bf16[256,256]{1,0:T(8,128)(2,1)S(1)}, u32[]{:S(2)}, u32[]{:S(2)}) collective-permute-start(bf16[256,256]{1,0:T(8,128)(2,1)S(1)} %get-tuple-element.30), channel_id=1, source_target_pairs={{0,3},{1,0},{2,1},{3,2},{4,7},{5,4},{6,5},{7,6},{8,11},{9,8},{10,9... | collective-permute-start | bytes 393224 | tf_op jit(solution)/shard_map/ppermute | solution.py:268
  107.4 1.3 %collective-permute-done.9.refs_1_ = bf16[256,256]{1,0:T(8,128)(2,1)S(1)} collective-permute-done((bf16[256,256]{1,0:T(8,128)(2,1)S(1)}, bf16[256,256]{1,0:T(8,128)(2,1)S(1)}, u32[]{:S(2)}, u32[]{:S(2)}) %collective-permute-start.9) | collective-permute-done | bytes 131104 | tf_op jit(solution)/shard_map/ppermute | solution.py:268
  108.7 2.4 %collective-permute-done.10.refs_2_ = bf16[256,256]{1,0:T(8,128)(2,1)S(1)} collective-permute-done((bf16[256,256]{1,0:T(8,128)(2,1)S(1)}, bf16[256,256]{1,0:T(8,128)(2,1)S(1)}, u32[]{:S(2)}, u32[]{:S(2)}) %collective-permute-start.10) | collective-permute-done | bytes 131104 | tf_op jit(solution)/shard_map/ppermute | solution.py:268
  111.1 1.2 %weight_total.1 = f32[512,2,128]{2,1,0:T(2,128)} custom-call(f32[256,256]{1,0:T(8,128)S(1)} %get-tuple-element.27.refs_0_, bf16[256,256]{1,0:T(8,128)(2,1)S(1)} %collective-permute-done.9.refs_1_, bf16[256,256]{1,0:T(8,128)(2,1)S(1)} %collective-permute-done.10.refs_2_, bf16[256,256]{1,0:T(8,128)(2,1)S(1)} %collective-permute-done.11.refs_3_, ...), custom_call_target="tpu_custom_call" | custom-call | tf_op jit(solution)/shard_map/weight_total/pallas_call | solution.py:411
  (26 shorter events, 1.7 us)
Async XLA Ops:
  2.1 15.5 %all-to-all-start = ((s32[16,1,128]{2,1,0:T(1,128)}), s32[16,1,128]{2,1,0:T(1,128)S(1)}, u32[]{:S(2)}, u32[]{:S(2)}) async-start(s32[16,1,128]{2,1,0:T(1,128)} %bitcast.30), calls=%async_computation | async-start | bytes 16384 | tf_op jit(solution)/shard_map/all_to_all | solution.py:314
  19.5 23.7 %all-to-all-start.1 = ((bf16[16,2,64,256]{3,2,1,0:T(8,128)(2,1)}), bf16[16,2,64,256]{3,2,1,0:T(8,128)(2,1)}, u32[]{:S(2)}, u32[]{:S(2)}) async-start(bf16[16,2,64,256]{3,2,1,0:T(8,128)(2,1)} %bitcast.6), calls=%async_computation.1 | async-start | bytes 2097152 | tf_op jit(solution)/shard_map/all_to_all | solution.py:330
  26.3 16.9 %copy-start.1 = (s32[12]{0:T(128)S(1)}, s32[12]{0:T(128)}, u32[]{:S(2)}) copy-start(s32[12]{0:T(128)} %lengths.1) | copy-start | bytes 148
  26.3 16.9 %copy-start.2 = (s32[48]{0:T(128)S(1)}, s32[48]{0:T(128)}, u32[]{:S(2)}) copy-start(s32[48]{0:T(128)} %get-tuple-element.19.meta) | copy-start | bytes 580
  30.6 30.8 %collective-permute-start.3 = (bf16[512,1024]{1,0:T(8,128)(2,1)}, bf16[512,1024]{1,0:T(8,128)(2,1)S(1)}, u32[]{:S(2)}, u32[]{:S(2)}) collective-permute-start(bf16[512,1024]{1,0:T(8,128)(2,1)} %get-tuple-element.24), channel_id=1, source_target_pairs={{0,4},{1,5},{2,6},{3,7},{4,8},{5,9},{6,10},{7,11},{8,12},{9,13},{1... | collective-permute-start | bytes 3145736 | tf_op jit(solution)/shard_map/ppermute | solution.py:279
  32.5 31.0 %collective-permute-start.4 = (bf16[512,1024]{1,0:T(8,128)(2,1)}, bf16[512,1024]{1,0:T(8,128)(2,1)S(1)}, u32[]{:S(2)}, u32[]{:S(2)}) collective-permute-start(bf16[512,1024]{1,0:T(8,128)(2,1)} %get-tuple-element.25), channel_id=1, source_target_pairs={{0,8},{1,9},{2,10},{3,11},{4,12},{5,13},{6,14},{7,15},{8,0},{9,1},... | collective-permute-start | bytes 3145736 | tf_op jit(solution)/shard_map/ppermute | solution.py:279
  35.2 28.9 %collective-permute-start.5 = (bf16[512,1024]{1,0:T(8,128)(2,1)}, bf16[512,1024]{1,0:T(8,128)(2,1)S(1)}, u32[]{:S(2)}, u32[]{:S(2)}) collective-permute-start(bf16[512,1024]{1,0:T(8,128)(2,1)} %get-tuple-element.26), channel_id=1, source_target_pairs={{0,12},{1,13},{2,14},{3,15},{4,0},{5,1},{6,2},{7,3},{8,4},{9,5},{1... | collective-permute-start | bytes 3145736 | tf_op jit(solution)/shard_map/ppermute | solution.py:279
  56.0 1.0 copy-start
  57.0 20.1 %all-to-all-start.2 = ((bf16[16,2,64,256]{3,2,1,0:T(8,128)(2,1)}), bf16[16,2,64,256]{3,2,1,0:T(8,128)(2,1)}, u32[]{:S(2)}, u32[]{:S(2)}) async-start(bf16[16,2,64,256]{3,2,1,0:T(8,128)(2,1)} %bitcast.21), calls=%async_computation.2 | async-start | bytes 2097152 | tf_op jit(solution)/shard_map/all_to_all | solution.py:369
  61.4 20.1 %collective-permute-start.6 = (bf16[512,1024]{1,0:T(8,128)(2,1)S(1)}, bf16[512,1024]{1,0:T(8,128)(2,1)}, u32[]{:S(2)}, u32[]{:S(2)}) collective-permute-start(bf16[512,1024]{1,0:T(8,128)(2,1)S(1)} %collective-permute-done.3.refs_5_), channel_id=1, source_target_pairs={{0,16},{16,0},{32,48},{48,32},{64,80},{80,64},{96,112},{112,96},{1... | collective-permute-start | bytes 3145736 | tf_op jit(solution)/shard_map/ppermute | solution.py:283
  63.5 18.0 %collective-permute-start.7 = (bf16[512,1024]{1,0:T(8,128)(2,1)S(1)}, bf16[512,1024]{1,0:T(8,128)(2,1)}, u32[]{:S(2)}, u32[]{:S(2)}) collective-permute-start(bf16[512,1024]{1,0:T(8,128)(2,1)S(1)} %collective-permute-done.4.refs_6_), channel_id=1, source_target_pairs={{0,16},{16,0},{32,48},{48,32},{64,80},{80,64},{96,112},{112,96},{1... | collective-permute-start | bytes 3145736 | tf_op jit(solution)/shard_map/ppermute | solution.py:283
  64.0 18.8 %collective-permute-start.8 = (bf16[512,1024]{1,0:T(8,128)(2,1)S(1)}, bf16[512,1024]{1,0:T(8,128)(2,1)}, u32[]{:S(2)}, u32[]{:S(2)}) collective-permute-start(bf16[512,1024]{1,0:T(8,128)(2,1)S(1)} %collective-permute-done.5.refs_7_), channel_id=1, source_target_pairs={{0,16},{16,0},{32,48},{48,32},{64,80},{80,64},{96,112},{112,96},{1... | collective-permute-start | bytes 3145736 | tf_op jit(solution)/shard_map/ppermute | solution.py:283
  78.8 8.4 %collective-permute-start.14 = (bf16[256,512]{1,0:T(8,128)(2,1)S(1)}, bf16[256,512]{1,0:T(8,128)(2,1)S(1)}, u32[]{:S(2)}, u32[]{:S(2)}) collective-permute-start(bf16[256,512]{1,0:T(8,128)(2,1)S(1)} %image_grads.1.refs_0_), channel_id=1, source_target_pairs={{0,3},{1,0},{2,1},{3,2},{4,7},{5,4},{6,5},{7,6},{8,11},{9,8},{10,9... | collective-permute-start | bytes 786440 | tf_op jit(solution)/shard_map/ppermute | solution.py:268
  79.4 9.5 %collective-permute-start.13 = (bf16[256,512]{1,0:T(8,128)(2,1)S(1)}, bf16[256,512]{1,0:T(8,128)(2,1)S(1)}, u32[]{:S(2)}, u32[]{:S(2)}) collective-permute-start(bf16[256,512]{1,0:T(8,128)(2,1)S(1)} %image_grads.1.refs_0_), channel_id=1, source_target_pairs={{0,2},{1,3},{2,0},{3,1},{4,6},{5,7},{6,4},{7,5},{8,10},{9,11},{10,... | collective-permute-start | bytes 786440 | tf_op jit(solution)/shard_map/ppermute | solution.py:268
  81.5 10.1 %collective-permute-start.12 = (bf16[256,512]{1,0:T(8,128)(2,1)S(1)}, bf16[256,512]{1,0:T(8,128)(2,1)S(1)}, u32[]{:S(2)}, u32[]{:S(2)}) collective-permute-start(bf16[256,512]{1,0:T(8,128)(2,1)S(1)} %image_grads.1.refs_0_), channel_id=1, source_target_pairs={{0,1},{1,2},{2,3},{3,0},{4,5},{5,6},{6,7},{7,4},{8,9},{9,10},{10,1... | collective-permute-start | bytes 786440 | tf_op jit(solution)/shard_map/ppermute | solution.py:268
  81.5 16.3 %collective-permute-start.2 = (bf16[256,512]{1,0:T(8,128)(2,1)S(1)}, bf16[256,512]{1,0:T(8,128)(2,1)S(1)}, u32[]{:S(2)}, u32[]{:S(2)}) collective-permute-start(bf16[256,512]{1,0:T(8,128)(2,1)S(1)} %image_grads.1.refs_0_), channel_id=1, source_target_pairs={{0,12},{1,13},{2,14},{3,15},{4,0},{5,1},{6,2},{7,3},{8,4},{9,5},{1... | collective-permute-start | bytes 786440 | tf_op jit(solution)/shard_map/ppermute | solution.py:268
  82.8 16.3 %collective-permute-start.1 = (bf16[256,512]{1,0:T(8,128)(2,1)S(1)}, bf16[256,512]{1,0:T(8,128)(2,1)S(1)}, u32[]{:S(2)}, u32[]{:S(2)}) collective-permute-start(bf16[256,512]{1,0:T(8,128)(2,1)S(1)} %image_grads.1.refs_0_), channel_id=1, source_target_pairs={{0,8},{1,9},{2,10},{3,11},{4,12},{5,13},{6,14},{7,15},{8,0},{9,1},... | collective-permute-start | bytes 786440 | tf_op jit(solution)/shard_map/ppermute | solution.py:268
  87.2 11.9 %collective-permute-start = (bf16[256,512]{1,0:T(8,128)(2,1)S(1)}, bf16[256,512]{1,0:T(8,128)(2,1)S(1)}, u32[]{:S(2)}, u32[]{:S(2)}) collective-permute-start(bf16[256,512]{1,0:T(8,128)(2,1)S(1)} %image_grads.1.refs_0_), channel_id=1, source_target_pairs={{0,4},{1,5},{2,6},{3,7},{4,8},{5,9},{6,10},{7,11},{8,12},{9,13},{1... | collective-permute-start | bytes 786440 | tf_op jit(solution)/shard_map/ppermute | solution.py:268
  95.0 9.9 %collective-permute-start.15 = (bf16[256,256]{1,0:T(8,128)(2,1)S(1)}, bf16[256,256]{1,0:T(8,128)(2,1)S(1)}, u32[]{:S(2)}, u32[]{:S(2)}) collective-permute-start(bf16[256,256]{1,0:T(8,128)(2,1)S(1)} %get-tuple-element.32), channel_id=1, source_target_pairs={{0,4},{1,5},{2,6},{3,7},{4,8},{5,9},{6,10},{7,11},{8,12},{9,13},{1... | collective-permute-start | bytes 393224 | tf_op jit(solution)/shard_map/ppermute | solution.py:268
  95.1 12.3 %collective-permute-start.16 = (bf16[256,256]{1,0:T(8,128)(2,1)S(1)}, bf16[256,256]{1,0:T(8,128)(2,1)S(1)}, u32[]{:S(2)}, u32[]{:S(2)}) collective-permute-start(bf16[256,256]{1,0:T(8,128)(2,1)S(1)} %get-tuple-element.33), channel_id=1, source_target_pairs={{0,8},{1,9},{2,10},{3,11},{4,12},{5,13},{6,14},{7,15},{8,0},{9,1},... | collective-permute-start | bytes 393224 | tf_op jit(solution)/shard_map/ppermute | solution.py:268
  97.8 9.6 %collective-permute-start.17 = (bf16[256,256]{1,0:T(8,128)(2,1)S(1)}, bf16[256,256]{1,0:T(8,128)(2,1)S(1)}, u32[]{:S(2)}, u32[]{:S(2)}) collective-permute-start(bf16[256,256]{1,0:T(8,128)(2,1)S(1)} %get-tuple-element.34), channel_id=1, source_target_pairs={{0,12},{1,13},{2,14},{3,15},{4,0},{5,1},{6,2},{7,3},{8,4},{9,5},{1... | collective-permute-start | bytes 393224 | tf_op jit(solution)/shard_map/ppermute | solution.py:268
  102.5 6.2 %collective-permute-start.9 = (bf16[256,256]{1,0:T(8,128)(2,1)S(1)}, bf16[256,256]{1,0:T(8,128)(2,1)S(1)}, u32[]{:S(2)}, u32[]{:S(2)}) collective-permute-start(bf16[256,256]{1,0:T(8,128)(2,1)S(1)} %get-tuple-element.28), channel_id=1, source_target_pairs={{0,1},{1,2},{2,3},{3,0},{4,5},{5,6},{6,7},{7,4},{8,9},{9,10},{10,1... | collective-permute-start | bytes 393224 | tf_op jit(solution)/shard_map/ppermute | solution.py:268
  104.6 6.5 %collective-permute-start.10 = (bf16[256,256]{1,0:T(8,128)(2,1)S(1)}, bf16[256,256]{1,0:T(8,128)(2,1)S(1)}, u32[]{:S(2)}, u32[]{:S(2)}) collective-permute-start(bf16[256,256]{1,0:T(8,128)(2,1)S(1)} %get-tuple-element.29), channel_id=1, source_target_pairs={{0,2},{1,3},{2,0},{3,1},{4,6},{5,7},{6,4},{7,5},{8,10},{9,11},{10,... | collective-permute-start | bytes 393224 | tf_op jit(solution)/shard_map/ppermute | solution.py:268
  105.0 6.1 %collective-permute-start.11 = (bf16[256,256]{1,0:T(8,128)(2,1)S(1)}, bf16[256,256]{1,0:T(8,128)(2,1)S(1)}, u32[]{:S(2)}, u32[]{:S(2)}) collective-permute-start(bf16[256,256]{1,0:T(8,128)(2,1)S(1)} %get-tuple-element.30), channel_id=1, source_target_pairs={{0,3},{1,0},{2,1},{3,2},{4,7},{5,4},{6,5},{7,6},{8,11},{9,8},{10,9... | collective-permute-start | bytes 393224 | tf_op jit(solution)/shard_map/ppermute | solution.py:268

commit v4 on v3

--- a/solution.py
+++ b/solution.py
@@ -172,9 +172,11 @@
             low = (lax.rem(x_at + step + 1, SIDE) * SIDE + k) * (2 * width)
             high = (k * SIDE + lax.rem(z_at + step + 1, SIDE)) * (2 * width) + width
             start = pl.multiple_of(jnp.where(core == 0, low, high), width)
+            count = out.shape[0]
+            first = pl.multiple_of(place[3] * count if step == 1 else 0, count)
             copies.append(
                 pltpu.make_async_copy(
-                    features.at[:, pl.ds(start, width)],
+                    features.at[pl.ds(first, count), pl.ds(start, width)],
                     out.at[:, pl.ds(k * width, width)],
                     sems.at[step, k],
                 )
@@ -199,54 +201,63 @@
     grad_low[...] = total.T.astype(BF16)
 
 
-def weight_kernel(place, *refs, half):
-    grads, features, sources = refs[:SIDE], refs[SIDE], refs[SIDE + 1 : 3 * SIDE - 1]
-    outs = refs[3 * SIDE - 1 : 4 * SIDE - 1]
-    rows, total, sems = refs[4 * SIDE - 1 :]
+def near_kernel(place, grad_low, features, *rest):
+    sources, (grad_again, rows, sems) = rest[:-3], rest[-3:]
     x_at, z_at, core = place[0], place[1], place[2]
-    width = rows.shape[2] // SIDE
-
-    def own_copy(k):
+    width = rows.shape[3] // SIDE
+
+    def own_copy(half, k):
         if half == 0:
             start = (x_at * SIDE + k) * (2 * width)
         else:
             start = (k * SIDE + z_at) * (2 * width) + width
         return pltpu.make_async_copy(
             features.at[:, pl.ds(pl.multiple_of(start, width), width)],
-            rows.at[0, :, pl.ds(k * width, width)],
-            sems.at[k],
-        )
-
-    def far_copy(step, source):
-        return pltpu.make_async_copy(source, rows.at[step + 1], sems.at[SIDE + step])
-
-    for k in range(SIDE):
-        own_copy(k).start()
-    for at, part in ((half, sources[: SIDE - 1]), (1 - half, sources[SIDE - 1 :])):
-
-        @pl.when(core == at)
-        def _():
-            for step in range(SIDE - 1):
-                far_copy(step, part[step]).start()
-
-    for k in range(SIDE):
-        own_copy(k).wait()
-    for index in range(SIDE):
-        if index:
-            far_copy(index - 1, sources[index - 1]).wait()
+            rows.at[half, 0, :, pl.ds(k * width, width)],
+            sems.at[half, k],
+        )
+
+    def far_copy(half, index, source):
+        to = rows.at[half, (1, 2, 2, 3)[index]]
+        if index in (1, 2):
+            count = source.shape[0]
+            first = place[3] if index == 1 else 1 - place[3]
+            to = to.at[pl.ds(pl.multiple_of(first * count, count), count)]
+        return pltpu.make_async_copy(source, to, sems.at[half, SIDE + index])
+
+    far = len(sources) // 2
+    for half in range(2):
         for k in range(SIDE):
+            own_copy(half, k).start()
+        for at, part in ((half, sources[:far]), (1 - half, sources[far:])):
+
+            @pl.when(core == at)
+            def _():
+                for step in range(far):
+                    far_copy(half, step, part[step]).start()
+
+    grad_again[...] = grad_low[...]
+    for half in range(2):
+        for k in range(SIDE):
+            own_copy(half, k).wait()
+        for step in range(far):
+            far_copy(half, step, sources[step]).wait()
+
+
+def weight_kernel(place, *refs, half):
+    grads, rows, outs = refs[:SIDE], refs[SIDE], refs[SIDE + 1 :]
+    width = rows.shape[3] // SIDE
+    for step in range(SIDE):
+        start = pl.multiple_of(lax.rem(place[1 - half] + step, SIDE) * width, width)
+        total = None
+        for index in range(SIDE):
             part = jnp.dot(
                 grads[index][...],
-                rows[index, :, k * width : (k + 1) * width],
+                rows[half, index, :, pl.ds(start, width)],
                 preferred_element_type=F32,
             )
-            if index:
-                total[k] += part
-            else:
-                total[k] = part
-    for step in range(SIDE):
-        piece = total[lax.rem(place[1 - half] + step, SIDE)]
-        outs[step][...] = piece.astype(outs[step].dtype)
+            total = part if index == 0 else total + part
+        outs[step][...] = total.astype(outs[step].dtype)
 
 
 def final_kernel(*refs):
@@ -279,8 +290,8 @@
     return lax.ppermute(values, ("img", "txt"), pairs)
 
 
-def swap_cores(values):
-    return lax.ppermute(values, "img", [(i, i ^ 1) for i in range(lax.axis_size("img"))])
+def swap_img(values, bit):
+    return lax.ppermute(values, "img", [(i, i ^ bit) for i in range(lax.axis_size("img"))])
 
 
 def shards(features, tile_count, kv_weight, queries, out_grad, image_ids, text_len):
@@ -312,7 +323,7 @@
         name="request_table",
     )(image_ids.T, tile_count)
     table = lax.all_to_all(wanted, "txt", 0, 0, tiled=True)
-    place = jnp.stack([shard_index // SIDE, shard_index % SIDE, lax.axis_index("img") % 2])
+    place = jnp.stack([shard_index // SIDE, shard_index % SIDE, lax.axis_index("img") % 2, lax.axis_index("img") // 2 % 2])
 
     flat_features = features.reshape(img_dev * keys_img, feat_width)
     own_pairs = jnp.dot(
@@ -333,10 +344,14 @@
 
     block = feat_width // txt_count
     width = block // 2
+    held_rows = img_dev * keys_img
     held_features = pltpu.with_memory_space_constraint(flat_features, pltpu.HBM)
     messages = pl.pallas_call(
         pack_kernel,
-        out_shape=[jax.ShapeDtypeStruct((img_dev * keys_img, SIDE * width), BF16)] * (SIDE - 1),
+        out_shape=[
+            jax.ShapeDtypeStruct((count, SIDE * width), BF16)
+            for count in (held_rows, held_rows // 2, held_rows)
+        ],
         in_specs=[scalars, in_hbm, in_hbm],
         out_specs=[whole] * (SIDE - 1),
         scratch_shapes=[pltpu.SemaphoreType.DMA((SIDE - 1, SIDE))],
@@ -347,7 +362,8 @@
         name="pack_features",
     )(place, sent_pairs, held_features)
     got_features = [feature_shift(part, step + 1) for step, part in enumerate(messages)]
-    swapped_features = [swap_cores(part) for part in got_features]
+    got_features.insert(2, swap_img(got_features[1], 2))
+    swapped_features = [swap_img(part, 1) for part in got_features]
     attended, grad_query, slot_grad = pl.pallas_call(
         functools.partial(attend_kernel, img_dev=img_dev),
         out_shape=[
@@ -379,8 +395,25 @@
         compiler_params=params(8),
         name="image_grads",
     )(table, back_grad)
+    grad_again, near = pl.pallas_call(
+        near_kernel,
+        out_shape=[
+            jax.ShapeDtypeStruct(grad_low.shape, BF16),
+            jax.ShapeDtypeStruct((2, SIDE, img_dev * keys_img, SIDE * width), BF16),
+        ],
+        in_specs=[scalars, whole] + [in_hbm] * (2 * SIDE + 1),
+        out_specs=[whole] * 2,
+        scratch_shapes=[pltpu.SemaphoreType.DMA((2, 2 * SIDE))],
+        compiler_params=params(4),
+        cost_estimate=pl.CostEstimate(
+            flops=0, bytes_accessed=2 * flat_features.size, transcendentals=0
+        ),
+        name="near_features",
+    )(place, grad_low, held_features, *got_features, *swapped_features)
     along = {
-        (half, step): shift(grad_low, "xz"[half], step) for step in (2, 1, 3) for half in range(2)
+        (half, step): shift(grad_again if (half, step) == (1, 3) else grad_low, "xz"[half], step)
+        for step in (2, 1, 3)
+        for half in range(2)
     }
     final = []
     for half in range(2):
@@ -390,23 +423,11 @@
                 jax.ShapeDtypeStruct((cols, width), F32 if step == 0 else BF16)
                 for step in range(SIDE)
             ],
-            in_specs=[scalars] + [whole] * SIDE + [in_hbm] * (2 * SIDE - 1),
+            in_specs=[scalars] + [whole] * (SIDE + 1),
             out_specs=[whole] * SIDE,
-            scratch_shapes=[
-                pltpu.VMEM((SIDE, img_dev * keys_img, SIDE * width), BF16),
-                pltpu.VMEM((SIDE, cols, width), F32),
-                pltpu.SemaphoreType.DMA((2 * SIDE,)),
-            ],
-            compiler_params=params(12),
+            compiler_params=params(8),
             name="weight_part",
-        )(
-            place,
-            grad_low,
-            *[along[half, step] for step in range(1, SIDE)],
-            held_features,
-            *got_features,
-            *swapped_features,
-        )
+        )(place, grad_low, *[along[half, step] for step in range(1, SIDE)], near)
         final += [own] + [shift(part, "zx"[half], step + 1) for step, part in enumerate(others)]
     weight_grad = pl.pallas_call(
         final_kernel,

time: 113 us -> 110 us (0.973)
  waiting for transfers between devices: 33.7 us -> 26.5 us
  starting transfers between devices: 39.8 us -> 45.2 us
    all_to_all x1, waiting for transfers between devices: 13 us -> 2.83 us  [shards(): lax.all_to_all(slot_grad.reshape(txt_count, CAP, keys_img, cols), 'txt',...]
    ppermute x3 -> x5, waiting for transfers between devices: 0.01 us -> 10.1 us  [swap_img(): lax.ppermute(values, 'img', [(i, i ^ bit) for i in range(lax.axis_size('i...]
    ppermute x12, waiting for transfers between devices: 11.4 us -> 5.54 us  [shift(): return lax.ppermute(values, 'txt', pairs)]
    ppermute x12, starting transfers between devices: 14 us -> 19.2 us  [shift(): return lax.ppermute(values, 'txt', pairs)]
    pallas_call x1 -> x2, Pallas kernels: 4.22 us -> 7.42 us  [the longest x1 3.84 us: shards(): pl.pallas_call(pack_kernel, out_shape=[jax.ShapeDtypeStruct((count, SIDE...]
    pallas_call x2, Pallas kernels: 6.78 us -> 3.66 us  [shards(): pl.pallas_call(functools.partial(weight_kernel, half=half), out_shape=[ja...]
    ppermute x3, waiting for transfers between devices: 2.1 us -> 0.01 us  [feature_shift(): return lax.ppermute(values, ('img', 'txt'), pairs)]
    ppermute x3 -> x5, starting transfers between devices: 0.6 us -> 2.25 us  [swap_img(): lax.ppermute(values, 'img', [(i, i ^ bit) for i in range(lax.axis_size('i...]
  transfers between devices with their start and end apart: 21 -> 23, of which waited for: 9 -> 9; matrix products, arithmetic and copies ran while one was open for 6% -> 6% of each run, Pallas kernels for 23% -> 23%
where the time goes in v4:
time: 110 us
  starting transfers between devices  45.2 us (41%)
  Pallas kernels  29.3 us (27%)
  waiting for transfers between devices  26.5 us (24%)
  matrix products  6.91 us (6%)
    ppermute x12, starting transfers between devices, shift(): return lax.ppermute(values, 'txt', pairs)  19.2 us
    pallas_call x1, Pallas kernels, shards(): pl.pallas_call(functools.partial(attend_kernel, img_dev=img_dev), out_sha...  12.5 us
    ppermute x5, waiting for transfers between devices, swap_img(): lax.ppermute(values, 'img', [(i, i ^ bit) for i in range(lax.axis_size('i...  10.1 us
    all_to_all x1, starting transfers between devices, shards(): table = lax.all_to_all(wanted, 'txt', 0, 0, tiled=True)  7.97 us
    all_to_all x1, waiting for transfers between devices, shards(): lax.all_to_all(sent_pairs.reshape(txt_count, CAP, keys_img, cols), 'txt',...  7.47 us
    dot_general x1, matrix products, shards(): jnp.dot(flat_features, kv_weight.reshape(feat_width, cols), preferred_ele...  6.91 us
    all_to_all x1, starting transfers between devices, shards(): lax.all_to_all(sent_pairs.reshape(txt_count, CAP, keys_img, cols), 'txt',...  6.67 us
    ppermute x12, waiting for transfers between devices, shift(): return lax.ppermute(values, 'txt', pairs)  5.54 us
  transfers between devices with their start and end apart: 23, of which 9 were waited for; matrix products, arithmetic and copies ran while one was open for 6% of the time, Pallas kernels for 23%

profile of v4, /device:TPU:0, one launch (start us, length us, event | category | flops | bytes accessed | tf_op | source)
XLA Modules:
  0.0 109.8 jit_solution(6533606844889308734)
XLA Ops:
  0.6 1.5 %request_table.1 = (s32[16,128]{1,0:T(8,128)}, s32[48]{0:T(128)}) custom-call(s32[2,12]{1,0:T(2,128)} %bitcast.34, s32[8]{0:T(128)} %counts.1), custom_call_target="tpu_custom_call" | custom-call | tf_op jit(solution)/shard_map/request_table/pallas_call | solution.py:314
  2.1 8.0 %all-to-all-start = ((s32[16,1,128]{2,1,0:T(1,128)}), s32[16,1,128]{2,1,0:T(1,128)S(1)}, u32[]{:S(2)}, u32[]{:S(2)}) async-start(s32[16,1,128]{2,1,0:T(1,128)} %bitcast.32), calls=%async_computation | async-start | bytes 16384 | tf_op jit(solution)/shard_map/all_to_all | solution.py:325
  10.1 6.9 %fusion.3 = bf16[512,256]{1,0:T(8,128)(2,1)S(1)} fusion(bf16[512,8192]{1,0:T(8,128)(2,1)} %bitcast.29, bf16[1024,8,2,128]{3,2,1,0:T(2,128)(2,1)} %bitcast.33), kind=kOutput, calls=%fused_computation.3 | convolution fusion | flops 2147614720 | bytes 12845056 | tf_op jit(solution)/shard_map/dot_general | solution.py:329
  17.6 1.9 %fill_slots.1.after = bf16[32,64,256]{2,1,0:T(8,128)(2,1)} custom-call(s32[16,128]{1,0:T(8,128)S(1)} %bitcast.26, bf16[8,64,256]{2,1,0:T(8,128)(2,1)S(1)} %bitcast.25), custom_call_target="tpu_custom_call" | custom-call | tf_op jit(solution)/shard_map/fill_slots/pallas_call | solution.py:332
  19.5 6.7 %all-to-all-start.1 = ((bf16[16,2,64,256]{3,2,1,0:T(8,128)(2,1)}), bf16[16,2,64,256]{3,2,1,0:T(8,128)(2,1)S(1)}, u32[]{:S(2)}, u32[]{:S(2)}) async-start(bf16[16,2,64,256]{3,2,1,0:T(8,128)(2,1)} %bitcast.6), calls=%async_computation.1 | async-start | bytes 2097152 | tf_op jit(solution)/shard_map/all_to_all | solution.py:341
  26.3 3.8 %pack_features.1 = (bf16[512,1024]{1,0:T(8,128)(2,1)}, bf16[256,1024]{1,0:T(8,128)(2,1)}, bf16[512,1024]{1,0:T(8,128)(2,1)}) custom-call(s32[4]{0:T(128)S(1)} %pad_add_fusion.place, bf16[32,64,256]{2,1,0:T(8,128)(2,1)} %fill_slots.1.after, bf16[512,8192]{1,0:T(8,128)(2,1)} %bitcast.30), custom_call_target="tpu_custom_call" | custom-call | bytes 8388608 | tf_op jit(solution)/shard_map/pack_features/pallas_call | solution.py:349
  30.2 3.2 %collective-permute-start.6 = (bf16[512,1024]{1,0:T(8,128)(2,1)}, bf16[512,1024]{1,0:T(8,128)(2,1)S(1)}, u32[]{:S(2)}, u32[]{:S(2)}) collective-permute-start(bf16[512,1024]{1,0:T(8,128)(2,1)} %get-tuple-element.28), channel_id=1, source_target_pairs={{0,12},{1,13},{2,14},{3,15},{4,0},{5,1},{6,2},{7,3},{8,4},{9,5},{1... | collective-permute-start | bytes 3145736 | tf_op jit(solution)/shard_map/ppermute | solution.py:290
  33.3 2.3 %collective-permute-start.4 = (bf16[256,1024]{1,0:T(8,128)(2,1)}, bf16[256,1024]{1,0:T(8,128)(2,1)}, u32[]{:S(2)}, u32[]{:S(2)}) collective-permute-start(bf16[256,1024]{1,0:T(8,128)(2,1)} %get-tuple-element.27), channel_id=1, source_target_pairs={{0,8},{1,9},{2,10},{3,11},{4,12},{5,13},{6,14},{7,15},{8,0},{9,1},... | collective-permute-start | bytes 1572872 | tf_op jit(solution)/shard_map/ppermute | solution.py:290
  35.6 7.5 %all-to-all-done.1 = bf16[16,2,64,256]{3,2,1,0:T(8,128)(2,1)S(1)} async-done(((bf16[16,2,64,256]{3,2,1,0:T(8,128)(2,1)}), bf16[16,2,64,256]{3,2,1,0:T(8,128)(2,1)S(1)}, u32[]{:S(2)}, u32[]{:S(2)}) %all-to-all-start.1) | async-done | bytes 1048608 | tf_op jit(solution)/shard_map/all_to_all | solution.py:341
  43.1 12.5 %attend.1 = (bf16[1536,1024]{1,0:T(8,128)(2,1)}, bf16[1536,1024]{1,0:T(8,128)(2,1)}, bf16[32,64,256]{2,1,0:T(8,128)(2,1)S(1)}) custom-call(s32[48]{0:T(128)S(1)} %copy-done.2, s32[16,128]{1,0:T(8,128)S(1)} %bitcast.27, s32[12]{0:T(128)S(1)} %copy-done.1, bf16[1536,1024]{1,0:T(8,128)(2,1)} %queries.1, bf16[1536,1024]{1,0:T(8,128)(2,1)} %grads.1, ...), custom_call_target="tpu_custom_call" | custom-call | tf_op jit(solution)/shard_map/attend/pallas_call | solution.py:367
  56.6 3.7 %all-to-all-start.2 = ((bf16[16,2,64,256]{3,2,1,0:T(8,128)(2,1)}), bf16[16,2,64,256]{3,2,1,0:T(8,128)(2,1)S(1)}, u32[]{:S(2)}, u32[]{:S(2)}) async-start(bf16[16,2,64,256]{3,2,1,0:T(8,128)(2,1)} %bitcast.24), calls=%async_computation.2 | async-start | bytes 2097152 | tf_op jit(solution)/shard_map/all_to_all | solution.py:385
  60.3 1.7 %collective-permute-start.5 = (bf16[256,1024]{1,0:T(8,128)(2,1)}, bf16[256,1024]{1,0:T(8,128)(2,1)}, u32[]{:S(2)}, u32[]{:S(2)}) collective-permute-start(bf16[256,1024]{1,0:T(8,128)(2,1)} %collective-permute-done.4.rest_1_), channel_id=1, source_target_pairs={{0,32},{16,48},{32,0},{48,16},{64,96},{80,112},{96,64},{112,80},{1... | collective-permute-start | bytes 1572872 | tf_op jit(solution)/shard_map/ppermute | solution.py:294
  62.6 10.1 %collective-permute-done.5.rest_2_ = bf16[256,1024]{1,0:T(8,128)(2,1)} collective-permute-done((bf16[256,1024]{1,0:T(8,128)(2,1)}, bf16[256,1024]{1,0:T(8,128)(2,1)}, u32[]{:S(2)}, u32[]{:S(2)}) %collective-permute-start.5) | collective-permute-done | bytes 524320 | tf_op jit(solution)/shard_map/ppermute | solution.py:294
  72.6 2.8 %all-to-all-done.2 = bf16[16,2,64,256]{3,2,1,0:T(8,128)(2,1)S(1)} async-done(((bf16[16,2,64,256]{3,2,1,0:T(8,128)(2,1)}), bf16[16,2,64,256]{3,2,1,0:T(8,128)(2,1)S(1)}, u32[]{:S(2)}, u32[]{:S(2)}) %all-to-all-start.2) | async-done | bytes 1048608 | tf_op jit(solution)/shard_map/all_to_all | solution.py:385
  75.5 1.2 %image_grads.1.grad_low.refs_0_ = bf16[256,512]{1,0:T(8,128)(2,1)S(1)} custom-call(s32[16,128]{1,0:T(8,128)S(1)} %bitcast.28, bf16[32,64,256]{2,1,0:T(8,128)(2,1)S(1)} %bitcast.23), custom_call_target="tpu_custom_call" | custom-call | tf_op jit(solution)/shard_map/image_grads/pallas_call | solution.py:389
  76.8 2.6 %collective-permute-start.1 = (bf16[256,512]{1,0:T(8,128)(2,1)S(1)}, bf16[256,512]{1,0:T(8,128)(2,1)S(1)}, u32[]{:S(2)}, u32[]{:S(2)}) collective-permute-start(bf16[256,512]{1,0:T(8,128)(2,1)S(1)} %image_grads.1.grad_low.refs_0_), channel_id=1, source_target_pairs={{0,8},{1,9},{2,10},{3,11},{4,12},{5,13},{6,14},{7,15},{8,0},{9,1},... | collective-permute-start | bytes 786440 | tf_op jit(solution)/shard_map/ppermute | solution.py:279
  79.4 1.1 collective-permute-start.2
  80.8 2.5 %collective-permute-start.15 = (bf16[256,512]{1,0:T(8,128)(2,1)S(1)}, bf16[256,512]{1,0:T(8,128)(2,1)S(1)}, u32[]{:S(2)}, u32[]{:S(2)}) collective-permute-start(bf16[256,512]{1,0:T(8,128)(2,1)S(1)} %image_grads.1.grad_low.refs_0_), channel_id=1, source_target_pairs={{0,2},{1,3},{2,0},{3,1},{4,6},{5,7},{6,4},{7,5},{8,10},{9,11},{10,... | collective-permute-start | bytes 786440 | tf_op jit(solution)/shard_map/ppermute | solution.py:279
  83.3 3.6 %near_features.1 = (bf16[256,512]{1,0:T(8,128)(2,1)S(1)}, bf16[2,4,512,1024]{3,2,1,0:T(8,128)(2,1)S(1)}) custom-call(s32[4]{0:T(128)S(1)} %pad_add_fusion.place, bf16[256,512]{1,0:T(8,128)(2,1)S(1)} %image_grads.1.grad_low.refs_0_, bf16[512,8192]{1,0:T(8,128)(2,1)} %bitcast.31, bf16[512,1024]{1,0:T(8,128)(2,1)S(1)} %collective-permute-done.3.rest_0_, ...), custom_call_target="tpu_custom_call" | custom-call | bytes 8388608 | tf_op jit(solution)/shard_map/near_features/pallas_call | solution.py:398
  86.9 1.5 %collective-permute-start.16 = (bf16[256,512]{1,0:T(8,128)(2,1)S(1)}, bf16[256,512]{1,0:T(8,128)(2,1)S(1)}, u32[]{:S(2)}, u32[]{:S(2)}) collective-permute-start(bf16[256,512]{1,0:T(8,128)(2,1)S(1)} %get-tuple-element.34), channel_id=1, source_target_pairs={{0,3},{1,0},{2,1},{3,2},{4,7},{5,4},{6,5},{7,6},{8,11},{9,8},{10,9... | collective-permute-start | bytes 786440 | tf_op jit(solution)/shard_map/ppermute | solution.py:279
  88.4 1.5 %collective-permute-done.1.refs_2_ = bf16[256,512]{1,0:T(8,128)(2,1)S(1)} collective-permute-done((bf16[256,512]{1,0:T(8,128)(2,1)S(1)}, bf16[256,512]{1,0:T(8,128)(2,1)S(1)}, u32[]{:S(2)}, u32[]{:S(2)}) %collective-permute-start.1) | collective-permute-done | bytes 262176 | tf_op jit(solution)/shard_map/ppermute | solution.py:279
  90.0 1.8 %weight_part.2 = (f32[256,256]{1,0:T(8,128)S(1)}, bf16[256,256]{1,0:T(8,128)(2,1)S(1)}, bf16[256,256]{1,0:T(8,128)(2,1)S(1)}, bf16[256,256]{1,0:T(8,128)(2,1)S(1)}) custom-call(s32[4]{0:T(128)S(1)} %pad_add_fusion.place, bf16[256,512]{1,0:T(8,128)(2,1)S(1)} %image_grads.1.grad_low.refs_0_, bf16[256,512]{1,0:T(8,128)(2,1)S(1)} %collective-permute-done.refs_1_, ...), custom_call_target="tpu_custom_call" | custom-call | tf_op jit(solution)/shard_map/weight_part/pallas_call | solution.py:420
  91.9 1.5 %collective-permute-start.11 = (bf16[256,256]{1,0:T(8,128)(2,1)S(1)}, bf16[256,256]{1,0:T(8,128)(2,1)S(1)}, u32[]{:S(2)}, u32[]{:S(2)}) collective-permute-start(bf16[256,256]{1,0:T(8,128)(2,1)S(1)} %get-tuple-element.31), channel_id=1, source_target_pairs={{0,1},{1,2},{2,3},{3,0},{4,5},{5,6},{6,7},{7,4},{8,9},{9,10},{10,1... | collective-permute-start | bytes 393224 | tf_op jit(solution)/shard_map/ppermute | solution.py:279
  93.4 2.7 %collective-permute-start.12 = (bf16[256,256]{1,0:T(8,128)(2,1)S(1)}, bf16[256,256]{1,0:T(8,128)(2,1)S(1)}, u32[]{:S(2)}, u32[]{:S(2)}) collective-permute-start(bf16[256,256]{1,0:T(8,128)(2,1)S(1)} %get-tuple-element.32), channel_id=1, source_target_pairs={{0,2},{1,3},{2,0},{3,1},{4,6},{5,7},{6,4},{7,5},{8,10},{9,11},{10,... | collective-permute-start | bytes 393224 | tf_op jit(solution)/shard_map/ppermute | solution.py:279
  96.0 1.5 %collective-permute-start.13 = (bf16[256,256]{1,0:T(8,128)(2,1)S(1)}, bf16[256,256]{1,0:T(8,128)(2,1)S(1)}, u32[]{:S(2)}, u32[]{:S(2)}) collective-permute-start(bf16[256,256]{1,0:T(8,128)(2,1)S(1)} %get-tuple-element.33), channel_id=1, source_target_pairs={{0,3},{1,0},{2,1},{3,2},{4,7},{5,4},{6,5},{7,6},{8,11},{9,8},{10,9... | collective-permute-start | bytes 393224 | tf_op jit(solution)/shard_map/ppermute | solution.py:279
  97.5 1.8 %weight_part.3 = (f32[256,256]{1,0:T(8,128)S(1)}, bf16[256,256]{1,0:T(8,128)(2,1)S(1)}, bf16[256,256]{1,0:T(8,128)(2,1)S(1)}, bf16[256,256]{1,0:T(8,128)(2,1)S(1)}) custom-call(s32[4]{0:T(128)S(1)} %pad_add_fusion.place, bf16[256,512]{1,0:T(8,128)(2,1)S(1)} %image_grads.1.grad_low.refs_0_, bf16[256,512]{1,0:T(8,128)(2,1)S(1)} %collective-permute-done.14.refs_1_, ...), custom_call_target="tpu_custom_call" | custom-call | tf_op jit(solution)/shard_map/weight_part/pallas_call | solution.py:420
  99.4 1.5 %collective-permute-start.17 = (bf16[256,256]{1,0:T(8,128)(2,1)S(1)}, bf16[256,256]{1,0:T(8,128)(2,1)S(1)}, u32[]{:S(2)}, u32[]{:S(2)}) collective-permute-start(bf16[256,256]{1,0:T(8,128)(2,1)S(1)} %get-tuple-element.36), channel_id=1, source_target_pairs={{0,4},{1,5},{2,6},{3,7},{4,8},{5,9},{6,10},{7,11},{8,12},{9,13},{1... | collective-permute-start | bytes 393224 | tf_op jit(solution)/shard_map/ppermute | solution.py:279
  100.9 2.4 %collective-permute-start.18 = (bf16[256,256]{1,0:T(8,128)(2,1)S(1)}, bf16[256,256]{1,0:T(8,128)(2,1)S(1)}, u32[]{:S(2)}, u32[]{:S(2)}) collective-permute-start(bf16[256,256]{1,0:T(8,128)(2,1)S(1)} %get-tuple-element.37), channel_id=1, source_target_pairs={{0,8},{1,9},{2,10},{3,11},{4,12},{5,13},{6,14},{7,15},{8,0},{9,1},... | collective-permute-start | bytes 393224 | tf_op jit(solution)/shard_map/ppermute | solution.py:279
  103.2 1.5 %collective-permute-start.19 = (bf16[256,256]{1,0:T(8,128)(2,1)S(1)}, bf16[256,256]{1,0:T(8,128)(2,1)S(1)}, u32[]{:S(2)}, u32[]{:S(2)}) collective-permute-start(bf16[256,256]{1,0:T(8,128)(2,1)S(1)} %get-tuple-element.38), channel_id=1, source_target_pairs={{0,12},{1,13},{2,14},{3,15},{4,0},{5,1},{6,2},{7,3},{8,4},{9,5},{1... | collective-permute-start | bytes 393224 | tf_op jit(solution)/shard_map/ppermute | solution.py:279
  104.8 2.3 %collective-permute-done.17.refs_5_ = bf16[256,256]{1,0:T(8,128)(2,1)S(1)} collective-permute-done((bf16[256,256]{1,0:T(8,128)(2,1)S(1)}, bf16[256,256]{1,0:T(8,128)(2,1)S(1)}, u32[]{:S(2)}, u32[]{:S(2)}) %collective-permute-start.17) | collective-permute-done | bytes 131104 | tf_op jit(solution)/shard_map/ppermute | solution.py:279
  107.0 1.6 %collective-permute-done.18.refs_6_ = bf16[256,256]{1,0:T(8,128)(2,1)S(1)} collective-permute-done((bf16[256,256]{1,0:T(8,128)(2,1)S(1)}, bf16[256,256]{1,0:T(8,128)(2,1)S(1)}, u32[]{:S(2)}, u32[]{:S(2)}) %collective-permute-start.18) | collective-permute-done | bytes 131104 | tf_op jit(solution)/shard_map/ppermute | solution.py:279
  108.7 1.2 %weight_total.1 = f32[512,2,128]{2,1,0:T(2,128)} custom-call(f32[256,256]{1,0:T(8,128)S(1)} %get-tuple-element.30.refs_0_, bf16[256,256]{1,0:T(8,128)(2,1)S(1)} %collective-permute-done.11.refs_1_, bf16[256,256]{1,0:T(8,128)(2,1)S(1)} %collective-permute-done.12.refs_2_, bf16[256,256]{1,0:T(8,128)(2,1)S(1)} %collective-permute-done.13.refs_3_, ...), custom_call_target="tpu_custom_call" | custom-call | tf_op jit(solution)/shard_map/weight_total/pallas_call | solution.py:432
  (31 shorter events, 2.8 us)
Async XLA Ops:
  2.1 15.5 %all-to-all-start = ((s32[16,1,128]{2,1,0:T(1,128)}), s32[16,1,128]{2,1,0:T(1,128)S(1)}, u32[]{:S(2)}, u32[]{:S(2)}) async-start(s32[16,1,128]{2,1,0:T(1,128)} %bitcast.32), calls=%async_computation | async-start | bytes 16384 | tf_op jit(solution)/shard_map/all_to_all | solution.py:325
  19.5 23.6 %all-to-all-start.1 = ((bf16[16,2,64,256]{3,2,1,0:T(8,128)(2,1)}), bf16[16,2,64,256]{3,2,1,0:T(8,128)(2,1)S(1)}, u32[]{:S(2)}, u32[]{:S(2)}) async-start(bf16[16,2,64,256]{3,2,1,0:T(8,128)(2,1)} %bitcast.6), calls=%async_computation.1 | async-start | bytes 2097152 | tf_op jit(solution)/shard_map/all_to_all | solution.py:341
  26.3 16.8 %copy-start.1 = (s32[12]{0:T(128)S(1)}, s32[12]{0:T(128)}, u32[]{:S(2)}) copy-start(s32[12]{0:T(128)} %lengths.1) | copy-start | bytes 148
  26.3 16.8 %copy-start.2 = (s32[48]{0:T(128)S(1)}, s32[48]{0:T(128)}, u32[]{:S(2)}) copy-start(s32[48]{0:T(128)} %get-tuple-element.21.meta) | copy-start | bytes 580
  30.2 31.8 %collective-permute-start.6 = (bf16[512,1024]{1,0:T(8,128)(2,1)}, bf16[512,1024]{1,0:T(8,128)(2,1)S(1)}, u32[]{:S(2)}, u32[]{:S(2)}) collective-permute-start(bf16[512,1024]{1,0:T(8,128)(2,1)} %get-tuple-element.28), channel_id=1, source_target_pairs={{0,12},{1,13},{2,14},{3,15},{4,0},{5,1},{6,2},{7,3},{8,4},{9,5},{1... | collective-permute-start | bytes 3145736 | tf_op jit(solution)/shard_map/ppermute | solution.py:290
  33.3 28.7 %collective-permute-start.3 = (bf16[512,1024]{1,0:T(8,128)(2,1)}, bf16[512,1024]{1,0:T(8,128)(2,1)S(1)}, u32[]{:S(2)}, u32[]{:S(2)}) collective-permute-start(bf16[512,1024]{1,0:T(8,128)(2,1)} %get-tuple-element.26), channel_id=1, source_target_pairs={{0,4},{1,5},{2,6},{3,7},{4,8},{5,9},{6,10},{7,11},{8,12},{9,13},{1... | collective-permute-start | bytes 3145736 | tf_op jit(solution)/shard_map/ppermute | solution.py:290
  33.3 27.0 %collective-permute-start.4 = (bf16[256,1024]{1,0:T(8,128)(2,1)}, bf16[256,1024]{1,0:T(8,128)(2,1)}, u32[]{:S(2)}, u32[]{:S(2)}) collective-permute-start(bf16[256,1024]{1,0:T(8,128)(2,1)} %get-tuple-element.27), channel_id=1, source_target_pairs={{0,8},{1,9},{2,10},{3,11},{4,12},{5,13},{6,14},{7,15},{8,0},{9,1},... | collective-permute-start | bytes 1572872 | tf_op jit(solution)/shard_map/ppermute | solution.py:290
  55.6 1.0 copy-start
  56.6 18.8 %all-to-all-start.2 = ((bf16[16,2,64,256]{3,2,1,0:T(8,128)(2,1)}), bf16[16,2,64,256]{3,2,1,0:T(8,128)(2,1)S(1)}, u32[]{:S(2)}, u32[]{:S(2)}) async-start(bf16[16,2,64,256]{3,2,1,0:T(8,128)(2,1)} %bitcast.24), calls=%async_computation.2 | async-start | bytes 2097152 | tf_op jit(solution)/shard_map/all_to_all | solution.py:385
  60.3 12.3 %collective-permute-start.5 = (bf16[256,1024]{1,0:T(8,128)(2,1)}, bf16[256,1024]{1,0:T(8,128)(2,1)}, u32[]{:S(2)}, u32[]{:S(2)}) collective-permute-start(bf16[256,1024]{1,0:T(8,128)(2,1)} %collective-permute-done.4.rest_1_), channel_id=1, source_target_pairs={{0,32},{16,48},{32,0},{48,16},{64,96},{80,112},{96,64},{112,80},{1... | collective-permute-start | bytes 1572872 | tf_op jit(solution)/shard_map/ppermute | solution.py:294
  62.0 18.5 %collective-permute-start.10 = (bf16[512,1024]{1,0:T(8,128)(2,1)S(1)}, bf16[512,1024]{1,0:T(8,128)(2,1)}, u32[]{:S(2)}, u32[]{:S(2)}) collective-permute-start(bf16[512,1024]{1,0:T(8,128)(2,1)S(1)} %collective-permute-done.6.rest_3_), channel_id=1, source_target_pairs={{0,16},{16,0},{32,48},{48,32},{64,80},{80,64},{96,112},{112,96},{1... | collective-permute-start | bytes 3145736 | tf_op jit(solution)/shard_map/ppermute | solution.py:294
  62.0 18.8 %collective-permute-start.7 = (bf16[512,1024]{1,0:T(8,128)(2,1)S(1)}, bf16[512,1024]{1,0:T(8,128)(2,1)}, u32[]{:S(2)}, u32[]{:S(2)}) collective-permute-start(bf16[512,1024]{1,0:T(8,128)(2,1)S(1)} %collective-permute-done.3.rest_0_), channel_id=1, source_target_pairs={{0,16},{16,0},{32,48},{48,32},{64,80},{80,64},{96,112},{112,96},{1... | collective-permute-start | bytes 3145736 | tf_op jit(solution)/shard_map/ppermute | solution.py:294
  62.5 14.2 %collective-permute-start.8 = (bf16[256,1024]{1,0:T(8,128)(2,1)}, bf16[256,1024]{1,0:T(8,128)(2,1)}, u32[]{:S(2)}, u32[]{:S(2)}) collective-permute-start(bf16[256,1024]{1,0:T(8,128)(2,1)} %collective-permute-done.4.rest_1_), channel_id=1, source_target_pairs={{0,16},{16,0},{32,48},{48,32},{64,80},{80,64},{96,112},{112,96},{1... | collective-permute-start | bytes 1572872 | tf_op jit(solution)/shard_map/ppermute | solution.py:294
  72.6 6.7 %collective-permute-start.9 = (bf16[256,1024]{1,0:T(8,128)(2,1)}, bf16[256,1024]{1,0:T(8,128)(2,1)}, u32[]{:S(2)}, u32[]{:S(2)}) collective-permute-start(bf16[256,1024]{1,0:T(8,128)(2,1)} %collective-permute-done.5.rest_2_), channel_id=1, source_target_pairs={{0,16},{16,0},{32,48},{48,32},{64,80},{80,64},{96,112},{112,96},{1... | collective-permute-start | bytes 1572872 | tf_op jit(solution)/shard_map/ppermute | solution.py:294
  76.7 10.2 %collective-permute-start = (bf16[256,512]{1,0:T(8,128)(2,1)S(1)}, bf16[256,512]{1,0:T(8,128)(2,1)S(1)}, u32[]{:S(2)}, u32[]{:S(2)}) collective-permute-start(bf16[256,512]{1,0:T(8,128)(2,1)S(1)} %image_grads.1.grad_low.refs_0_), channel_id=1, source_target_pairs={{0,4},{1,5},{2,6},{3,7},{4,8},{5,9},{6,10},{7,11},{8,12},{9,13},{1... | collective-permute-start | bytes 786440 | tf_op jit(solution)/shard_map/ppermute | solution.py:279
  76.8 13.2 %collective-permute-start.1 = (bf16[256,512]{1,0:T(8,128)(2,1)S(1)}, bf16[256,512]{1,0:T(8,128)(2,1)S(1)}, u32[]{:S(2)}, u32[]{:S(2)}) collective-permute-start(bf16[256,512]{1,0:T(8,128)(2,1)S(1)} %image_grads.1.grad_low.refs_0_), channel_id=1, source_target_pairs={{0,8},{1,9},{2,10},{3,11},{4,12},{5,13},{6,14},{7,15},{8,0},{9,1},... | collective-permute-start | bytes 786440 | tf_op jit(solution)/shard_map/ppermute | solution.py:279
  79.4 10.7 %collective-permute-start.2 = (bf16[256,512]{1,0:T(8,128)(2,1)S(1)}, bf16[256,512]{1,0:T(8,128)(2,1)S(1)}, u32[]{:S(2)}, u32[]{:S(2)}) collective-permute-start(bf16[256,512]{1,0:T(8,128)(2,1)S(1)} %image_grads.1.grad_low.refs_0_), channel_id=1, source_target_pairs={{0,12},{1,13},{2,14},{3,15},{4,0},{5,1},{6,2},{7,3},{8,4},{9,5},{1... | collective-permute-start | bytes 786440 | tf_op jit(solution)/shard_map/ppermute | solution.py:279
  80.5 15.6 %collective-permute-start.14 = (bf16[256,512]{1,0:T(8,128)(2,1)S(1)}, bf16[256,512]{1,0:T(8,128)(2,1)S(1)}, u32[]{:S(2)}, u32[]{:S(2)}) collective-permute-start(bf16[256,512]{1,0:T(8,128)(2,1)S(1)} %image_grads.1.grad_low.refs_0_), channel_id=1, source_target_pairs={{0,1},{1,2},{2,3},{3,0},{4,5},{5,6},{6,7},{7,4},{8,9},{9,10},{10,1... | collective-permute-start | bytes 786440 | tf_op jit(solution)/shard_map/ppermute | solution.py:279
  80.8 16.8 %collective-permute-start.15 = (bf16[256,512]{1,0:T(8,128)(2,1)S(1)}, bf16[256,512]{1,0:T(8,128)(2,1)S(1)}, u32[]{:S(2)}, u32[]{:S(2)}) collective-permute-start(bf16[256,512]{1,0:T(8,128)(2,1)S(1)} %image_grads.1.grad_low.refs_0_), channel_id=1, source_target_pairs={{0,2},{1,3},{2,0},{3,1},{4,6},{5,7},{6,4},{7,5},{8,10},{9,11},{10,... | collective-permute-start | bytes 786440 | tf_op jit(solution)/shard_map/ppermute | solution.py:279
  86.9 10.6 %collective-permute-start.16 = (bf16[256,512]{1,0:T(8,128)(2,1)S(1)}, bf16[256,512]{1,0:T(8,128)(2,1)S(1)}, u32[]{:S(2)}, u32[]{:S(2)}) collective-permute-start(bf16[256,512]{1,0:T(8,128)(2,1)S(1)} %get-tuple-element.34), channel_id=1, source_target_pairs={{0,3},{1,0},{2,1},{3,2},{4,7},{5,4},{6,5},{7,6},{8,11},{9,8},{10,9... | collective-permute-start | bytes 786440 | tf_op jit(solution)/shard_map/ppermute | solution.py:279
  91.9 11.4 %collective-permute-start.11 = (bf16[256,256]{1,0:T(8,128)(2,1)S(1)}, bf16[256,256]{1,0:T(8,128)(2,1)S(1)}, u32[]{:S(2)}, u32[]{:S(2)}) collective-permute-start(bf16[256,256]{1,0:T(8,128)(2,1)S(1)} %get-tuple-element.31), channel_id=1, source_target_pairs={{0,1},{1,2},{2,3},{3,0},{4,5},{5,6},{6,7},{7,4},{8,9},{9,10},{10,1... | collective-permute-start | bytes 393224 | tf_op jit(solution)/shard_map/ppermute | solution.py:279
  93.4 11.4 %collective-permute-start.12 = (bf16[256,256]{1,0:T(8,128)(2,1)S(1)}, bf16[256,256]{1,0:T(8,128)(2,1)S(1)}, u32[]{:S(2)}, u32[]{:S(2)}) collective-permute-start(bf16[256,256]{1,0:T(8,128)(2,1)S(1)} %get-tuple-element.32), channel_id=1, source_target_pairs={{0,2},{1,3},{2,0},{3,1},{4,6},{5,7},{6,4},{7,5},{8,10},{9,11},{10,... | collective-permute-start | bytes 393224 | tf_op jit(solution)/shard_map/ppermute | solution.py:279
  96.0 8.7 %collective-permute-start.13 = (bf16[256,256]{1,0:T(8,128)(2,1)S(1)}, bf16[256,256]{1,0:T(8,128)(2,1)S(1)}, u32[]{:S(2)}, u32[]{:S(2)}) collective-permute-start(bf16[256,256]{1,0:T(8,128)(2,1)S(1)} %get-tuple-element.33), channel_id=1, source_target_pairs={{0,3},{1,0},{2,1},{3,2},{4,7},{5,4},{6,5},{7,6},{8,11},{9,8},{10,9... | collective-permute-start | bytes 393224 | tf_op jit(solution)/shard_map/ppermute | solution.py:279
  99.4 7.7 %collective-permute-start.17 = (bf16[256,256]{1,0:T(8,128)(2,1)S(1)}, bf16[256,256]{1,0:T(8,128)(2,1)S(1)}, u32[]{:S(2)}, u32[]{:S(2)}) collective-permute-start(bf16[256,256]{1,0:T(8,128)(2,1)S(1)} %get-tuple-element.36), channel_id=1, source_target_pairs={{0,4},{1,5},{2,6},{3,7},{4,8},{5,9},{6,10},{7,11},{8,12},{9,13},{1... | collective-permute-start | bytes 393224 | tf_op jit(solution)/shard_map/ppermute | solution.py:279
  100.9 7.7 %collective-permute-start.18 = (bf16[256,256]{1,0:T(8,128)(2,1)S(1)}, bf16[256,256]{1,0:T(8,128)(2,1)S(1)}, u32[]{:S(2)}, u32[]{:S(2)}) collective-permute-start(bf16[256,256]{1,0:T(8,128)(2,1)S(1)} %get-tuple-element.37), channel_id=1, source_target_pairs={{0,8},{1,9},{2,10},{3,11},{4,12},{5,13},{6,14},{7,15},{8,0},{9,1},... | collective-permute-start | bytes 393224 | tf_op jit(solution)/shard_map/ppermute | solution.py:279
  103.2 5.4 %collective-permute-start.19 = (bf16[256,256]{1,0:T(8,128)(2,1)S(1)}, bf16[256,256]{1,0:T(8,128)(2,1)S(1)}, u32[]{:S(2)}, u32[]{:S(2)}) collective-permute-start(bf16[256,256]{1,0:T(8,128)(2,1)S(1)} %get-tuple-element.38), channel_id=1, source_target_pairs={{0,12},{1,13},{2,14},{3,15},{4,0},{5,1},{6,2},{7,3},{8,4},{9,5},{1... | collective-permute-start | bytes 393224 | tf_op jit(solution)/shard_map/ppermute | solution.py:279

commit v5 on v4

--- a/solution.py
+++ b/solution.py
@@ -40,19 +40,14 @@
     table[...] = value
 
 
-def fill_kernel(table, pairs, slots, sems):
-    copies = []
+def fill_kernel(table, pairs, slots):
     for slot in range(slots.shape[0]):
         image = jnp.maximum(table[slot // CAP, slot % CAP] - 1, 0)
-        copies.append(pltpu.make_async_copy(pairs.at[image], slots.at[slot], sems.at[slot]))
-    for copy in copies:
-        copy.start()
-    for copy in copies:
-        copy.wait()
+        slots[slot] = pairs[image]
 
 
 def attend_kernel(meta, table, lengths, queries, grads, slots, attn, query_grad, slot_grad, *scratch, img_dev):
-    q_all, g_all, out_all, dq_all, pair_grad, sems, pair_sems = scratch
+    q_all, g_all, out_all, dq_all, sems = scratch
     seq_dev = lengths.shape[0]
     seq_len = queries.shape[0] // seq_dev
     groups = queries.shape[1] // HD
@@ -74,12 +69,6 @@
             )
             for kind in kinds
         ]
-
-    def pair_copy(seq, pick):
-        at = 2 * seq + pick
-        return pltpu.make_async_copy(
-            pair_grad.at[at], slot_grad.at[meta[at]], pair_sems.at[at]
-        )
 
     def begin(seq):
         for copy in copies(seq, (0, 1)):
@@ -112,10 +101,10 @@
             axis=0,
         )
         wide = lax.dot_general(key_val, both, (((1,), (1,)), ((), ())), preferred_element_type=F32)
-        return val_key, both, wide[: 2 * keys_img] + bias, wide[2 * keys_img :]
+        return slot_ids, val_key, both, wide[: 2 * keys_img] + bias, wide[2 * keys_img :]
 
     def finish(seq, state):
-        val_key, both, scores, grad_probs = state
+        slot_ids, val_key, both, scores, grad_probs = state
         token = lax.broadcasted_iota(jnp.int32, (1, groups * seq_len), 1)
         live = token % seq_len < lengths[seq]
         top = jnp.max(scores, axis=0, keepdims=True)
@@ -138,8 +127,7 @@
         key_grad = (back[2 * keys_img :, :HD] * inv_root).astype(BF16)
         for pick in range(2):
             part = slice(pick * keys_img, (pick + 1) * keys_img)
-            pair_grad[2 * seq + pick] = jnp.concatenate([key_grad[part], val_grad[part]], axis=1)
-            pair_copy(seq, pick).start()
+            slot_grad[slot_ids[pick]] = jnp.concatenate([key_grad[part], val_grad[part]], axis=1)
 
     for seq in range(seq_dev):
         for copy in copies(seq, (0, 1)):
@@ -157,8 +145,6 @@
     for seq in range(seq_dev):
         for copy in copies(seq, (2, 3)):
             copy.wait()
-        for pick in range(2):
-            pair_copy(seq, pick).wait()
 
 
 def pack_kernel(place, after, features, *rest):
@@ -333,8 +319,7 @@
         fill_kernel,
         out_shape=jax.ShapeDtypeStruct((slot_total, keys_img, cols), BF16),
         in_specs=[scalars, whole],
-        out_specs=in_hbm,
-        scratch_shapes=[pltpu.SemaphoreType.DMA((slot_total,))],
+        out_specs=whole,
         compiler_params=params(8),
         name="fill_slots",
     )(table, own_pairs.reshape(img_dev, keys_img, cols))
@@ -372,13 +357,9 @@
             jax.ShapeDtypeStruct((slot_total, keys_img, cols), BF16),
         ],
         in_specs=[scalars, scalars, scalars, in_hbm, in_hbm, whole],
-        out_specs=[in_hbm] * 3,
+        out_specs=[in_hbm, in_hbm, whole],
         scratch_shapes=[pltpu.VMEM(queries.shape, BF16)] * 4
-        + [
-            pltpu.VMEM((request_total, keys_img, cols), BF16),
-            pltpu.SemaphoreType.DMA((4, seq_dev)),
-            pltpu.SemaphoreType.DMA((request_total,)),
-        ],
+        + [pltpu.SemaphoreType.DMA((4, seq_dev))],
         compiler_params=params(24),
         name="attend",
     )(meta, table, text_len, *[pltpu.with_memory_space_constraint(x, pltpu.HBM) for x in (queries, out_grad)], got_pairs)

time: 110 us -> 109 us (level)
  starting transfers between devices: 45.2 us -> 43 us
  waiting for transfers between devices: 26.5 us -> 28.7 us
  Pallas kernels: 29.3 us -> 27.7 us
    ppermute x12, starting transfers between devices: 19.2 us -> 16.9 us  [shift(): return lax.ppermute(values, 'txt', pairs)]
    ppermute x12, waiting for transfers between devices: 5.54 us -> 7.79 us  [shift(): return lax.ppermute(values, 'txt', pairs)]
    pallas_call x1, Pallas kernels: 12.5 us -> 11 us  [shards(): pl.pallas_call(functools.partial(attend_kernel, img_dev=img_dev), out_sha...]
    all_to_all x1, waiting for transfers between devices: 2.83 us -> 1.32 us  [shards(): lax.all_to_all(slot_grad.reshape(txt_count, CAP, keys_img, cols), 'txt',...]
    ppermute x5, waiting for transfers between devices: 10.1 us -> 11.6 us  [swap_img(): lax.ppermute(values, 'img', [(i, i ^ bit) for i in range(lax.axis_size('i...]
  transfers between devices with their start and end apart: 23 -> 23, of which waited for: 9 -> 8; matrix products, arithmetic and copies ran while one was open for 6% -> 6% of each run, Pallas kernels for 23% -> 22%
where the time goes in v5:
time: 109 us; the launch traced here: 108 us
  starting transfers between devices  43 us (39%)
  waiting for transfers between devices  28.7 us (26%)
  Pallas kernels  27.7 us (25%)
  matrix products  6.91 us (6%)
    ppermute x12, starting transfers between devices, shift(): return lax.ppermute(values, 'txt', pairs)  16.9 us
    ppermute x5, waiting for transfers between devices, swap_img(): lax.ppermute(values, 'img', [(i, i ^ bit) for i in range(lax.axis_size('i...  11.6 us
    pallas_call x1, Pallas kernels, shards(): pl.pallas_call(functools.partial(attend_kernel, img_dev=img_dev), out_sha...  11 us
    all_to_all x1, starting transfers between devices, shards(): table = lax.all_to_all(wanted, 'txt', 0, 0, tiled=True)  7.97 us
    ppermute x12, waiting for transfers between devices, shift(): return lax.ppermute(values, 'txt', pairs)  7.79 us
    all_to_all x1, waiting for transfers between devices, shards(): lax.all_to_all(sent_pairs.reshape(txt_count, CAP, keys_img, cols), 'txt',...  7.47 us
    dot_general x1, matrix products, shards(): jnp.dot(flat_features, kv_weight.reshape(feat_width, cols), preferred_ele...  6.91 us
    all_to_all x1, starting transfers between devices, shards(): lax.all_to_all(sent_pairs.reshape(txt_count, CAP, keys_img, cols), 'txt',...  6.66 us
  transfers between devices with their start and end apart: 23, of which 8 were waited for; matrix products, arithmetic and copies ran while one was open for 6% of the time, Pallas kernels for 22%

profile of v5, /device:TPU:0, one launch (start us, length us, event | category | flops | bytes accessed | tf_op | source)
XLA Modules:
  0.0 108.1 jit_solution(1837320832663767482)
XLA Ops:
  0.6 1.5 %request_table.1 = (s32[16,128]{1,0:T(8,128)}, s32[48]{0:T(128)}) custom-call(s32[2,12]{1,0:T(2,128)} %bitcast.34, s32[8]{0:T(128)} %counts.1), custom_call_target="tpu_custom_call" | custom-call | tf_op jit(solution)/shard_map/request_table/pallas_call | solution.py:300
  2.1 8.0 %all-to-all-start = ((s32[16,1,128]{2,1,0:T(1,128)}), s32[16,1,128]{2,1,0:T(1,128)S(1)}, u32[]{:S(2)}, u32[]{:S(2)}) async-start(s32[16,1,128]{2,1,0:T(1,128)} %bitcast.32), calls=%async_computation | async-start | bytes 16384 | tf_op jit(solution)/shard_map/all_to_all | solution.py:311
  10.1 6.9 %fusion.3 = bf16[512,256]{1,0:T(8,128)(2,1)S(1)} fusion(bf16[512,8192]{1,0:T(8,128)(2,1)} %bitcast.29, bf16[1024,8,2,128]{3,2,1,0:T(2,128)(2,1)} %bitcast.33), kind=kOutput, calls=%fused_computation.3 | convolution fusion | flops 2147614720 | bytes 12845056 | tf_op jit(solution)/shard_map/dot_general | solution.py:315
  17.6 1.7 %fill_slots.1.after = bf16[32,64,256]{2,1,0:T(8,128)(2,1)} custom-call(s32[16,128]{1,0:T(8,128)S(1)} %bitcast.26, bf16[8,64,256]{2,1,0:T(8,128)(2,1)S(1)} %bitcast.25), custom_call_target="tpu_custom_call" | custom-call | tf_op jit(solution)/shard_map/fill_slots/pallas_call | solution.py:318
  19.3 6.7 %all-to-all-start.1 = ((bf16[16,2,64,256]{3,2,1,0:T(8,128)(2,1)}), bf16[16,2,64,256]{3,2,1,0:T(8,128)(2,1)S(1)}, u32[]{:S(2)}, u32[]{:S(2)}) async-start(bf16[16,2,64,256]{3,2,1,0:T(8,128)(2,1)} %bitcast.6), calls=%async_computation.1 | async-start | bytes 2097152 | tf_op jit(solution)/shard_map/all_to_all | solution.py:326
  26.1 3.8 %pack_features.1 = (bf16[512,1024]{1,0:T(8,128)(2,1)}, bf16[256,1024]{1,0:T(8,128)(2,1)}, bf16[512,1024]{1,0:T(8,128)(2,1)}) custom-call(s32[4]{0:T(128)S(1)} %pad_add_fusion.place, bf16[32,64,256]{2,1,0:T(8,128)(2,1)} %fill_slots.1.after, bf16[512,8192]{1,0:T(8,128)(2,1)} %bitcast.30), custom_call_target="tpu_custom_call" | custom-call | bytes 8388608 | tf_op jit(solution)/shard_map/pack_features/pallas_call | solution.py:334
  30.0 3.2 %collective-permute-start.6 = (bf16[512,1024]{1,0:T(8,128)(2,1)}, bf16[512,1024]{1,0:T(8,128)(2,1)S(1)}, u32[]{:S(2)}, u32[]{:S(2)}) collective-permute-start(bf16[512,1024]{1,0:T(8,128)(2,1)} %get-tuple-element.28), channel_id=1, source_target_pairs={{0,12},{1,13},{2,14},{3,15},{4,0},{5,1},{6,2},{7,3},{8,4},{9,5},{1... | collective-permute-start | bytes 3145736 | tf_op jit(solution)/shard_map/ppermute | solution.py:276
  33.1 2.3 %collective-permute-start.4 = (bf16[256,1024]{1,0:T(8,128)(2,1)}, bf16[256,1024]{1,0:T(8,128)(2,1)}, u32[]{:S(2)}, u32[]{:S(2)}) collective-permute-start(bf16[256,1024]{1,0:T(8,128)(2,1)} %get-tuple-element.27), channel_id=1, source_target_pairs={{0,8},{1,9},{2,10},{3,11},{4,12},{5,13},{6,14},{7,15},{8,0},{9,1},... | collective-permute-start | bytes 1572872 | tf_op jit(solution)/shard_map/ppermute | solution.py:276
  35.4 7.5 %all-to-all-done.1 = bf16[16,2,64,256]{3,2,1,0:T(8,128)(2,1)S(1)} async-done(((bf16[16,2,64,256]{3,2,1,0:T(8,128)(2,1)}), bf16[16,2,64,256]{3,2,1,0:T(8,128)(2,1)S(1)}, u32[]{:S(2)}, u32[]{:S(2)}) %all-to-all-start.1) | async-done | bytes 1048608 | tf_op jit(solution)/shard_map/all_to_all | solution.py:326
  42.9 11.0 %attend.1 = (bf16[1536,1024]{1,0:T(8,128)(2,1)}, bf16[1536,1024]{1,0:T(8,128)(2,1)}, bf16[32,64,256]{2,1,0:T(8,128)(2,1)S(1)}) custom-call(s32[48]{0:T(128)S(1)} %copy-done.2, s32[16,128]{1,0:T(8,128)S(1)} %bitcast.27, s32[12]{0:T(128)S(1)} %copy-done.1, bf16[1536,1024]{1,0:T(8,128)(2,1)} %queries.1, bf16[1536,1024]{1,0:T(8,128)(2,1)} %grads.1, ...), custom_call_target="tpu_custom_call" | custom-call | tf_op jit(solution)/shard_map/attend/pallas_call | solution.py:352
  53.9 1.0 copy-done
  54.9 3.7 %all-to-all-start.2 = ((bf16[16,2,64,256]{3,2,1,0:T(8,128)(2,1)}), bf16[16,2,64,256]{3,2,1,0:T(8,128)(2,1)S(1)}, u32[]{:S(2)}, u32[]{:S(2)}) async-start(bf16[16,2,64,256]{3,2,1,0:T(8,128)(2,1)} %bitcast.24), calls=%async_computation.2 | async-start | bytes 2097152 | tf_op jit(solution)/shard_map/all_to_all | solution.py:366
  58.6 1.7 %collective-permute-start.5 = (bf16[256,1024]{1,0:T(8,128)(2,1)}, bf16[256,1024]{1,0:T(8,128)(2,1)}, u32[]{:S(2)}, u32[]{:S(2)}) collective-permute-start(bf16[256,1024]{1,0:T(8,128)(2,1)} %collective-permute-done.4.rest_1_), channel_id=1, source_target_pairs={{0,32},{16,48},{32,0},{48,16},{64,96},{80,112},{96,64},{112,80},{1... | collective-permute-start | bytes 1572872 | tf_op jit(solution)/shard_map/ppermute | solution.py:280
  60.9 11.5 %collective-permute-done.5.rest_2_ = bf16[256,1024]{1,0:T(8,128)(2,1)} collective-permute-done((bf16[256,1024]{1,0:T(8,128)(2,1)}, bf16[256,1024]{1,0:T(8,128)(2,1)}, u32[]{:S(2)}, u32[]{:S(2)}) %collective-permute-start.5) | collective-permute-done | bytes 524320 | tf_op jit(solution)/shard_map/ppermute | solution.py:280
  72.4 1.3 %all-to-all-done.2 = bf16[16,2,64,256]{3,2,1,0:T(8,128)(2,1)S(1)} async-done(((bf16[16,2,64,256]{3,2,1,0:T(8,128)(2,1)}), bf16[16,2,64,256]{3,2,1,0:T(8,128)(2,1)S(1)}, u32[]{:S(2)}, u32[]{:S(2)}) %all-to-all-start.2) | async-done | bytes 1048608 | tf_op jit(solution)/shard_map/all_to_all | solution.py:366
  73.8 1.2 %image_grads.1.grad_low.refs_0_ = bf16[256,512]{1,0:T(8,128)(2,1)S(1)} custom-call(s32[16,128]{1,0:T(8,128)S(1)} %bitcast.28, bf16[32,64,256]{2,1,0:T(8,128)(2,1)S(1)} %bitcast.23), custom_call_target="tpu_custom_call" | custom-call | tf_op jit(solution)/shard_map/image_grads/pallas_call | solution.py:370
  75.0 2.6 %collective-permute-start.1 = (bf16[256,512]{1,0:T(8,128)(2,1)S(1)}, bf16[256,512]{1,0:T(8,128)(2,1)S(1)}, u32[]{:S(2)}, u32[]{:S(2)}) collective-permute-start(bf16[256,512]{1,0:T(8,128)(2,1)S(1)} %image_grads.1.grad_low.refs_0_), channel_id=1, source_target_pairs={{0,8},{1,9},{2,10},{3,11},{4,12},{5,13},{6,14},{7,15},{8,0},{9,1},... | collective-permute-start | bytes 786440 | tf_op jit(solution)/shard_map/ppermute | solution.py:265
  77.7 1.1 collective-permute-start.2
  79.0 2.5 %collective-permute-start.15 = (bf16[256,512]{1,0:T(8,128)(2,1)S(1)}, bf16[256,512]{1,0:T(8,128)(2,1)S(1)}, u32[]{:S(2)}, u32[]{:S(2)}) collective-permute-start(bf16[256,512]{1,0:T(8,128)(2,1)S(1)} %image_grads.1.grad_low.refs_0_), channel_id=1, source_target_pairs={{0,2},{1,3},{2,0},{3,1},{4,6},{5,7},{6,4},{7,5},{8,10},{9,11},{10,... | collective-permute-start | bytes 786440 | tf_op jit(solution)/shard_map/ppermute | solution.py:265
  81.6 3.6 %near_features.1 = (bf16[256,512]{1,0:T(8,128)(2,1)S(1)}, bf16[2,4,512,1024]{3,2,1,0:T(8,128)(2,1)S(1)}) custom-call(s32[4]{0:T(128)S(1)} %pad_add_fusion.place, bf16[256,512]{1,0:T(8,128)(2,1)S(1)} %image_grads.1.grad_low.refs_0_, bf16[512,8192]{1,0:T(8,128)(2,1)} %bitcast.31, bf16[512,1024]{1,0:T(8,128)(2,1)S(1)} %collective-permute-done.3.rest_0_, ...), custom_call_target="tpu_custom_call" | custom-call | bytes 8388608 | tf_op jit(solution)/shard_map/near_features/pallas_call | solution.py:379
  85.2 4.0 %collective-permute-done.refs_1_ = bf16[256,512]{1,0:T(8,128)(2,1)S(1)} collective-permute-done((bf16[256,512]{1,0:T(8,128)(2,1)S(1)}, bf16[256,512]{1,0:T(8,128)(2,1)S(1)}, u32[]{:S(2)}, u32[]{:S(2)}) %collective-permute-start) | collective-permute-done | bytes 262176 | tf_op jit(solution)/shard_map/ppermute | solution.py:265
  89.9 1.8 %weight_part.2 = (f32[256,256]{1,0:T(8,128)S(1)}, bf16[256,256]{1,0:T(8,128)(2,1)S(1)}, bf16[256,256]{1,0:T(8,128)(2,1)S(1)}, bf16[256,256]{1,0:T(8,128)(2,1)S(1)}) custom-call(s32[4]{0:T(128)S(1)} %pad_add_fusion.place, bf16[256,512]{1,0:T(8,128)(2,1)S(1)} %image_grads.1.grad_low.refs_0_, bf16[256,512]{1,0:T(8,128)(2,1)S(1)} %collective-permute-done.refs_1_, ...), custom_call_target="tpu_custom_call" | custom-call | tf_op jit(solution)/shard_map/weight_part/pallas_call | solution.py:401
  91.7 1.5 %collective-permute-start.11 = (bf16[256,256]{1,0:T(8,128)(2,1)S(1)}, bf16[256,256]{1,0:T(8,128)(2,1)S(1)}, u32[]{:S(2)}, u32[]{:S(2)}) collective-permute-start(bf16[256,256]{1,0:T(8,128)(2,1)S(1)} %get-tuple-element.31), channel_id=1, source_target_pairs={{0,1},{1,2},{2,3},{3,0},{4,5},{5,6},{6,7},{7,4},{8,9},{9,10},{10,1... | collective-permute-start | bytes 393224 | tf_op jit(solution)/shard_map/ppermute | solution.py:265
  93.2 1.1 %collective-permute-start.12 = (bf16[256,256]{1,0:T(8,128)(2,1)S(1)}, bf16[256,256]{1,0:T(8,128)(2,1)S(1)}, u32[]{:S(2)}, u32[]{:S(2)}) collective-permute-start(bf16[256,256]{1,0:T(8,128)(2,1)S(1)} %get-tuple-element.32), channel_id=1, source_target_pairs={{0,2},{1,3},{2,0},{3,1},{4,6},{5,7},{6,4},{7,5},{8,10},{9,11},{10,... | collective-permute-start | bytes 393224 | tf_op jit(solution)/shard_map/ppermute | solution.py:265
  94.3 2.2 %collective-permute-start.13 = (bf16[256,256]{1,0:T(8,128)(2,1)S(1)}, bf16[256,256]{1,0:T(8,128)(2,1)S(1)}, u32[]{:S(2)}, u32[]{:S(2)}) collective-permute-start(bf16[256,256]{1,0:T(8,128)(2,1)S(1)} %get-tuple-element.33), channel_id=1, source_target_pairs={{0,3},{1,0},{2,1},{3,2},{4,7},{5,4},{6,5},{7,6},{8,11},{9,8},{10,9... | collective-permute-start | bytes 393224 | tf_op jit(solution)/shard_map/ppermute | solution.py:265
  96.6 1.8 %weight_part.3 = (f32[256,256]{1,0:T(8,128)S(1)}, bf16[256,256]{1,0:T(8,128)(2,1)S(1)}, bf16[256,256]{1,0:T(8,128)(2,1)S(1)}, bf16[256,256]{1,0:T(8,128)(2,1)S(1)}) custom-call(s32[4]{0:T(128)S(1)} %pad_add_fusion.place, bf16[256,512]{1,0:T(8,128)(2,1)S(1)} %image_grads.1.grad_low.refs_0_, bf16[256,512]{1,0:T(8,128)(2,1)S(1)} %collective-permute-done.14.refs_1_, ...), custom_call_target="tpu_custom_call" | custom-call | tf_op jit(solution)/shard_map/weight_part/pallas_call | solution.py:401
  98.4 0.7 collective-permute-start.17
  99.1 2.4 %collective-permute-start.18 = (bf16[256,256]{1,0:T(8,128)(2,1)S(1)}, bf16[256,256]{1,0:T(8,128)(2,1)S(1)}, u32[]{:S(2)}, u32[]{:S(2)}) collective-permute-start(bf16[256,256]{1,0:T(8,128)(2,1)S(1)} %get-tuple-element.37), channel_id=1, source_target_pairs={{0,8},{1,9},{2,10},{3,11},{4,12},{5,13},{6,14},{7,15},{8,0},{9,1},... | collective-permute-start | bytes 393224 | tf_op jit(solution)/shard_map/ppermute | solution.py:265
  101.5 2.3 %collective-permute-start.19 = (bf16[256,256]{1,0:T(8,128)(2,1)S(1)}, bf16[256,256]{1,0:T(8,128)(2,1)S(1)}, u32[]{:S(2)}, u32[]{:S(2)}) collective-permute-start(bf16[256,256]{1,0:T(8,128)(2,1)S(1)} %get-tuple-element.38), channel_id=1, source_target_pairs={{0,12},{1,13},{2,14},{3,15},{4,0},{5,1},{6,2},{7,3},{8,4},{9,5},{1... | collective-permute-start | bytes 393224 | tf_op jit(solution)/shard_map/ppermute | solution.py:265
  103.9 1.7 %collective-permute-done.17.refs_5_ = bf16[256,256]{1,0:T(8,128)(2,1)S(1)} collective-permute-done((bf16[256,256]{1,0:T(8,128)(2,1)S(1)}, bf16[256,256]{1,0:T(8,128)(2,1)S(1)}, u32[]{:S(2)}, u32[]{:S(2)}) %collective-permute-start.17) | collective-permute-done | bytes 131104 | tf_op jit(solution)/shard_map/ppermute | solution.py:265
  105.6 1.4 %collective-permute-done.18.refs_6_ = bf16[256,256]{1,0:T(8,128)(2,1)S(1)} collective-permute-done((bf16[256,256]{1,0:T(8,128)(2,1)S(1)}, bf16[256,256]{1,0:T(8,128)(2,1)S(1)}, u32[]{:S(2)}, u32[]{:S(2)}) %collective-permute-start.18) | collective-permute-done | bytes 131104 | tf_op jit(solution)/shard_map/ppermute | solution.py:265
  107.0 1.2 %weight_total.1 = f32[512,2,128]{2,1,0:T(2,128)} custom-call(f32[256,256]{1,0:T(8,128)S(1)} %get-tuple-element.30.refs_0_, bf16[256,256]{1,0:T(8,128)(2,1)S(1)} %collective-permute-done.11.refs_1_, bf16[256,256]{1,0:T(8,128)(2,1)S(1)} %collective-permute-done.12.refs_2_, bf16[256,256]{1,0:T(8,128)(2,1)S(1)} %collective-permute-done.13.refs_3_, ...), custom_call_target="tpu_custom_call" | custom-call | tf_op jit(solution)/shard_map/weight_total/pallas_call | solution.py:413
  (31 shorter events, 2.3 us)
Async XLA Ops:
  2.1 15.5 %all-to-all-start = ((s32[16,1,128]{2,1,0:T(1,128)}), s32[16,1,128]{2,1,0:T(1,128)S(1)}, u32[]{:S(2)}, u32[]{:S(2)}) async-start(s32[16,1,128]{2,1,0:T(1,128)} %bitcast.32), calls=%async_computation | async-start | bytes 16384 | tf_op jit(solution)/shard_map/all_to_all | solution.py:311
  19.3 23.6 %all-to-all-start.1 = ((bf16[16,2,64,256]{3,2,1,0:T(8,128)(2,1)}), bf16[16,2,64,256]{3,2,1,0:T(8,128)(2,1)S(1)}, u32[]{:S(2)}, u32[]{:S(2)}) async-start(bf16[16,2,64,256]{3,2,1,0:T(8,128)(2,1)} %bitcast.6), calls=%async_computation.1 | async-start | bytes 2097152 | tf_op jit(solution)/shard_map/all_to_all | solution.py:326
  26.1 16.8 %copy-start.1 = (s32[12]{0:T(128)S(1)}, s32[12]{0:T(128)}, u32[]{:S(2)}) copy-start(s32[12]{0:T(128)} %lengths.1) | copy-start | bytes 148
  26.1 16.8 %copy-start.2 = (s32[48]{0:T(128)S(1)}, s32[48]{0:T(128)}, u32[]{:S(2)}) copy-start(s32[48]{0:T(128)} %get-tuple-element.21.meta) | copy-start | bytes 580
  30.0 30.3 %collective-permute-start.6 = (bf16[512,1024]{1,0:T(8,128)(2,1)}, bf16[512,1024]{1,0:T(8,128)(2,1)S(1)}, u32[]{:S(2)}, u32[]{:S(2)}) collective-permute-start(bf16[512,1024]{1,0:T(8,128)(2,1)} %get-tuple-element.28), channel_id=1, source_target_pairs={{0,12},{1,13},{2,14},{3,15},{4,0},{5,1},{6,2},{7,3},{8,4},{9,5},{1... | collective-permute-start | bytes 3145736 | tf_op jit(solution)/shard_map/ppermute | solution.py:276
  33.1 27.2 %collective-permute-start.3 = (bf16[512,1024]{1,0:T(8,128)(2,1)}, bf16[512,1024]{1,0:T(8,128)(2,1)S(1)}, u32[]{:S(2)}, u32[]{:S(2)}) collective-permute-start(bf16[512,1024]{1,0:T(8,128)(2,1)} %get-tuple-element.26), channel_id=1, source_target_pairs={{0,4},{1,5},{2,6},{3,7},{4,8},{5,9},{6,10},{7,11},{8,12},{9,13},{1... | collective-permute-start | bytes 3145736 | tf_op jit(solution)/shard_map/ppermute | solution.py:276
  33.1 25.5 %collective-permute-start.4 = (bf16[256,1024]{1,0:T(8,128)(2,1)}, bf16[256,1024]{1,0:T(8,128)(2,1)}, u32[]{:S(2)}, u32[]{:S(2)}) collective-permute-start(bf16[256,1024]{1,0:T(8,128)(2,1)} %get-tuple-element.27), channel_id=1, source_target_pairs={{0,8},{1,9},{2,10},{3,11},{4,12},{5,13},{6,14},{7,15},{8,0},{9,1},... | collective-permute-start | bytes 1572872 | tf_op jit(solution)/shard_map/ppermute | solution.py:276
  53.9 1.0 copy-start
  54.9 18.9 %all-to-all-start.2 = ((bf16[16,2,64,256]{3,2,1,0:T(8,128)(2,1)}), bf16[16,2,64,256]{3,2,1,0:T(8,128)(2,1)S(1)}, u32[]{:S(2)}, u32[]{:S(2)}) async-start(bf16[16,2,64,256]{3,2,1,0:T(8,128)(2,1)} %bitcast.24), calls=%async_computation.2 | async-start | bytes 2097152 | tf_op jit(solution)/shard_map/all_to_all | solution.py:366
  58.6 13.8 %collective-permute-start.5 = (bf16[256,1024]{1,0:T(8,128)(2,1)}, bf16[256,1024]{1,0:T(8,128)(2,1)}, u32[]{:S(2)}, u32[]{:S(2)}) collective-permute-start(bf16[256,1024]{1,0:T(8,128)(2,1)} %collective-permute-done.4.rest_1_), channel_id=1, source_target_pairs={{0,32},{16,48},{32,0},{48,16},{64,96},{80,112},{96,64},{112,80},{1... | collective-permute-start | bytes 1572872 | tf_op jit(solution)/shard_map/ppermute | solution.py:280
  60.3 18.5 %collective-permute-start.10 = (bf16[512,1024]{1,0:T(8,128)(2,1)S(1)}, bf16[512,1024]{1,0:T(8,128)(2,1)}, u32[]{:S(2)}, u32[]{:S(2)}) collective-permute-start(bf16[512,1024]{1,0:T(8,128)(2,1)S(1)} %collective-permute-done.6.rest_3_), channel_id=1, source_target_pairs={{0,16},{16,0},{32,48},{48,32},{64,80},{80,64},{96,112},{112,96},{1... | collective-permute-start | bytes 3145736 | tf_op jit(solution)/shard_map/ppermute | solution.py:280
  60.3 18.7 %collective-permute-start.7 = (bf16[512,1024]{1,0:T(8,128)(2,1)S(1)}, bf16[512,1024]{1,0:T(8,128)(2,1)}, u32[]{:S(2)}, u32[]{:S(2)}) collective-permute-start(bf16[512,1024]{1,0:T(8,128)(2,1)S(1)} %collective-permute-done.3.rest_0_), channel_id=1, source_target_pairs={{0,16},{16,0},{32,48},{48,32},{64,80},{80,64},{96,112},{112,96},{1... | collective-permute-start | bytes 3145736 | tf_op jit(solution)/shard_map/ppermute | solution.py:280
  60.8 14.2 %collective-permute-start.8 = (bf16[256,1024]{1,0:T(8,128)(2,1)}, bf16[256,1024]{1,0:T(8,128)(2,1)}, u32[]{:S(2)}, u32[]{:S(2)}) collective-permute-start(bf16[256,1024]{1,0:T(8,128)(2,1)} %collective-permute-done.4.rest_1_), channel_id=1, source_target_pairs={{0,16},{16,0},{32,48},{48,32},{64,80},{80,64},{96,112},{112,96},{1... | collective-permute-start | bytes 1572872 | tf_op jit(solution)/shard_map/ppermute | solution.py:280
  72.4 5.3 %collective-permute-start.9 = (bf16[256,1024]{1,0:T(8,128)(2,1)}, bf16[256,1024]{1,0:T(8,128)(2,1)}, u32[]{:S(2)}, u32[]{:S(2)}) collective-permute-start(bf16[256,1024]{1,0:T(8,128)(2,1)} %collective-permute-done.5.rest_2_), channel_id=1, source_target_pairs={{0,16},{16,0},{32,48},{48,32},{64,80},{80,64},{96,112},{112,96},{1... | collective-permute-start | bytes 1572872 | tf_op jit(solution)/shard_map/ppermute | solution.py:280
  74.9 14.3 %collective-permute-start = (bf16[256,512]{1,0:T(8,128)(2,1)S(1)}, bf16[256,512]{1,0:T(8,128)(2,1)S(1)}, u32[]{:S(2)}, u32[]{:S(2)}) collective-permute-start(bf16[256,512]{1,0:T(8,128)(2,1)S(1)} %image_grads.1.grad_low.refs_0_), channel_id=1, source_target_pairs={{0,4},{1,5},{2,6},{3,7},{4,8},{5,9},{6,10},{7,11},{8,12},{9,13},{1... | collective-permute-start | bytes 786440 | tf_op jit(solution)/shard_map/ppermute | solution.py:265
  75.0 14.2 %collective-permute-start.1 = (bf16[256,512]{1,0:T(8,128)(2,1)S(1)}, bf16[256,512]{1,0:T(8,128)(2,1)S(1)}, u32[]{:S(2)}, u32[]{:S(2)}) collective-permute-start(bf16[256,512]{1,0:T(8,128)(2,1)S(1)} %image_grads.1.grad_low.refs_0_), channel_id=1, source_target_pairs={{0,8},{1,9},{2,10},{3,11},{4,12},{5,13},{6,14},{7,15},{8,0},{9,1},... | collective-permute-start | bytes 786440 | tf_op jit(solution)/shard_map/ppermute | solution.py:265
  77.7 12.2 %collective-permute-start.2 = (bf16[256,512]{1,0:T(8,128)(2,1)S(1)}, bf16[256,512]{1,0:T(8,128)(2,1)S(1)}, u32[]{:S(2)}, u32[]{:S(2)}) collective-permute-start(bf16[256,512]{1,0:T(8,128)(2,1)S(1)} %image_grads.1.grad_low.refs_0_), channel_id=1, source_target_pairs={{0,12},{1,13},{2,14},{3,15},{4,0},{5,1},{6,2},{7,3},{8,4},{9,5},{1... | collective-permute-start | bytes 786440 | tf_op jit(solution)/shard_map/ppermute | solution.py:265
  78.7 15.6 %collective-permute-start.14 = (bf16[256,512]{1,0:T(8,128)(2,1)S(1)}, bf16[256,512]{1,0:T(8,128)(2,1)S(1)}, u32[]{:S(2)}, u32[]{:S(2)}) collective-permute-start(bf16[256,512]{1,0:T(8,128)(2,1)S(1)} %image_grads.1.grad_low.refs_0_), channel_id=1, source_target_pairs={{0,1},{1,2},{2,3},{3,0},{4,5},{5,6},{6,7},{7,4},{8,9},{9,10},{10,1... | collective-permute-start | bytes 786440 | tf_op jit(solution)/shard_map/ppermute | solution.py:265
  79.0 17.5 %collective-permute-start.15 = (bf16[256,512]{1,0:T(8,128)(2,1)S(1)}, bf16[256,512]{1,0:T(8,128)(2,1)S(1)}, u32[]{:S(2)}, u32[]{:S(2)}) collective-permute-start(bf16[256,512]{1,0:T(8,128)(2,1)S(1)} %image_grads.1.grad_low.refs_0_), channel_id=1, source_target_pairs={{0,2},{1,3},{2,0},{3,1},{4,6},{5,7},{6,4},{7,5},{8,10},{9,11},{10,... | collective-permute-start | bytes 786440 | tf_op jit(solution)/shard_map/ppermute | solution.py:265
  89.2 7.3 %collective-permute-start.16 = (bf16[256,512]{1,0:T(8,128)(2,1)S(1)}, bf16[256,512]{1,0:T(8,128)(2,1)S(1)}, u32[]{:S(2)}, u32[]{:S(2)}) collective-permute-start(bf16[256,512]{1,0:T(8,128)(2,1)S(1)} %get-tuple-element.34), channel_id=1, source_target_pairs={{0,3},{1,0},{2,1},{3,2},{4,7},{5,4},{6,5},{7,6},{8,11},{9,8},{10,9... | collective-permute-start | bytes 786440 | tf_op jit(solution)/shard_map/ppermute | solution.py:265
  91.7 9.8 %collective-permute-start.11 = (bf16[256,256]{1,0:T(8,128)(2,1)S(1)}, bf16[256,256]{1,0:T(8,128)(2,1)S(1)}, u32[]{:S(2)}, u32[]{:S(2)}) collective-permute-start(bf16[256,256]{1,0:T(8,128)(2,1)S(1)} %get-tuple-element.31), channel_id=1, source_target_pairs={{0,1},{1,2},{2,3},{3,0},{4,5},{5,6},{6,7},{7,4},{8,9},{9,10},{10,1... | collective-permute-start | bytes 393224 | tf_op jit(solution)/shard_map/ppermute | solution.py:265
  93.2 10.7 %collective-permute-start.12 = (bf16[256,256]{1,0:T(8,128)(2,1)S(1)}, bf16[256,256]{1,0:T(8,128)(2,1)S(1)}, u32[]{:S(2)}, u32[]{:S(2)}) collective-permute-start(bf16[256,256]{1,0:T(8,128)(2,1)S(1)} %get-tuple-element.32), channel_id=1, source_target_pairs={{0,2},{1,3},{2,0},{3,1},{4,6},{5,7},{6,4},{7,5},{8,10},{9,11},{10,... | collective-permute-start | bytes 393224 | tf_op jit(solution)/shard_map/ppermute | solution.py:265
  94.3 9.5 %collective-permute-start.13 = (bf16[256,256]{1,0:T(8,128)(2,1)S(1)}, bf16[256,256]{1,0:T(8,128)(2,1)S(1)}, u32[]{:S(2)}, u32[]{:S(2)}) collective-permute-start(bf16[256,256]{1,0:T(8,128)(2,1)S(1)} %get-tuple-element.33), channel_id=1, source_target_pairs={{0,3},{1,0},{2,1},{3,2},{4,7},{5,4},{6,5},{7,6},{8,11},{9,8},{10,9... | collective-permute-start | bytes 393224 | tf_op jit(solution)/shard_map/ppermute | solution.py:265
  98.4 7.2 %collective-permute-start.17 = (bf16[256,256]{1,0:T(8,128)(2,1)S(1)}, bf16[256,256]{1,0:T(8,128)(2,1)S(1)}, u32[]{:S(2)}, u32[]{:S(2)}) collective-permute-start(bf16[256,256]{1,0:T(8,128)(2,1)S(1)} %get-tuple-element.36), channel_id=1, source_target_pairs={{0,4},{1,5},{2,6},{3,7},{4,8},{5,9},{6,10},{7,11},{8,12},{9,13},{1... | collective-permute-start | bytes 393224 | tf_op jit(solution)/shard_map/ppermute | solution.py:265
  99.1 7.8 %collective-permute-start.18 = (bf16[256,256]{1,0:T(8,128)(2,1)S(1)}, bf16[256,256]{1,0:T(8,128)(2,1)S(1)}, u32[]{:S(2)}, u32[]{:S(2)}) collective-permute-start(bf16[256,256]{1,0:T(8,128)(2,1)S(1)} %get-tuple-element.37), channel_id=1, source_target_pairs={{0,8},{1,9},{2,10},{3,11},{4,12},{5,13},{6,14},{7,15},{8,0},{9,1},... | collective-permute-start | bytes 393224 | tf_op jit(solution)/shard_map/ppermute | solution.py:265
  101.5 5.4 %collective-permute-start.19 = (bf16[256,256]{1,0:T(8,128)(2,1)S(1)}, bf16[256,256]{1,0:T(8,128)(2,1)S(1)}, u32[]{:S(2)}, u32[]{:S(2)}) collective-permute-start(bf16[256,256]{1,0:T(8,128)(2,1)S(1)} %get-tuple-element.38), channel_id=1, source_target_pairs={{0,12},{1,13},{2,14},{3,15},{4,0},{5,1},{6,2},{7,3},{8,4},{9,5},{1... | collective-permute-start | bytes 393224 | tf_op jit(solution)/shard_map/ppermute | solution.py:265

commit v6 on v5

--- a/solution.py
+++ b/solution.py
@@ -409,7 +409,8 @@
             compiler_params=params(8),
             name="weight_part",
         )(place, grad_low, *[along[half, step] for step in range(1, SIDE)], near)
-        final += [own] + [shift(part, "zx"[half], step + 1) for step, part in enumerate(others)]
+        sent = {step: shift(others[step - 1], "zx"[half], step) for step in (2, 1, 3)}
+        final += [own] + [sent[step] for step in range(1, SIDE)]
     weight_grad = pl.pallas_call(
         final_kernel,
         out_shape=jax.ShapeDtypeStruct((block, 2, head_cols), F32),

time: 109 us -> 109 us (level)
  no operation moved by 1% of the time
where the time goes in v6:
time: 109 us; the launch traced here: 108 us
  starting transfers between devices  43 us (39%)
  waiting for transfers between devices  28.7 us (26%)
  Pallas kernels  27.6 us (25%)
  matrix products  6.91 us (6%)
    ppermute x12, starting transfers between devices, shift(): return lax.ppermute(values, 'txt', pairs)  16.9 us
    ppermute x5, waiting for transfers between devices, swap_img(): lax.ppermute(values, 'img', [(i, i ^ bit) for i in range(lax.axis_size('i...  11.6 us
    pallas_call x1, Pallas kernels, shards(): pl.pallas_call(functools.partial(attend_kernel, img_dev=img_dev), out_sha...  11 us
    all_to_all x1, starting transfers between devices, shards(): table = lax.all_to_all(wanted, 'txt', 0, 0, tiled=True)  7.97 us
    ppermute x12, waiting for transfers between devices, shift(): return lax.ppermute(values, 'txt', pairs)  7.82 us
    all_to_all x1, waiting for transfers between devices, shards(): lax.all_to_all(sent_pairs.reshape(txt_count, CAP, keys_img, cols), 'txt',...  7.47 us
    dot_general x1, matrix products, shards(): jnp.dot(flat_features, kv_weight.reshape(feat_width, cols), preferred_ele...  6.91 us
    all_to_all x1, starting transfers between devices, shards(): lax.all_to_all(sent_pairs.reshape(txt_count, CAP, keys_img, cols), 'txt',...  6.66 us
  transfers between devices with their start and end apart: 23, of which 8 were waited for; matrix products, arithmetic and copies ran while one was open for 6% of the time, Pallas kernels for 22%

profile of v6, /device:TPU:0, one launch (start us, length us, event | category | flops | bytes accessed | tf_op | source)
XLA Modules:
  0.0 108.1 jit_solution(1837320832663767482)
XLA Ops:
  0.6 1.5 %request_table.1 = (s32[16,128]{1,0:T(8,128)}, s32[48]{0:T(128)}) custom-call(s32[2,12]{1,0:T(2,128)} %bitcast.34, s32[8]{0:T(128)} %counts.1), custom_call_target="tpu_custom_call" | custom-call | tf_op jit(solution)/shard_map/request_table/pallas_call | solution.py:300
  2.1 8.0 %all-to-all-start = ((s32[16,1,128]{2,1,0:T(1,128)}), s32[16,1,128]{2,1,0:T(1,128)S(1)}, u32[]{:S(2)}, u32[]{:S(2)}) async-start(s32[16,1,128]{2,1,0:T(1,128)} %bitcast.32), calls=%async_computation | async-start | bytes 16384 | tf_op jit(solution)/shard_map/all_to_all | solution.py:311
  10.1 6.9 %fusion.3 = bf16[512,256]{1,0:T(8,128)(2,1)S(1)} fusion(bf16[512,8192]{1,0:T(8,128)(2,1)} %bitcast.29, bf16[1024,8,2,128]{3,2,1,0:T(2,128)(2,1)} %bitcast.33), kind=kOutput, calls=%fused_computation.3 | convolution fusion | flops 2147614720 | bytes 12845056 | tf_op jit(solution)/shard_map/dot_general | solution.py:315
  17.6 1.7 %fill_slots.1.after = bf16[32,64,256]{2,1,0:T(8,128)(2,1)} custom-call(s32[16,128]{1,0:T(8,128)S(1)} %bitcast.26, bf16[8,64,256]{2,1,0:T(8,128)(2,1)S(1)} %bitcast.25), custom_call_target="tpu_custom_call" | custom-call | tf_op jit(solution)/shard_map/fill_slots/pallas_call | solution.py:318
  19.3 6.7 %all-to-all-start.1 = ((bf16[16,2,64,256]{3,2,1,0:T(8,128)(2,1)}), bf16[16,2,64,256]{3,2,1,0:T(8,128)(2,1)S(1)}, u32[]{:S(2)}, u32[]{:S(2)}) async-start(bf16[16,2,64,256]{3,2,1,0:T(8,128)(2,1)} %bitcast.6), calls=%async_computation.1 | async-start | bytes 2097152 | tf_op jit(solution)/shard_map/all_to_all | solution.py:326
  26.1 3.8 %pack_features.1 = (bf16[512,1024]{1,0:T(8,128)(2,1)}, bf16[256,1024]{1,0:T(8,128)(2,1)}, bf16[512,1024]{1,0:T(8,128)(2,1)}) custom-call(s32[4]{0:T(128)S(1)} %pad_add_fusion.place, bf16[32,64,256]{2,1,0:T(8,128)(2,1)} %fill_slots.1.after, bf16[512,8192]{1,0:T(8,128)(2,1)} %bitcast.30), custom_call_target="tpu_custom_call" | custom-call | bytes 8388608 | tf_op jit(solution)/shard_map/pack_features/pallas_call | solution.py:334
  30.0 3.2 %collective-permute-start.6 = (bf16[512,1024]{1,0:T(8,128)(2,1)}, bf16[512,1024]{1,0:T(8,128)(2,1)S(1)}, u32[]{:S(2)}, u32[]{:S(2)}) collective-permute-start(bf16[512,1024]{1,0:T(8,128)(2,1)} %get-tuple-element.28), channel_id=1, source_target_pairs={{0,12},{1,13},{2,14},{3,15},{4,0},{5,1},{6,2},{7,3},{8,4},{9,5},{1... | collective-permute-start | bytes 3145736 | tf_op jit(solution)/shard_map/ppermute | solution.py:276
  33.1 2.3 %collective-permute-start.4 = (bf16[256,1024]{1,0:T(8,128)(2,1)}, bf16[256,1024]{1,0:T(8,128)(2,1)}, u32[]{:S(2)}, u32[]{:S(2)}) collective-permute-start(bf16[256,1024]{1,0:T(8,128)(2,1)} %get-tuple-element.27), channel_id=1, source_target_pairs={{0,8},{1,9},{2,10},{3,11},{4,12},{5,13},{6,14},{7,15},{8,0},{9,1},... | collective-permute-start | bytes 1572872 | tf_op jit(solution)/shard_map/ppermute | solution.py:276
  35.4 7.5 %all-to-all-done.1 = bf16[16,2,64,256]{3,2,1,0:T(8,128)(2,1)S(1)} async-done(((bf16[16,2,64,256]{3,2,1,0:T(8,128)(2,1)}), bf16[16,2,64,256]{3,2,1,0:T(8,128)(2,1)S(1)}, u32[]{:S(2)}, u32[]{:S(2)}) %all-to-all-start.1) | async-done | bytes 1048608 | tf_op jit(solution)/shard_map/all_to_all | solution.py:326
  42.9 11.0 %attend.1 = (bf16[1536,1024]{1,0:T(8,128)(2,1)}, bf16[1536,1024]{1,0:T(8,128)(2,1)}, bf16[32,64,256]{2,1,0:T(8,128)(2,1)S(1)}) custom-call(s32[48]{0:T(128)S(1)} %copy-done.2, s32[16,128]{1,0:T(8,128)S(1)} %bitcast.27, s32[12]{0:T(128)S(1)} %copy-done.1, bf16[1536,1024]{1,0:T(8,128)(2,1)} %queries.1, bf16[1536,1024]{1,0:T(8,128)(2,1)} %grads.1, ...), custom_call_target="tpu_custom_call" | custom-call | tf_op jit(solution)/shard_map/attend/pallas_call | solution.py:352
  53.9 1.0 copy-done
  54.9 3.7 %all-to-all-start.2 = ((bf16[16,2,64,256]{3,2,1,0:T(8,128)(2,1)}), bf16[16,2,64,256]{3,2,1,0:T(8,128)(2,1)S(1)}, u32[]{:S(2)}, u32[]{:S(2)}) async-start(bf16[16,2,64,256]{3,2,1,0:T(8,128)(2,1)} %bitcast.24), calls=%async_computation.2 | async-start | bytes 2097152 | tf_op jit(solution)/shard_map/all_to_all | solution.py:366
  58.6 1.7 %collective-permute-start.5 = (bf16[256,1024]{1,0:T(8,128)(2,1)}, bf16[256,1024]{1,0:T(8,128)(2,1)}, u32[]{:S(2)}, u32[]{:S(2)}) collective-permute-start(bf16[256,1024]{1,0:T(8,128)(2,1)} %collective-permute-done.4.rest_1_), channel_id=1, source_target_pairs={{0,32},{16,48},{32,0},{48,16},{64,96},{80,112},{96,64},{112,80},{1... | collective-permute-start | bytes 1572872 | tf_op jit(solution)/shard_map/ppermute | solution.py:280
  60.9 11.5 %collective-permute-done.5.rest_2_ = bf16[256,1024]{1,0:T(8,128)(2,1)} collective-permute-done((bf16[256,1024]{1,0:T(8,128)(2,1)}, bf16[256,1024]{1,0:T(8,128)(2,1)}, u32[]{:S(2)}, u32[]{:S(2)}) %collective-permute-start.5) | collective-permute-done | bytes 524320 | tf_op jit(solution)/shard_map/ppermute | solution.py:280
  72.4 1.3 %all-to-all-done.2 = bf16[16,2,64,256]{3,2,1,0:T(8,128)(2,1)S(1)} async-done(((bf16[16,2,64,256]{3,2,1,0:T(8,128)(2,1)}), bf16[16,2,64,256]{3,2,1,0:T(8,128)(2,1)S(1)}, u32[]{:S(2)}, u32[]{:S(2)}) %all-to-all-start.2) | async-done | bytes 1048608 | tf_op jit(solution)/shard_map/all_to_all | solution.py:366
  73.8 1.2 %image_grads.1.grad_low.refs_0_ = bf16[256,512]{1,0:T(8,128)(2,1)S(1)} custom-call(s32[16,128]{1,0:T(8,128)S(1)} %bitcast.28, bf16[32,64,256]{2,1,0:T(8,128)(2,1)S(1)} %bitcast.23), custom_call_target="tpu_custom_call" | custom-call | tf_op jit(solution)/shard_map/image_grads/pallas_call | solution.py:370
  75.0 2.7 %collective-permute-start.1 = (bf16[256,512]{1,0:T(8,128)(2,1)S(1)}, bf16[256,512]{1,0:T(8,128)(2,1)S(1)}, u32[]{:S(2)}, u32[]{:S(2)}) collective-permute-start(bf16[256,512]{1,0:T(8,128)(2,1)S(1)} %image_grads.1.grad_low.refs_0_), channel_id=1, source_target_pairs={{0,8},{1,9},{2,10},{3,11},{4,12},{5,13},{6,14},{7,15},{8,0},{9,1},... | collective-permute-start | bytes 786440 | tf_op jit(solution)/shard_map/ppermute | solution.py:265
  77.7 1.0 collective-permute-start.2
  79.0 2.5 %collective-permute-start.15 = (bf16[256,512]{1,0:T(8,128)(2,1)S(1)}, bf16[256,512]{1,0:T(8,128)(2,1)S(1)}, u32[]{:S(2)}, u32[]{:S(2)}) collective-permute-start(bf16[256,512]{1,0:T(8,128)(2,1)S(1)} %image_grads.1.grad_low.refs_0_), channel_id=1, source_target_pairs={{0,2},{1,3},{2,0},{3,1},{4,6},{5,7},{6,4},{7,5},{8,10},{9,11},{10,... | collective-permute-start | bytes 786440 | tf_op jit(solution)/shard_map/ppermute | solution.py:265
  81.6 3.6 %near_features.1 = (bf16[256,512]{1,0:T(8,128)(2,1)S(1)}, bf16[2,4,512,1024]{3,2,1,0:T(8,128)(2,1)S(1)}) custom-call(s32[4]{0:T(128)S(1)} %pad_add_fusion.place, bf16[256,512]{1,0:T(8,128)(2,1)S(1)} %image_grads.1.grad_low.refs_0_, bf16[512,8192]{1,0:T(8,128)(2,1)} %bitcast.31, bf16[512,1024]{1,0:T(8,128)(2,1)S(1)} %collective-permute-done.3.rest_0_, ...), custom_call_target="tpu_custom_call" | custom-call | bytes 8388608 | tf_op jit(solution)/shard_map/near_features/pallas_call | solution.py:379
  85.2 4.0 %collective-permute-done.refs_1_ = bf16[256,512]{1,0:T(8,128)(2,1)S(1)} collective-permute-done((bf16[256,512]{1,0:T(8,128)(2,1)S(1)}, bf16[256,512]{1,0:T(8,128)(2,1)S(1)}, u32[]{:S(2)}, u32[]{:S(2)}) %collective-permute-start) | collective-permute-done | bytes 262176 | tf_op jit(solution)/shard_map/ppermute | solution.py:265
  89.9 1.8 %weight_part.2 = (f32[256,256]{1,0:T(8,128)S(1)}, bf16[256,256]{1,0:T(8,128)(2,1)S(1)}, bf16[256,256]{1,0:T(8,128)(2,1)S(1)}, bf16[256,256]{1,0:T(8,128)(2,1)S(1)}) custom-call(s32[4]{0:T(128)S(1)} %pad_add_fusion.place, bf16[256,512]{1,0:T(8,128)(2,1)S(1)} %image_grads.1.grad_low.refs_0_, bf16[256,512]{1,0:T(8,128)(2,1)S(1)} %collective-permute-done.refs_1_, ...), custom_call_target="tpu_custom_call" | custom-call | tf_op jit(solution)/shard_map/weight_part/pallas_call | solution.py:401
  91.7 1.5 %collective-permute-start.11 = (bf16[256,256]{1,0:T(8,128)(2,1)S(1)}, bf16[256,256]{1,0:T(8,128)(2,1)S(1)}, u32[]{:S(2)}, u32[]{:S(2)}) collective-permute-start(bf16[256,256]{1,0:T(8,128)(2,1)S(1)} %get-tuple-element.31), channel_id=1, source_target_pairs={{0,1},{1,2},{2,3},{3,0},{4,5},{5,6},{6,7},{7,4},{8,9},{9,10},{10,1... | collective-permute-start | bytes 393224 | tf_op jit(solution)/shard_map/ppermute | solution.py:265
  93.2 1.2 %collective-permute-start.12 = (bf16[256,256]{1,0:T(8,128)(2,1)S(1)}, bf16[256,256]{1,0:T(8,128)(2,1)S(1)}, u32[]{:S(2)}, u32[]{:S(2)}) collective-permute-start(bf16[256,256]{1,0:T(8,128)(2,1)S(1)} %get-tuple-element.32), channel_id=1, source_target_pairs={{0,2},{1,3},{2,0},{3,1},{4,6},{5,7},{6,4},{7,5},{8,10},{9,11},{10,... | collective-permute-start | bytes 393224 | tf_op jit(solution)/shard_map/ppermute | solution.py:265
  94.3 2.2 %collective-permute-start.13 = (bf16[256,256]{1,0:T(8,128)(2,1)S(1)}, bf16[256,256]{1,0:T(8,128)(2,1)S(1)}, u32[]{:S(2)}, u32[]{:S(2)}) collective-permute-start(bf16[256,256]{1,0:T(8,128)(2,1)S(1)} %get-tuple-element.33), channel_id=1, source_target_pairs={{0,3},{1,0},{2,1},{3,2},{4,7},{5,4},{6,5},{7,6},{8,11},{9,8},{10,9... | collective-permute-start | bytes 393224 | tf_op jit(solution)/shard_map/ppermute | solution.py:265
  96.6 1.8 %weight_part.3 = (f32[256,256]{1,0:T(8,128)S(1)}, bf16[256,256]{1,0:T(8,128)(2,1)S(1)}, bf16[256,256]{1,0:T(8,128)(2,1)S(1)}, bf16[256,256]{1,0:T(8,128)(2,1)S(1)}) custom-call(s32[4]{0:T(128)S(1)} %pad_add_fusion.place, bf16[256,512]{1,0:T(8,128)(2,1)S(1)} %image_grads.1.grad_low.refs_0_, bf16[256,512]{1,0:T(8,128)(2,1)S(1)} %collective-permute-done.14.refs_1_, ...), custom_call_target="tpu_custom_call" | custom-call | tf_op jit(solution)/shard_map/weight_part/pallas_call | solution.py:401
  98.4 0.7 collective-permute-start.17
  99.1 2.4 %collective-permute-start.18 = (bf16[256,256]{1,0:T(8,128)(2,1)S(1)}, bf16[256,256]{1,0:T(8,128)(2,1)S(1)}, u32[]{:S(2)}, u32[]{:S(2)}) collective-permute-start(bf16[256,256]{1,0:T(8,128)(2,1)S(1)} %get-tuple-element.37), channel_id=1, source_target_pairs={{0,8},{1,9},{2,10},{3,11},{4,12},{5,13},{6,14},{7,15},{8,0},{9,1},... | collective-permute-start | bytes 393224 | tf_op jit(solution)/shard_map/ppermute | solution.py:265
  101.5 2.3 %collective-permute-start.19 = (bf16[256,256]{1,0:T(8,128)(2,1)S(1)}, bf16[256,256]{1,0:T(8,128)(2,1)S(1)}, u32[]{:S(2)}, u32[]{:S(2)}) collective-permute-start(bf16[256,256]{1,0:T(8,128)(2,1)S(1)} %get-tuple-element.38), channel_id=1, source_target_pairs={{0,12},{1,13},{2,14},{3,15},{4,0},{5,1},{6,2},{7,3},{8,4},{9,5},{1... | collective-permute-start | bytes 393224 | tf_op jit(solution)/shard_map/ppermute | solution.py:265
  103.8 1.7 %collective-permute-done.17.refs_5_ = bf16[256,256]{1,0:T(8,128)(2,1)S(1)} collective-permute-done((bf16[256,256]{1,0:T(8,128)(2,1)S(1)}, bf16[256,256]{1,0:T(8,128)(2,1)S(1)}, u32[]{:S(2)}, u32[]{:S(2)}) %collective-permute-start.17) | collective-permute-done | bytes 131104 | tf_op jit(solution)/shard_map/ppermute | solution.py:265
  105.6 1.4 %collective-permute-done.18.refs_6_ = bf16[256,256]{1,0:T(8,128)(2,1)S(1)} collective-permute-done((bf16[256,256]{1,0:T(8,128)(2,1)S(1)}, bf16[256,256]{1,0:T(8,128)(2,1)S(1)}, u32[]{:S(2)}, u32[]{:S(2)}) %collective-permute-start.18) | collective-permute-done | bytes 131104 | tf_op jit(solution)/shard_map/ppermute | solution.py:265
  107.0 1.2 %weight_total.1 = f32[512,2,128]{2,1,0:T(2,128)} custom-call(f32[256,256]{1,0:T(8,128)S(1)} %get-tuple-element.30.refs_0_, bf16[256,256]{1,0:T(8,128)(2,1)S(1)} %collective-permute-done.11.refs_1_, bf16[256,256]{1,0:T(8,128)(2,1)S(1)} %collective-permute-done.12.refs_2_, bf16[256,256]{1,0:T(8,128)(2,1)S(1)} %collective-permute-done.13.refs_3_, ...), custom_call_target="tpu_custom_call" | custom-call | tf_op jit(solution)/shard_map/weight_total/pallas_call | solution.py:414
  (31 shorter events, 2.3 us)
Async XLA Ops:
  2.1 15.5 %all-to-all-start = ((s32[16,1,128]{2,1,0:T(1,128)}), s32[16,1,128]{2,1,0:T(1,128)S(1)}, u32[]{:S(2)}, u32[]{:S(2)}) async-start(s32[16,1,128]{2,1,0:T(1,128)} %bitcast.32), calls=%async_computation | async-start | bytes 16384 | tf_op jit(solution)/shard_map/all_to_all | solution.py:311
  19.3 23.6 %all-to-all-start.1 = ((bf16[16,2,64,256]{3,2,1,0:T(8,128)(2,1)}), bf16[16,2,64,256]{3,2,1,0:T(8,128)(2,1)S(1)}, u32[]{:S(2)}, u32[]{:S(2)}) async-start(bf16[16,2,64,256]{3,2,1,0:T(8,128)(2,1)} %bitcast.6), calls=%async_computation.1 | async-start | bytes 2097152 | tf_op jit(solution)/shard_map/all_to_all | solution.py:326
  26.1 16.8 %copy-start.1 = (s32[12]{0:T(128)S(1)}, s32[12]{0:T(128)}, u32[]{:S(2)}) copy-start(s32[12]{0:T(128)} %lengths.1) | copy-start | bytes 148
  26.1 16.8 %copy-start.2 = (s32[48]{0:T(128)S(1)}, s32[48]{0:T(128)}, u32[]{:S(2)}) copy-start(s32[48]{0:T(128)} %get-tuple-element.21.meta) | copy-start | bytes 580
  30.0 30.3 %collective-permute-start.6 = (bf16[512,1024]{1,0:T(8,128)(2,1)}, bf16[512,1024]{1,0:T(8,128)(2,1)S(1)}, u32[]{:S(2)}, u32[]{:S(2)}) collective-permute-start(bf16[512,1024]{1,0:T(8,128)(2,1)} %get-tuple-element.28), channel_id=1, source_target_pairs={{0,12},{1,13},{2,14},{3,15},{4,0},{5,1},{6,2},{7,3},{8,4},{9,5},{1... | collective-permute-start | bytes 3145736 | tf_op jit(solution)/shard_map/ppermute | solution.py:276
  33.1 27.2 %collective-permute-start.3 = (bf16[512,1024]{1,0:T(8,128)(2,1)}, bf16[512,1024]{1,0:T(8,128)(2,1)S(1)}, u32[]{:S(2)}, u32[]{:S(2)}) collective-permute-start(bf16[512,1024]{1,0:T(8,128)(2,1)} %get-tuple-element.26), channel_id=1, source_target_pairs={{0,4},{1,5},{2,6},{3,7},{4,8},{5,9},{6,10},{7,11},{8,12},{9,13},{1... | collective-permute-start | bytes 3145736 | tf_op jit(solution)/shard_map/ppermute | solution.py:276
  33.1 25.5 %collective-permute-start.4 = (bf16[256,1024]{1,0:T(8,128)(2,1)}, bf16[256,1024]{1,0:T(8,128)(2,1)}, u32[]{:S(2)}, u32[]{:S(2)}) collective-permute-start(bf16[256,1024]{1,0:T(8,128)(2,1)} %get-tuple-element.27), channel_id=1, source_target_pairs={{0,8},{1,9},{2,10},{3,11},{4,12},{5,13},{6,14},{7,15},{8,0},{9,1},... | collective-permute-start | bytes 1572872 | tf_op jit(solution)/shard_map/ppermute | solution.py:276
  53.9 1.0 copy-start
  54.9 18.9 %all-to-all-start.2 = ((bf16[16,2,64,256]{3,2,1,0:T(8,128)(2,1)}), bf16[16,2,64,256]{3,2,1,0:T(8,128)(2,1)S(1)}, u32[]{:S(2)}, u32[]{:S(2)}) async-start(bf16[16,2,64,256]{3,2,1,0:T(8,128)(2,1)} %bitcast.24), calls=%async_computation.2 | async-start | bytes 2097152 | tf_op jit(solution)/shard_map/all_to_all | solution.py:366
  58.6 13.8 %collective-permute-start.5 = (bf16[256,1024]{1,0:T(8,128)(2,1)}, bf16[256,1024]{1,0:T(8,128)(2,1)}, u32[]{:S(2)}, u32[]{:S(2)}) collective-permute-start(bf16[256,1024]{1,0:T(8,128)(2,1)} %collective-permute-done.4.rest_1_), channel_id=1, source_target_pairs={{0,32},{16,48},{32,0},{48,16},{64,96},{80,112},{96,64},{112,80},{1... | collective-permute-start | bytes 1572872 | tf_op jit(solution)/shard_map/ppermute | solution.py:280
  60.3 18.4 %collective-permute-start.10 = (bf16[512,1024]{1,0:T(8,128)(2,1)S(1)}, bf16[512,1024]{1,0:T(8,128)(2,1)}, u32[]{:S(2)}, u32[]{:S(2)}) collective-permute-start(bf16[512,1024]{1,0:T(8,128)(2,1)S(1)} %collective-permute-done.6.rest_3_), channel_id=1, source_target_pairs={{0,16},{16,0},{32,48},{48,32},{64,80},{80,64},{96,112},{112,96},{1... | collective-permute-start | bytes 3145736 | tf_op jit(solution)/shard_map/ppermute | solution.py:280
  60.3 18.7 %collective-permute-start.7 = (bf16[512,1024]{1,0:T(8,128)(2,1)S(1)}, bf16[512,1024]{1,0:T(8,128)(2,1)}, u32[]{:S(2)}, u32[]{:S(2)}) collective-permute-start(bf16[512,1024]{1,0:T(8,128)(2,1)S(1)} %collective-permute-done.3.rest_0_), channel_id=1, source_target_pairs={{0,16},{16,0},{32,48},{48,32},{64,80},{80,64},{96,112},{112,96},{1... | collective-permute-start | bytes 3145736 | tf_op jit(solution)/shard_map/ppermute | solution.py:280
  60.8 14.2 %collective-permute-start.8 = (bf16[256,1024]{1,0:T(8,128)(2,1)}, bf16[256,1024]{1,0:T(8,128)(2,1)}, u32[]{:S(2)}, u32[]{:S(2)}) collective-permute-start(bf16[256,1024]{1,0:T(8,128)(2,1)} %collective-permute-done.4.rest_1_), channel_id=1, source_target_pairs={{0,16},{16,0},{32,48},{48,32},{64,80},{80,64},{96,112},{112,96},{1... | collective-permute-start | bytes 1572872 | tf_op jit(solution)/shard_map/ppermute | solution.py:280
  72.4 5.3 %collective-permute-start.9 = (bf16[256,1024]{1,0:T(8,128)(2,1)}, bf16[256,1024]{1,0:T(8,128)(2,1)}, u32[]{:S(2)}, u32[]{:S(2)}) collective-permute-start(bf16[256,1024]{1,0:T(8,128)(2,1)} %collective-permute-done.5.rest_2_), channel_id=1, source_target_pairs={{0,16},{16,0},{32,48},{48,32},{64,80},{80,64},{96,112},{112,96},{1... | collective-permute-start | bytes 1572872 | tf_op jit(solution)/shard_map/ppermute | solution.py:280
  74.9 14.3 %collective-permute-start = (bf16[256,512]{1,0:T(8,128)(2,1)S(1)}, bf16[256,512]{1,0:T(8,128)(2,1)S(1)}, u32[]{:S(2)}, u32[]{:S(2)}) collective-permute-start(bf16[256,512]{1,0:T(8,128)(2,1)S(1)} %image_grads.1.grad_low.refs_0_), channel_id=1, source_target_pairs={{0,4},{1,5},{2,6},{3,7},{4,8},{5,9},{6,10},{7,11},{8,12},{9,13},{1... | collective-permute-start | bytes 786440 | tf_op jit(solution)/shard_map/ppermute | solution.py:265
  75.0 14.2 %collective-permute-start.1 = (bf16[256,512]{1,0:T(8,128)(2,1)S(1)}, bf16[256,512]{1,0:T(8,128)(2,1)S(1)}, u32[]{:S(2)}, u32[]{:S(2)}) collective-permute-start(bf16[256,512]{1,0:T(8,128)(2,1)S(1)} %image_grads.1.grad_low.refs_0_), channel_id=1, source_target_pairs={{0,8},{1,9},{2,10},{3,11},{4,12},{5,13},{6,14},{7,15},{8,0},{9,1},... | collective-permute-start | bytes 786440 | tf_op jit(solution)/shard_map/ppermute | solution.py:265
  77.7 12.2 %collective-permute-start.2 = (bf16[256,512]{1,0:T(8,128)(2,1)S(1)}, bf16[256,512]{1,0:T(8,128)(2,1)S(1)}, u32[]{:S(2)}, u32[]{:S(2)}) collective-permute-start(bf16[256,512]{1,0:T(8,128)(2,1)S(1)} %image_grads.1.grad_low.refs_0_), channel_id=1, source_target_pairs={{0,12},{1,13},{2,14},{3,15},{4,0},{5,1},{6,2},{7,3},{8,4},{9,5},{1... | collective-permute-start | bytes 786440 | tf_op jit(solution)/shard_map/ppermute | solution.py:265
  78.7 15.6 %collective-permute-start.14 = (bf16[256,512]{1,0:T(8,128)(2,1)S(1)}, bf16[256,512]{1,0:T(8,128)(2,1)S(1)}, u32[]{:S(2)}, u32[]{:S(2)}) collective-permute-start(bf16[256,512]{1,0:T(8,128)(2,1)S(1)} %image_grads.1.grad_low.refs_0_), channel_id=1, source_target_pairs={{0,1},{1,2},{2,3},{3,0},{4,5},{5,6},{6,7},{7,4},{8,9},{9,10},{10,1... | collective-permute-start | bytes 786440 | tf_op jit(solution)/shard_map/ppermute | solution.py:265
  79.0 17.5 %collective-permute-start.15 = (bf16[256,512]{1,0:T(8,128)(2,1)S(1)}, bf16[256,512]{1,0:T(8,128)(2,1)S(1)}, u32[]{:S(2)}, u32[]{:S(2)}) collective-permute-start(bf16[256,512]{1,0:T(8,128)(2,1)S(1)} %image_grads.1.grad_low.refs_0_), channel_id=1, source_target_pairs={{0,2},{1,3},{2,0},{3,1},{4,6},{5,7},{6,4},{7,5},{8,10},{9,11},{10,... | collective-permute-start | bytes 786440 | tf_op jit(solution)/shard_map/ppermute | solution.py:265
  89.2 7.3 %collective-permute-start.16 = (bf16[256,512]{1,0:T(8,128)(2,1)S(1)}, bf16[256,512]{1,0:T(8,128)(2,1)S(1)}, u32[]{:S(2)}, u32[]{:S(2)}) collective-permute-start(bf16[256,512]{1,0:T(8,128)(2,1)S(1)} %get-tuple-element.34), channel_id=1, source_target_pairs={{0,3},{1,0},{2,1},{3,2},{4,7},{5,4},{6,5},{7,6},{8,11},{9,8},{10,9... | collective-permute-start | bytes 786440 | tf_op jit(solution)/shard_map/ppermute | solution.py:265
  91.7 9.8 %collective-permute-start.11 = (bf16[256,256]{1,0:T(8,128)(2,1)S(1)}, bf16[256,256]{1,0:T(8,128)(2,1)S(1)}, u32[]{:S(2)}, u32[]{:S(2)}) collective-permute-start(bf16[256,256]{1,0:T(8,128)(2,1)S(1)} %get-tuple-element.31), channel_id=1, source_target_pairs={{0,1},{1,2},{2,3},{3,0},{4,5},{5,6},{6,7},{7,4},{8,9},{9,10},{10,1... | collective-permute-start | bytes 393224 | tf_op jit(solution)/shard_map/ppermute | solution.py:265
  93.2 10.7 %collective-permute-start.12 = (bf16[256,256]{1,0:T(8,128)(2,1)S(1)}, bf16[256,256]{1,0:T(8,128)(2,1)S(1)}, u32[]{:S(2)}, u32[]{:S(2)}) collective-permute-start(bf16[256,256]{1,0:T(8,128)(2,1)S(1)} %get-tuple-element.32), channel_id=1, source_target_pairs={{0,2},{1,3},{2,0},{3,1},{4,6},{5,7},{6,4},{7,5},{8,10},{9,11},{10,... | collective-permute-start | bytes 393224 | tf_op jit(solution)/shard_map/ppermute | solution.py:265
  94.3 9.5 %collective-permute-start.13 = (bf16[256,256]{1,0:T(8,128)(2,1)S(1)}, bf16[256,256]{1,0:T(8,128)(2,1)S(1)}, u32[]{:S(2)}, u32[]{:S(2)}) collective-permute-start(bf16[256,256]{1,0:T(8,128)(2,1)S(1)} %get-tuple-element.33), channel_id=1, source_target_pairs={{0,3},{1,0},{2,1},{3,2},{4,7},{5,4},{6,5},{7,6},{8,11},{9,8},{10,9... | collective-permute-start | bytes 393224 | tf_op jit(solution)/shard_map/ppermute | solution.py:265
  98.4 7.2 %collective-permute-start.17 = (bf16[256,256]{1,0:T(8,128)(2,1)S(1)}, bf16[256,256]{1,0:T(8,128)(2,1)S(1)}, u32[]{:S(2)}, u32[]{:S(2)}) collective-permute-start(bf16[256,256]{1,0:T(8,128)(2,1)S(1)} %get-tuple-element.36), channel_id=1, source_target_pairs={{0,4},{1,5},{2,6},{3,7},{4,8},{5,9},{6,10},{7,11},{8,12},{9,13},{1... | collective-permute-start | bytes 393224 | tf_op jit(solution)/shard_map/ppermute | solution.py:265
  99.1 7.8 %collective-permute-start.18 = (bf16[256,256]{1,0:T(8,128)(2,1)S(1)}, bf16[256,256]{1,0:T(8,128)(2,1)S(1)}, u32[]{:S(2)}, u32[]{:S(2)}) collective-permute-start(bf16[256,256]{1,0:T(8,128)(2,1)S(1)} %get-tuple-element.37), channel_id=1, source_target_pairs={{0,8},{1,9},{2,10},{3,11},{4,12},{5,13},{6,14},{7,15},{8,0},{9,1},... | collective-permute-start | bytes 393224 | tf_op jit(solution)/shard_map/ppermute | solution.py:265
  101.5 5.4 %collective-permute-start.19 = (bf16[256,256]{1,0:T(8,128)(2,1)S(1)}, bf16[256,256]{1,0:T(8,128)(2,1)S(1)}, u32[]{:S(2)}, u32[]{:S(2)}) collective-permute-start(bf16[256,256]{1,0:T(8,128)(2,1)S(1)} %get-tuple-element.38), channel_id=1, source_target_pairs={{0,12},{1,13},{2,14},{3,15},{4,0},{5,1},{6,2},{7,3},{8,4},{9,5},{1... | collective-permute-start | bytes 393224 | tf_op jit(solution)/shard_map/ppermute | solution.py:265
